TPU v7x, 128 devices: a whole 4x4x4 slice. The times are simulated.
128 devices in a mesh: aux: 4 (over x_hi, core), row: 32 (over z, x_lo, y).
Axes of the slice: x: 4 (x_hi: 2, x_lo: 2; x = x_hi * 2 + x_lo), y: 4, z: 4, core: 2. Of those that a mesh axis runs over, the one named last changes fastest.
Arguments:
- slab: bfloat16 [20, 8192, 8192], P('aux', 'row'), may hold values from -6 to 6
- screen: int32 [4, 64, 64], P('aux', 'row'), may hold values 0 or 1
- orbitals: bfloat16 [8192, 128], P('row'), may hold values from -0.0625 to 0.0625
- hcore: float32 [8192, 8192], P('row', 'aux'), may hold values from -6 to 6
Outputs:
- exchange: float32 [8192, 8192], P('row', 'aux')
- gradient: float32 [8192, 128], P('row')
All inputs are finite; a program needn't handle non-finite values. No bound on the sum of `screen` on one device may be relied on, other than what follows from the above.
Results may differ from a plain program's by a relative error of at most 0.0035.
Values may be sent and summed in bfloat16 or wider, within the bound.
No kernel may reach another device: no remote copies, remote signals or barrier semaphores. Data moves between devices by JAX's collectives and lax.ppermute only.
A program may use at most 128 MiB of HBM per device.

v0:
```python
import math

import jax
import jax.numpy as jnp
from jax import lax
from jax.sharding import PartitionSpec as P


def on_device(slab, screen, orbitals, hcore):
    local_auxiliary_rows, row_count, basis_count = slab.shape
    row_tiles = screen.shape[1]
    col_tiles = screen.shape[2]
    tile_size = row_count // row_tiles
    everything = lax.all_gather(orbitals, "row", axis=0, tiled=True)
    screen_bf = screen[0].astype(slab.dtype)
    masked = (
        slab.reshape(local_auxiliary_rows, row_tiles, tile_size, col_tiles, tile_size)
        * screen_bf[None, :, None, :, None]
    )
    half_slab = jnp.einsum(
        "qmn,ni->qmi",
        masked.reshape(local_auxiliary_rows, row_count, basis_count),
        everything,
        preferred_element_type=jnp.float32,
    ).astype(jnp.bfloat16)
    number_of_groups = lax.axis_size("aux")
    exchange_scale = 1.0 / math.sqrt(local_auxiliary_rows * number_of_groups * orbitals.shape[1])
    col_count = basis_count // number_of_groups
    partial_rows = jnp.einsum(
        "qmi,qni->mn",
        half_slab,
        lax.all_gather(half_slab, "row", axis=1, tiled=True),
        preferred_element_type=jnp.float32,
    )
    owned_column_slice = lax.psum_scatter(partial_rows, "aux", scatter_dimension=1, tiled=True)
    exchange = owned_column_slice * exchange_scale
    fock_bf = (hcore - 0.5 * exchange).astype(jnp.bfloat16)
    column_orbitals = lax.dynamic_slice_in_dim(
        everything, lax.axis_index("aux") * col_count, col_count, 0
    )
    applied = lax.psum(jnp.dot(fock_bf, column_orbitals, preferred_element_type=jnp.float32), "aux")
    orbit_rows = orbitals.astype(jnp.float32)
    projection = lax.psum(jnp.dot(orbit_rows.T, applied, precision=lax.Precision.HIGHEST), "row")
    gradient = applied - jnp.dot(orbit_rows, projection, precision=lax.Precision.HIGHEST)
    return (exchange, gradient)


def solution(mesh):
    in_specs = (P("aux", "row", None), P("aux", "row", None), P("row", None), P("row", "aux"))
    out_specs = (P("row", "aux"), P("row", None))
    return jax.shard_map(
        on_device, mesh=mesh, in_specs=in_specs, out_specs=out_specs, check_vma=False
    )
```

profile of v0, /device:TPU:1, one launch (start us, length us, event | category | flops | bytes accessed | tf_op | source)
XLA Modules:
  0.0 748.8 jit_solution(9627809027993757195)
XLA Ops:
  7.2 0.0 all-gather.3.cloned.1.call-start
  7.2 0.7 all-gather.3.cloned.1.call-update
  7.9 0.0 all-gather.5.cloned.1.call-start
  7.9 0.7 convert_bitcast_fusion
  8.6 1.1 mul.28
  9.8 10.1 %copy.10 = bf16[32,8,64,128]{3,1,2,0:T(8,128)(2,1)} copy(bf16[32,8,64,128]{3,2,1,0:T(8,128)(2,1)S(1)} %bitcast.26) | data formatting | bytes 8388608
  19.9 125.2 %all-gather.3.cloned.1.call-done = bf16[8192,128]{1,0:T(8,128)(2,1)} async-done(((bf16[256,128]{1,0:T(8,128)(2,1)}), bf16[8192,128]{1,0:T(8,128)(2,1)}) %all-gather.3.cloned.1.call-update) | async-done | bytes 2097168 | tf_op jit(solution)/shard_map/all_gather | solution.py:14
  145.1 12.3 %fusion.4 = bf16[5,256,128]{2,1,0:T(8,128)(2,1)} fusion(bf16[8192,128]{1,0:T(8,128)(2,1)} %all-gather.3.cloned.1.call-done, bf16[5,256,8192]{2,1,0:T(8,128)(2,1)} %param.4, bf16[256,8192]{1,0:T(8,128)(2,1)} %bitcast.27), kind=kOutput, calls=%fused_computation.7 | convolution fusion | flops 2695004160 | bytes 27590656 | tf_op jit(solution)/shard_map/qmn,ni->qmi/dot_general | solution.py:20
  157.4 0.0 all-gather.5.cloned.1.call-update
  157.4 0.2 reduce-scatter.2.cloned.1.call-start
  157.6 174.3 %all-gather.5.cloned.1.call-done = bf16[5,8192,128]{2,1,0:T(8,128)(2,1)} async-done(((bf16[5,256,128]{2,1,0:T(8,128)(2,1)}), bf16[5,8192,128]{2,1,0:T(8,128)(2,1)}) %all-gather.5.cloned.1.call-update) | async-done | bytes 10485776 | tf_op jit(solution)/shard_map/all_gather | solution.py:32
  331.9 10.9 %convolution_bitcast_fusion = f32[256,8192]{1,0:T(8,128)} fusion(bf16[5,256,128]{2,1,0:T(8,128)(2,1)} %fusion.4, bf16[5,8192,128]{2,1,0:T(8,128)(2,1)} %all-gather.5.cloned.1.call-done), kind=kOutput, calls=%fused_computation.2 | convolution fusion | flops 2684354560 | bytes 19202048 | tf_op jit(solution)/shard_map/qmi,qni->mn/dot_general | solution.py:29
  342.8 0.0 reduce-scatter.2.cloned.1.call-update
  342.8 0.0 all-reduce.3.cloned.1.call-start
  342.9 0.0 copy-start.1
  342.9 95.9 %reduce-scatter.2.cloned.1.call-done = f32[256,2048]{1,0:T(8,128)} async-done(((f32[256,8192]{1,0:T(8,128)}), f32[256,2048]{1,0:T(8,128)}) %reduce-scatter.2.cloned.1.call-update) | async-done | bytes 2097168 | tf_op jit(solution)/shard_map/reduce_scatter | solution.py:35
  438.7 0.0 copy-start
  438.7 3.5 fusion.10
  442.3 0.0 all-reduce.3.cloned.1.call-update
  442.3 0.0 all-reduce.5.cloned.1.call-start
  442.4 40.2 %all-reduce.3.cloned.1.call-done = f32[256,128]{1,0:T(8,128)} async-done(((f32[256,128]{1,0:T(8,128)}), f32[256,128]{1,0:T(8,128)}) %all-reduce.3.cloned.1.call-update) | async-done | bytes 131088 | tf_op jit(solution)/shard_map/psum | solution.py:41
  482.5 0.0 copy-done.1
  482.5 1.8 convolution_bitcast_fusion.2
  484.4 0.0 all-reduce.5.cloned.1.call-update
  484.4 0.0 copy-done
  484.4 0.0 copy-start.2
  484.4 1.5 broadcast_multiply_fusion
  485.9 254.7 %all-reduce.5.cloned.1.call-done = f32[128,128]{0,1:T(8,128)} async-done(((f32[128,128]{0,1:T(8,128)}), f32[128,128]{0,1:T(8,128)}) %all-reduce.5.cloned.1.call-update) | async-done | bytes 65552 | tf_op jit(solution)/shard_map/psum | solution.py:43
  740.6 0.0 copy-done.2
  740.6 1.7 fusion.9
Async XLA Ops:
  7.2 137.9 %all-gather.3.cloned.1.call-start = ((), (), s32[]{:S(2)}) async-start(), calls=%async_computation.1 | async-start | bytes 2162688 | tf_op jit(solution)/shard_map/all_gather | solution.py:14
  7.9 324.0 %all-gather.5.cloned.1.call-start = ((), (), s32[]{:S(2)}) async-start(), calls=%async_computation.2 | async-start | bytes 10813440 | tf_op jit(solution)/shard_map/all_gather | solution.py:32
  157.4 281.4 %reduce-scatter.2.cloned.1.call-start = ((), (), s32[]{:S(2)}) async-start(), calls=%async_computation.3 | async-start | bytes 10485760 | tf_op jit(solution)/shard_map/reduce_scatter | solution.py:35
  342.8 139.7 %all-reduce.3.cloned.1.call-start = ((), (), s32[]{:S(2)}) async-start(), calls=%async_computation.4 | async-start | bytes 262144 | tf_op jit(solution)/shard_map/psum | solution.py:41
  342.9 139.7 %copy-start.1 = (bf16[256,128]{1,0:T(8,128)(2,1)S(1)}, bf16[256,128]{1,0:T(8,128)(2,1)}, u32[]{:S(2)}) copy-start(bf16[256,128]{1,0:T(8,128)(2,1)} %param.6) | copy-start | bytes 196612
  438.7 45.6 %copy-start = (f32[256,2048]{1,0:T(8,128)S(1)}, f32[256,2048]{1,0:T(8,128)}, u32[]{:S(2)}) copy-start(f32[256,2048]{1,0:T(8,128)} %reduce-scatter.2.cloned.1.call-done) | copy-start | bytes 6291460
  442.3 298.3 %all-reduce.5.cloned.1.call-start = ((), (), s32[]{:S(2)}) async-start(), calls=%async_computation.5 | async-start | bytes 131072 | tf_op jit(solution)/shard_map/psum | solution.py:43
  484.4 256.2 %copy-start.2 = (f32[256,128]{1,0:T(8,128)S(1)}, f32[256,128]{1,0:T(8,128)}, u32[]{:S(2)}) copy-start(f32[256,128]{1,0:T(8,128)} %all-reduce.3.cloned.1.call-done) | copy-start | bytes 393220
Sparse Core Ops, SparseCore 0:
  9.6 135.3 all-gather.2
  157.5 174.3 all-gather.4
  342.9 95.7 reduce-scatter.1
  442.4 40.0 all-reduce.2
  485.4 255.1 all-reduce.4
where the time goes:
time: 763 us; the launch traced here: 749 us
  waiting for transfers between devices  691 us (91%)
  matrix products  30.3 us (4%)
  between operations  13.8 us (2%)
  local copies, waits for them, and re-layouts  11.2 us (1%)
    psum x1, waiting for transfers between devices, on_device(): lax.psum(jnp.dot(orbit_rows.T, applied, precision=lax.Precision.HIGHEST),...  255 us
    all_gather x1, waiting for transfers between devices, on_device(): lax.all_gather(half_slab, 'row', axis=1, tiled=True)  174 us
    all_gather x1, waiting for transfers between devices, on_device(): everything = lax.all_gather(orbitals, 'row', axis=0, tiled=True)  125 us
    reduce_scatter x1, waiting for transfers between devices, on_device(): lax.psum_scatter(partial_rows, 'aux', scatter_dimension=1, tiled=True)  95.9 us
    psum x1, waiting for transfers between devices, on_device(): lax.psum(jnp.dot(fock_bf, column_orbitals, preferred_element_type=jnp.flo...  40.2 us
  transfers between devices with their start and end apart: 5, of which 5 were waited for; matrix products, arithmetic and copies ran while one was open for 2% of the time, Pallas kernels for 0%

commit v1 on v0

v1 whole, which is shorter than its diff:
```python
import math

import jax
import jax.numpy as jnp
from jax import lax
from jax.sharding import Mesh, PartitionSpec as P

ROW = ("z", "xl", "y")
AUX = ("xh", "core")
PLANE = ("xl", "y")
BF = jnp.bfloat16
F32 = jnp.float32


def flip(value, axis, mask, size):
    return lax.ppermute(value, axis, [(k, k ^ mask) for k in range(size)])


def shift(value, axis, step, size):
    return lax.ppermute(value, axis, [(k, (k + step) % size) for k in range(size)])


def two_term(value):
    high = lax.reduce_precision(value, 8, 7)
    return high.astype(BF), (value - high).astype(BF)


def on_device(slab, screen, orbitals, hcore):
    quantity, row_count, basis = slab.shape
    occupied = orbitals.shape[1]
    core = lax.axis_index("core")
    aux = lax.axis_index(AUX)
    z = lax.axis_index("z")
    plane = lax.axis_index(PLANE)
    row_devices = lax.axis_size(ROW)
    scale = 1.0 / math.sqrt(quantity * 4 * occupied)

    halves = orbitals.reshape(2, row_count // 2, occupied)
    own = lax.dynamic_index_in_dim(halves, core, 0, keepdims=False)
    mine = lax.all_to_all(
        jnp.broadcast_to(own[None], (row_devices,) + own.shape), ROW, 0, 0, tiled=True
    )
    other = flip(mine, "core", 1, 2)
    first = jnp.where(core == 0, mine, other)
    second = jnp.where(core == 0, other, mine)
    everything = jnp.stack([first, second], axis=1)

    tile = basis // screen.shape[2]
    tiles = everything.reshape(screen.shape[2], tile, occupied)
    parts = []
    for t in range(screen.shape[1]):
        kept = (tiles * screen[0, t].astype(BF)[:, None, None]).reshape(basis, occupied)
        block = slab[:, t * tile : (t + 1) * tile, :]
        parts.append(
            jnp.einsum("qmn,ni->qmi", block, kept, preferred_element_type=F32).astype(BF)
        )
    half = jnp.concatenate(parts, axis=1)
    flat = jnp.transpose(half, (1, 0, 2)).reshape(row_count, quantity * occupied)
    depth = quantity * occupied

    swapped = lax.ppermute(
        flat, ("xh", "core", "z"), [(a * 4 + k, k * 4 + a) for a in range(4) for k in range(4)]
    )
    rows = [swapped] + [flip(swapped, AUX, m, 4) for m in (1, 2, 3)]
    rows = jnp.stack(rows)
    cols = jnp.zeros((8, row_count, depth), BF)
    cols = lax.dynamic_update_index_in_dim(cols, swapped, plane, 0)
    for m in range(1, 8):
        cols = lax.dynamic_update_index_in_dim(cols, flip(swapped, PLANE, m, 8), plane ^ m, 0)
    cols = cols.reshape(8 * row_count, depth)

    def product(step):
        block = lax.dynamic_index_in_dim(rows, ((z + step) % 4) ^ aux, 0, keepdims=False)
        return lax.dot_general(
            block, cols, (((1,), (1,)), ((), ())), preferred_element_type=F32
        )

    width = cols.shape[0] // 2
    far = product(2).astype(BF)
    far_a = shift(far[:, :width], "z", 1, 4)
    far_b = shift(far[:, width:], "z", -1, 4)
    up = product(1)
    down = product(3)
    up_b = shift(up[:, width:].astype(BF), "z", 1, 4)
    down_a = shift(down[:, :width].astype(BF), "z", -1, 4)
    up_a = shift((up[:, :width] + far_a.astype(F32)).astype(BF), "z", 1, 4)
    down_b = shift((down[:, width:] + far_b.astype(F32)).astype(BF), "z", -1, 4)
    home = product(0)
    left = home[:, :width] + up_a.astype(F32) + down_a.astype(F32)
    right = home[:, width:] + up_b.astype(F32) + down_b.astype(F32)
    exchange = jnp.concatenate([left, right], axis=1) * scale

    col_count = hcore.shape[1]
    column_orbitals = lax.dynamic_slice_in_dim(
        everything.reshape(basis, occupied), aux * col_count, col_count, 0
    )
    high, low = two_term(hcore)
    core_part = jnp.dot(high, column_orbitals, preferred_element_type=F32) + jnp.dot(
        low, column_orbitals, preferred_element_type=F32
    )
    orbit_rows = orbitals.astype(F32)
    core_projection = jnp.dot(orbit_rows.T, core_part, precision=lax.Precision.HIGHEST)
    overlap = lax.dot_general(
        flat, orbitals, (((0,), (0,)), ((), ())), preferred_element_type=F32
    )
    summed = jnp.concatenate([overlap, core_projection], axis=0)
    pieces = summed.reshape(row_devices, -1, occupied)
    piece = jnp.sum(lax.all_to_all(pieces, ROW, 0, 0, tiled=True), axis=0)
    summed = lax.all_to_all(
        jnp.broadcast_to(piece[None], pieces.shape), ROW, 0, 0, tiled=True
    ).reshape(summed.shape)
    overlap, core_projection = summed[:depth], summed[depth:]
    o_high, o_low = two_term(overlap)
    exchange_part = jnp.dot(flat, o_high, preferred_element_type=F32) + jnp.dot(
        flat, o_low, preferred_element_type=F32
    )
    applied = core_part - (0.5 * scale) * exchange_part
    projection = core_projection - (0.5 * scale) * jnp.dot(
        overlap.T, overlap, precision=lax.Precision.HIGHEST
    )
    both = jnp.concatenate([applied, projection], axis=0)
    both = both + flip(both, "core", 1, 2)
    both = both + flip(both, "xh", 1, 2)
    applied, projection = both[:row_count], both[row_count:]
    gradient = applied - jnp.dot(orbit_rows, projection, precision=lax.Precision.HIGHEST)
    return (exchange, gradient)


def solution(mesh):
    finer = Mesh(mesh.devices.reshape(2, 2, 4, 2, 4), AUX + ROW)
    in_specs = (P(AUX, ROW, None), P(AUX, ROW, None), P(ROW, None), P(ROW, AUX))
    out_specs = (P(ROW, AUX), P(ROW, None))
    return jax.shard_map(
        on_device, mesh=finer, in_specs=in_specs, out_specs=out_specs, check_vma=False
    )
```

time: 763 us -> 173 us (0.23); the launches traced: 749 us -> 172 us
  waiting for transfers between devices: 691 us -> 22.9 us
  starting transfers between devices: 0.38 us -> 57.5 us
  blocking collectives: 0 us -> 25.1 us
  local copies, waits for them, and re-layouts: 11.2 us -> 26.8 us
  between operations: 13.8 us -> 1.1 us
  other arithmetic: 2.19 us -> 11 us
    all_gather x2 -> x0, waiting for transfers between devices: 299 us -> none  [the longest x1 174 us: on_device(): lax.all_gather(half_slab, 'row', axis=1, tiled=True)]
    psum x2 -> x0, waiting for transfers between devices: 295 us -> none  [the longest x1 255 us: on_device(): lax.psum(jnp.dot(orbit_rows.T, applied, precision=lax.Precision.HIGHEST),...]
    reduce_scatter x1 -> x0, waiting for transfers between devices: 95.9 us -> none  [on_device(): lax.psum_scatter(partial_rows, 'aux', scatter_dimension=1, tiled=True)]
    ppermute x0 -> x20, starting transfers between devices: none -> 43.2 us  [the longest x13 34.1 us: flip(): return lax.ppermute(value, axis, [(k, k ^ mask) for k in range(size)])]
    all_to_all x0 -> x1, blocking collectives: none -> 25.1 us  [on_device(): lax.all_to_all(jnp.broadcast_to(own[None], (row_devices,) + own.shape), R...]
    ppermute x0 -> x20, waiting for transfers between devices: none -> 22.9 us  [the longest x6 13 us: shift(): lax.ppermute(value, axis, [(k, (k + step) % size) for k in range(size)])]
    all_to_all x0 -> x2, starting transfers between devices: none -> 14.3 us  [the longest x1 10.5 us: on_device(): piece = jnp.sum(lax.all_to_all(pieces, ROW, 0, 0, tiled=True), axis=0)]
    broadcast_in_dim x0 -> x11, local copies, waits for them, and re-layouts: none -> 14.3 us  [the longest x7 13.1 us: on_device(): lax.dynamic_update_index_in_dim(cols, flip(swapped, PLANE, m, 8), plane ^...]
  transfers between devices with their start and end apart: 5 -> 22, of which waited for: 5 -> 6; matrix products, arithmetic and copies ran while one was open for 2% -> 24% of each run, Pallas kernels for 0% -> 0%
where the time goes in v1:
time: 173 us; the launch traced here: 172 us
  starting transfers between devices  57.5 us (33%)
  matrix products  27.2 us (16%)
  local copies, waits for them, and re-layouts  26.8 us (15%)
  blocking collectives  25.1 us (15%)
  waiting for transfers between devices  22.9 us (13%)
  other arithmetic  11 us (6%)
    ppermute x13, starting transfers between devices, flip(): return lax.ppermute(value, axis, [(k, k ^ mask) for k in range(size)])  34.1 us
    all_to_all x1, blocking collectives, on_device(): lax.all_to_all(jnp.broadcast_to(own[None], (row_devices,) + own.shape), R...  25.1 us
    dot_general x2, matrix products, on_device(): jnp.einsum('qmn,ni->qmi', block, kept, preferred_element_type=F32)  14.1 us
    broadcast_in_dim x7, local copies, waits for them, and re-layouts, on_device(): lax.dynamic_update_index_in_dim(cols, flip(swapped, PLANE, m, 8), plane ^...  13.1 us
    ppermute x6, waiting for transfers between devices, shift(): lax.ppermute(value, axis, [(k, (k + step) % size) for k in range(size)])  13 us
    all_to_all x1, starting transfers between devices, on_device(): piece = jnp.sum(lax.all_to_all(pieces, ROW, 0, 0, tiled=True), axis=0)  10.5 us
    ppermute x6, starting transfers between devices, shift(): lax.ppermute(value, axis, [(k, (k + step) % size) for k in range(size)])  6.63 us
    unnamed x44, local copies, waits for them, and re-layouts  6.48 us
  transfers between devices with their start and end apart: 22, of which 6 were waited for; matrix products, arithmetic and copies ran while one was open for 24% of the time, Pallas kernels for 0%

profile of v1, /device:TPU:1, one launch (start us, length us, event | category | flops | bytes accessed | tf_op | source)
XLA Modules:
  0.0 171.5 jit_solution(15445388998682795704)
XLA Ops:
  1.7 25.1 %all_to_all.15 = bf16[32,128,128]{2,1,0:T(8,128)(2,1)S(1)} all-to-all(bf16[32,128,128]{2,1,0:T(8,128)(2,1)S(1)} %broadcast_in_dim.43), channel_id=1, replica_groups=mesh['xh'=2,'core'=2,'z'=4,'xl'=2,'y'=4] {'z','xl','y'}, dimensions={0} | all-to-all | bytes 2097152 | tf_op jit(solution)/shard_map/all_to_all | solution.py:40
  26.8 1.8 %collective-permute-start = (bf16[32,128,128]{2,1,0:T(8,128)(2,1)S(1)}, bf16[32,128,128]{2,1,0:T(8,128)(2,1)S(1)}, u32[]{:S(2)}, u32[]{:S(2)}) collective-permute-start(bf16[32,128,128]{2,1,0:T(8,128)(2,1)S(1)} %all_to_all.15), channel_id=1, source_target_pairs={{0,32},{32,0},{1,33},{33,1},{2,34},{34,2},{3,35},{35,3},{4,36},{36... | collective-permute-start | bytes 3145736 | tf_op jit(solution)/shard_map/ppermute | solution.py:16
  28.8 2.2 %collective-permute-done = bf16[32,128,128]{2,1,0:T(8,128)(2,1)S(1)} collective-permute-done((bf16[32,128,128]{2,1,0:T(8,128)(2,1)S(1)}, bf16[32,128,128]{2,1,0:T(8,128)(2,1)S(1)}, u32[]{:S(2)}, u32[]{:S(2)}) %collective-permute-start) | collective-permute-done | bytes 1048608 | tf_op jit(solution)/shard_map/ppermute | solution.py:16
  31.3 7.4 %fusion.19 = bf16[5,128,128]{2,1,0:T(8,128)(2,1)S(1)} fusion(bf16[5,256,8192]{2,1,0:T(8,128)(2,1)} %param.4, bf16[8192,128]{1,0:T(8,128)(2,1)S(1)} %bitcast.97, bf16[8192]{0:T(1024)(128)(2,1)S(1)} %get-tuple-element.16), kind=kOutput, calls=%fused_computation.17 | convolution fusion | flops 1346453504 | bytes 12763136 | tf_op jit(solution)/shard_map/qmn,ni->qmi/dot_general | solution.py:55
  38.7 6.8 %fusion.24 = bf16[5,128,128]{2,1,0:T(8,128)(2,1)S(1)} fusion(bf16[5,256,8192]{2,1,0:T(8,128)(2,1)} %param.4, bf16[8192,128]{1,0:T(8,128)(2,1)S(1)} %bitcast.98, bf16[8192]{0:T(1024)(128)(2,1)S(1)} %get-tuple-element.17), kind=kOutput, calls=%fused_computation.18 | convolution fusion | flops 1346453504 | bytes 12763136 | tf_op jit(solution)/shard_map/qmn,ni->qmi/dot_general | solution.py:55
  45.7 2.4 %collective-permute-start.1 = (bf16[256,640]{0,1:T(8,128)(2,1)S(1)}, bf16[256,640]{0,1:T(8,128)(2,1)}, u32[]{:S(2)}, u32[]{:S(2)}) collective-permute-start(bf16[256,640]{0,1:T(8,128)(2,1)S(1)} %bitcast.93), channel_id=1, source_target_pairs={{0,0},{8,32},{16,64},{24,96},{32,8},{40,40},{48,72},{56,104},{64,1... | collective-permute-start | bytes 983048 | tf_op jit(solution)/shard_map/ppermute | solution.py:61
  48.1 1.5 convolution_bitcast_fusion.1
  49.9 1.5 convolution_add_fusion.1
  51.4 4.1 %collective-permute-done.1 = bf16[256,640]{0,1:T(8,128)(2,1)} collective-permute-done((bf16[256,640]{0,1:T(8,128)(2,1)S(1)}, bf16[256,640]{0,1:T(8,128)(2,1)}, u32[]{:S(2)}, u32[]{:S(2)}) %collective-permute-start.1) | collective-permute-done | bytes 327712 | tf_op jit(solution)/shard_map/ppermute | solution.py:61
  55.6 1.7 collective-permute-start.11
  57.3 3.6 %collective-permute-start.10 = (bf16[256,640]{0,1:T(8,128)(2,1)}, bf16[256,640]{0,1:T(8,128)(2,1)S(1)}, u32[]{:S(2)}, u32[]{:S(2)}) collective-permute-start(bf16[256,640]{0,1:T(8,128)(2,1)} %collective-permute-done.1), channel_id=1, source_target_pairs={{0,6},{1,7},{2,4},{3,5},{4,2},{5,3},{6,0},{7,1},{8,14},{9,15},{10,... | collective-permute-start | bytes 983048 | tf_op jit(solution)/shard_map/ppermute | solution.py:16
  63.0 10.5 %all-to-all-start.1 = ((f32[32,24,128]{2,1,0:T(8,128)}), f32[32,24,128]{2,1,0:T(8,128)S(1)}, u32[]{:S(2)}, u32[]{:S(2)}) async-start(f32[32,24,128]{2,1,0:T(8,128)} %bitcast.34), calls=%async_computation.1 | async-start | bytes 786432 | tf_op jit(solution)/shard_map/all_to_all | solution.py:108
  73.4 2.8 %collective-permute-start.6 = (bf16[256,640]{0,1:T(8,128)(2,1)}, bf16[256,640]{0,1:T(8,128)(2,1)}, u32[]{:S(2)}, u32[]{:S(2)}) collective-permute-start(bf16[256,640]{0,1:T(8,128)(2,1)} %collective-permute-done.1), channel_id=1, source_target_pairs={{0,2},{1,3},{2,0},{3,1},{4,6},{5,7},{6,4},{7,5},{8,10},{9,11},{10,... | collective-permute-start | bytes 983048 | tf_op jit(solution)/shard_map/ppermute | solution.py:16
  76.5 3.5 %collective-permute-done.9 = bf16[256,640]{0,1:T(8,128)(2,1)S(1)} collective-permute-done((bf16[256,640]{0,1:T(8,128)(2,1)}, bf16[256,640]{0,1:T(8,128)(2,1)S(1)}, u32[]{:S(2)}, u32[]{:S(2)}) %collective-permute-start.9) | collective-permute-done | bytes 327712 | tf_op jit(solution)/shard_map/ppermute | solution.py:16
  80.1 10.9 %collective-permute-start.4 = (bf16[256,640]{0,1:T(8,128)(2,1)}, bf16[256,640]{0,1:T(8,128)(2,1)}, u32[]{:S(2)}, u32[]{:S(2)}) collective-permute-start(bf16[256,640]{0,1:T(8,128)(2,1)} %collective-permute-done.1), channel_id=1, source_target_pairs={{0,96},{32,64},{64,32},{96,0},{1,97},{33,65},{65,33},{97,1},{2,98}... | collective-permute-start | bytes 983048 | tf_op jit(solution)/shard_map/ppermute | solution.py:16
  91.0 3.9 %collective-permute-start.3 = (bf16[256,640]{0,1:T(8,128)(2,1)}, bf16[256,640]{0,1:T(8,128)(2,1)}, u32[]{:S(2)}, u32[]{:S(2)}) collective-permute-start(bf16[256,640]{0,1:T(8,128)(2,1)} %collective-permute-done.1), channel_id=1, source_target_pairs={{0,64},{32,96},{64,0},{96,32},{1,65},{33,97},{65,1},{97,33},{2,66}... | collective-permute-start | bytes 983048 | tf_op jit(solution)/shard_map/ppermute | solution.py:16
  94.9 3.0 %collective-permute-start.2 = (bf16[256,640]{0,1:T(8,128)(2,1)}, bf16[256,640]{0,1:T(8,128)(2,1)}, u32[]{:S(2)}, u32[]{:S(2)}) collective-permute-start(bf16[256,640]{0,1:T(8,128)(2,1)} %collective-permute-done.1), channel_id=1, source_target_pairs={{0,32},{32,0},{64,96},{96,64},{1,33},{33,1},{65,97},{97,65},{2,34}... | collective-permute-start | bytes 983048 | tf_op jit(solution)/shard_map/ppermute | solution.py:16
  97.9 1.9 %copy.22 = bf16[1,256,640]{2,1,0:T(8,128)(2,1)} copy(bf16[1,256,640]{1,2,0:T(8,128)(2,1)} %bitcast.16) | data formatting | bytes 655360 | tf_op jit(solution)/shard_map/stack | solution.py:65
  101.6 3.9 %all-to-all-start.2 = ((f32[32,24,128]{2,1,0:T(8,128)}), f32[32,24,128]{2,1,0:T(8,128)S(1)}, u32[]{:S(2)}, u32[]{:S(2)}) async-start(f32[32,24,128]{2,1,0:T(8,128)} %broadcast_in_dim.52), calls=%async_computation.2 | async-start | bytes 786432 | tf_op jit(solution)/shard_map/all_to_all | solution.py:109
  105.5 1.9 %copy.29 = bf16[1,256,640]{2,1,0:T(8,128)(2,1)} copy(bf16[1,256,640]{1,2,0:T(8,128)(2,1)} %bitcast.101) | data formatting | bytes 655360 | tf_op jit(solution)/shard_map/jit(dynamic_update_index_in_dim)/broadcast_in_dim | solution.py:69
  107.4 1.9 %copy.28 = bf16[1,256,640]{2,1,0:T(8,128)(2,1)} copy(bf16[1,256,640]{1,2,0:T(8,128)(2,1)} %bitcast.102) | data formatting | bytes 655360 | tf_op jit(solution)/shard_map/jit(dynamic_update_index_in_dim)/broadcast_in_dim | solution.py:69
  109.3 1.9 %copy.27 = bf16[1,256,640]{2,1,0:T(8,128)(2,1)} copy(bf16[1,256,640]{1,2,0:T(8,128)(2,1)} %bitcast.103) | data formatting | bytes 655360 | tf_op jit(solution)/shard_map/jit(dynamic_update_index_in_dim)/broadcast_in_dim | solution.py:69
  111.2 1.9 %copy.26 = bf16[1,256,640]{2,1,0:T(8,128)(2,1)} copy(bf16[1,256,640]{1,2,0:T(8,128)(2,1)} %bitcast.104) | data formatting | bytes 655360 | tf_op jit(solution)/shard_map/jit(dynamic_update_index_in_dim)/broadcast_in_dim | solution.py:69
  113.0 1.9 %copy.25 = bf16[1,256,640]{2,1,0:T(8,128)(2,1)} copy(bf16[1,256,640]{1,2,0:T(8,128)(2,1)} %bitcast.105) | data formatting | bytes 655360 | tf_op jit(solution)/shard_map/jit(dynamic_update_index_in_dim)/broadcast_in_dim | solution.py:69
  114.9 1.9 %copy.24 = bf16[1,256,640]{2,1,0:T(8,128)(2,1)} copy(bf16[1,256,640]{1,2,0:T(8,128)(2,1)} %bitcast.22) | data formatting | bytes 655360 | tf_op jit(solution)/shard_map/jit(dynamic_update_index_in_dim)/broadcast_in_dim | solution.py:69
  116.8 1.9 %copy.23 = bf16[1,256,640]{2,1,0:T(8,128)(2,1)} copy(bf16[1,256,640]{1,2,0:T(8,128)(2,1)} %bitcast.21) | data formatting | bytes 655360 | tf_op jit(solution)/shard_map/jit(dynamic_update_index_in_dim)/broadcast_in_dim | solution.py:69
  118.7 1.5 pad_maximum_fusion.1
  121.9 1.1 convolution_convert_fusion
  124.0 1.2 collective-permute-start.12
  125.1 1.5 collective-permute-start.16
  126.7 1.1 fusion.42
  127.7 1.3 copy-done.2
  129.9 1.3 collective-permute-start.14
  132.7 1.6 copy.40
  134.3 1.6 fusion.31
  135.9 1.2 fusion.30
  137.2 2.0 %collective-permute-start.18 = (f32[384,128]{0,1:T(8,128)S(1)}, f32[384,128]{0,1:T(8,128)S(1)}, u32[]{:S(2)}, u32[]{:S(2)}) collective-permute-start(f32[384,128]{0,1:T(8,128)S(1)} %pad_maximum_fusion.3), channel_id=1, source_target_pairs={{0,32},{32,0},{1,33},{33,1},{2,34},{34,2},{3,35},{35,3},{4,36},{36... | collective-permute-start | bytes 589832 | tf_op jit(solution)/shard_map/ppermute | solution.py:16
  139.2 1.1 fusion.45
  141.1 3.1 %collective-permute-start.19 = (f32[384,128]{0,1:T(8,128)S(1)}, f32[384,128]{0,1:T(8,128)S(1)}, u32[]{:S(2)}, u32[]{:S(2)}) collective-permute-start(f32[384,128]{0,1:T(8,128)S(1)} %fusion.65), channel_id=1, source_target_pairs={{0,64},{64,0},{1,65},{65,1},{2,66},{66,2},{3,67},{67,3},{4,68},{68... | collective-permute-start | bytes 589832 | tf_op jit(solution)/shard_map/ppermute | solution.py:16
  144.3 2.0 %fusion.33 = bf16[256,1024]{1,0:T(8,128)(2,1)} fusion(f32[256,2048]{1,0:T(8,128)S(1)} %copy-done.3, bf16[256,1024]{1,0:T(8,128)(2,1)} %collective-permute-done.16), kind=kLoop, calls=%fused_computation.29 | loop fusion | flops 786432 | bytes 2097152 | tf_op jit(solution)/shard_map/convert_element_type | solution.py:87
  146.3 2.7 %collective-permute-start.17 = (bf16[256,1024]{1,0:T(8,128)(2,1)}, bf16[256,1024]{1,0:T(8,128)(2,1)}, u32[]{:S(2)}, u32[]{:S(2)}) collective-permute-start(bf16[256,1024]{1,0:T(8,128)(2,1)} %fusion.33), channel_id=1, source_target_pairs={{0,24},{8,0},{16,8},{24,16},{1,25},{9,1},{17,9},{25,17},{2,26},{10... | collective-permute-start | bytes 1572872 | tf_op jit(solution)/shard_map/ppermute | solution.py:20
  148.9 2.0 %fusion.35 = bf16[256,1024]{1,0:T(8,128)(2,1)} fusion(f32[256,2048]{1,0:T(8,128)S(1)} %fusion.45, bf16[256,1024]{1,0:T(8,128)(2,1)} %collective-permute-done.12), kind=kLoop, calls=%fused_computation.35 | loop fusion | flops 786432 | bytes 2097152 | tf_op jit(solution)/shard_map/convert_element_type | solution.py:86
  151.0 2.4 %fusion.47 = f32[256,2048]{1,0:T(8,128)} fusion(bf16[2048,640]{1,0:T(8,128)(2,1)S(1)} %bitcast.88, bf16[4,256,640]{1,2,0:T(8,128)(2,1)S(1)} %copy-done.5, s32[]{:T(128)S(6)} %select_n.81), kind=kOutput, calls=%fused_computation.54 | convolution fusion | flops 671088640 | bytes 5046276 | tf_op jit(solution)/shard_map/dot_general | solution.py:74
  154.4 1.8 %collective-permute-done.15 = bf16[256,1024]{1,0:T(8,128)(2,1)} collective-permute-done((bf16[256,1024]{1,0:T(8,128)(2,1)}, bf16[256,1024]{1,0:T(8,128)(2,1)}, u32[]{:S(2)}, u32[]{:S(2)}) %collective-permute-start.15) | collective-permute-done | bytes 524320 | tf_op jit(solution)/shard_map/ppermute | solution.py:20
  156.2 4.4 %collective-permute-done.17 = bf16[256,1024]{1,0:T(8,128)(2,1)} collective-permute-done((bf16[256,1024]{1,0:T(8,128)(2,1)}, bf16[256,1024]{1,0:T(8,128)(2,1)}, u32[]{:S(2)}, u32[]{:S(2)}) %collective-permute-start.17) | collective-permute-done | bytes 524320 | tf_op jit(solution)/shard_map/ppermute | solution.py:20
  160.6 6.8 %collective-permute-done.13 = bf16[256,1024]{1,0:T(8,128)(2,1)} collective-permute-done((bf16[256,1024]{1,0:T(8,128)(2,1)}, bf16[256,1024]{1,0:T(8,128)(2,1)}, u32[]{:S(2)}, u32[]{:S(2)}) %collective-permute-start.13) | collective-permute-done | bytes 524320 | tf_op jit(solution)/shard_map/ppermute | solution.py:20
  167.4 2.6 %fusion.36 = (f32[256,1024]{1,0:T(8,128)S(1)}, f32[256,1024]{1,0:T(8,128)S(1)}) fusion(f32[256,2048]{1,0:T(8,128)} %fusion.47, bf16[256,1024]{1,0:T(8,128)(2,1)} %collective-permute-done.14, bf16[256,1024]{1,0:T(8,128)(2,1)} %collective-permute-done.13, bf16[256,1024]{1,0:T(8,128)(2,1)} %collective-permute-done.17, bf16[256,1024]{1,0:T(8,128)(2,1)} %collective-permute-done.15), kind=kLoop, calls=%fused_computation.37 | loop fusion | flops 2097152 | bytes 6291456 | tf_op jit(solution)/shard_map/add | solution.py:89
  170.0 1.5 maximum_multiply_fusion
  (96 shorter events, 13.2 us)
Async XLA Ops:
  0.6 0.8 copy-start
  0.6 28.0 %copy-start.20 = (s32[1,2,64]{2,1,0:T(2,128)S(1)}, s32[1,2,64]{2,1,0:T(2,128)}, u32[]{:S(2)}) copy-start(s32[1,2,64]{2,1,0:T(2,128)} %param.5) | copy-start | bytes 1540
  26.8 4.1 %collective-permute-start = (bf16[32,128,128]{2,1,0:T(8,128)(2,1)S(1)}, bf16[32,128,128]{2,1,0:T(8,128)(2,1)S(1)}, u32[]{:S(2)}, u32[]{:S(2)}) collective-permute-start(bf16[32,128,128]{2,1,0:T(8,128)(2,1)S(1)} %all_to_all.15), channel_id=1, source_target_pairs={{0,32},{32,0},{1,33},{33,1},{2,34},{34,2},{3,35},{35,3},{4,36},{36... | collective-permute-start | bytes 3145736 | tf_op jit(solution)/shard_map/ppermute | solution.py:16
  31.3 7.4 %copy-start.6 = (bf16[32,2,128,128]{3,2,1,0:T(8,128)(2,1)}, bf16[32,2,128,128]{3,2,1,0:T(8,128)(2,1)S(1)}, u32[]{:S(2)}) copy-start(bf16[32,2,128,128]{3,2,1,0:T(8,128)(2,1)S(1)} %pad_maximum_fusion) | copy-start | bytes 6291460
  38.7 9.4 %copy-start.1 = (f32[256,2048]{1,0:T(8,128)S(1)}, f32[256,2048]{1,0:T(8,128)}, u32[]{:S(2)}) copy-start(f32[256,2048]{1,0:T(8,128)} %param.7) | copy-start | bytes 6291460
  45.7 9.9 %collective-permute-start.1 = (bf16[256,640]{0,1:T(8,128)(2,1)S(1)}, bf16[256,640]{0,1:T(8,128)(2,1)}, u32[]{:S(2)}, u32[]{:S(2)}) collective-permute-start(bf16[256,640]{0,1:T(8,128)(2,1)S(1)} %bitcast.93), channel_id=1, source_target_pairs={{0,0},{8,32},{16,64},{24,96},{32,8},{40,40},{48,72},{56,104},{64,1... | collective-permute-start | bytes 983048 | tf_op jit(solution)/shard_map/ppermute | solution.py:61
  55.6 17.9 %collective-permute-start.11 = (bf16[256,640]{0,1:T(8,128)(2,1)}, bf16[256,640]{0,1:T(8,128)(2,1)S(1)}, u32[]{:S(2)}, u32[]{:S(2)}) collective-permute-start(bf16[256,640]{0,1:T(8,128)(2,1)} %collective-permute-done.1), channel_id=1, source_target_pairs={{0,7},{1,6},{2,5},{3,4},{4,3},{5,2},{6,1},{7,0},{8,15},{9,14},{10,... | collective-permute-start | bytes 983048 | tf_op jit(solution)/shard_map/ppermute | solution.py:16
  57.3 19.0 %collective-permute-start.10 = (bf16[256,640]{0,1:T(8,128)(2,1)}, bf16[256,640]{0,1:T(8,128)(2,1)S(1)}, u32[]{:S(2)}, u32[]{:S(2)}) collective-permute-start(bf16[256,640]{0,1:T(8,128)(2,1)} %collective-permute-done.1), channel_id=1, source_target_pairs={{0,6},{1,7},{2,4},{3,5},{4,2},{5,3},{6,0},{7,1},{8,14},{9,15},{10,... | collective-permute-start | bytes 983048 | tf_op jit(solution)/shard_map/ppermute | solution.py:16
  60.8 19.2 %collective-permute-start.9 = (bf16[256,640]{0,1:T(8,128)(2,1)}, bf16[256,640]{0,1:T(8,128)(2,1)S(1)}, u32[]{:S(2)}, u32[]{:S(2)}) collective-permute-start(bf16[256,640]{0,1:T(8,128)(2,1)} %collective-permute-done.1), channel_id=1, source_target_pairs={{0,5},{1,4},{2,7},{3,6},{4,1},{5,0},{6,3},{7,2},{8,13},{9,12},{10,... | collective-permute-start | bytes 983048 | tf_op jit(solution)/shard_map/ppermute | solution.py:16
  61.1 29.9 %collective-permute-start.8 = (bf16[256,640]{0,1:T(8,128)(2,1)}, bf16[256,640]{0,1:T(8,128)(2,1)S(1)}, u32[]{:S(2)}, u32[]{:S(2)}) collective-permute-start(bf16[256,640]{0,1:T(8,128)(2,1)} %collective-permute-done.1), channel_id=1, source_target_pairs={{0,4},{1,5},{2,6},{3,7},{4,0},{5,1},{6,2},{7,3},{8,12},{9,13},{10,... | collective-permute-start | bytes 983048 | tf_op jit(solution)/shard_map/ppermute | solution.py:16
  61.1 33.7 %collective-permute-start.7 = (bf16[256,640]{0,1:T(8,128)(2,1)}, bf16[256,640]{0,1:T(8,128)(2,1)S(1)}, u32[]{:S(2)}, u32[]{:S(2)}) collective-permute-start(bf16[256,640]{0,1:T(8,128)(2,1)} %collective-permute-done.1), channel_id=1, source_target_pairs={{0,3},{1,2},{2,1},{3,0},{4,7},{5,6},{6,5},{7,4},{8,11},{9,10},{10,... | collective-permute-start | bytes 983048 | tf_op jit(solution)/shard_map/ppermute | solution.py:16
  63.0 37.8 %all-to-all-start.1 = ((f32[32,24,128]{2,1,0:T(8,128)}), f32[32,24,128]{2,1,0:T(8,128)S(1)}, u32[]{:S(2)}, u32[]{:S(2)}) async-start(f32[32,24,128]{2,1,0:T(8,128)} %bitcast.34), calls=%async_computation.1 | async-start | bytes 786432 | tf_op jit(solution)/shard_map/all_to_all | solution.py:108
  73.4 24.4 %copy-start.15 = (bf16[256,640]{0,1:T(8,128)(2,1)}, bf16[256,640]{0,1:T(8,128)(2,1)S(1)}, u32[]{:S(2)}) copy-start(bf16[256,640]{0,1:T(8,128)(2,1)S(1)} %collective-permute-done.11) | copy-start | bytes 983044
  73.4 41.5 %collective-permute-start.6 = (bf16[256,640]{0,1:T(8,128)(2,1)}, bf16[256,640]{0,1:T(8,128)(2,1)}, u32[]{:S(2)}, u32[]{:S(2)}) collective-permute-start(bf16[256,640]{0,1:T(8,128)(2,1)} %collective-permute-done.1), channel_id=1, source_target_pairs={{0,2},{1,3},{2,0},{3,1},{4,6},{5,7},{6,4},{7,5},{8,10},{9,11},{10,... | collective-permute-start | bytes 983048 | tf_op jit(solution)/shard_map/ppermute | solution.py:16
  76.3 21.6 %copy-start.16 = (bf16[256,640]{0,1:T(8,128)(2,1)}, bf16[256,640]{0,1:T(8,128)(2,1)S(1)}, u32[]{:S(2)}) copy-start(bf16[256,640]{0,1:T(8,128)(2,1)S(1)} %collective-permute-done.10) | copy-start | bytes 983044
  76.3 40.5 %collective-permute-start.5 = (bf16[256,640]{0,1:T(8,128)(2,1)}, bf16[256,640]{0,1:T(8,128)(2,1)}, u32[]{:S(2)}, u32[]{:S(2)}) collective-permute-start(bf16[256,640]{0,1:T(8,128)(2,1)} %collective-permute-done.1), channel_id=1, source_target_pairs={{0,1},{1,0},{2,3},{3,2},{4,5},{5,4},{6,7},{7,6},{8,9},{9,8},{10,11... | collective-permute-start | bytes 983048 | tf_op jit(solution)/shard_map/ppermute | solution.py:16
  80.1 17.8 %copy-start.17 = (bf16[256,640]{0,1:T(8,128)(2,1)}, bf16[256,640]{0,1:T(8,128)(2,1)S(1)}, u32[]{:S(2)}) copy-start(bf16[256,640]{0,1:T(8,128)(2,1)S(1)} %collective-permute-done.9) | copy-start | bytes 983044
  80.1 38.6 %collective-permute-start.4 = (bf16[256,640]{0,1:T(8,128)(2,1)}, bf16[256,640]{0,1:T(8,128)(2,1)}, u32[]{:S(2)}, u32[]{:S(2)}) collective-permute-start(bf16[256,640]{0,1:T(8,128)(2,1)} %collective-permute-done.1), channel_id=1, source_target_pairs={{0,96},{32,64},{64,32},{96,0},{1,97},{33,65},{65,33},{97,1},{2,98}... | collective-permute-start | bytes 983048 | tf_op jit(solution)/shard_map/ppermute | solution.py:16
  91.0 6.9 %copy-start.18 = (bf16[256,640]{0,1:T(8,128)(2,1)}, bf16[256,640]{0,1:T(8,128)(2,1)S(1)}, u32[]{:S(2)}) copy-start(bf16[256,640]{0,1:T(8,128)(2,1)S(1)} %collective-permute-done.8) | copy-start | bytes 983044
  91.0 27.7 %collective-permute-start.3 = (bf16[256,640]{0,1:T(8,128)(2,1)}, bf16[256,640]{0,1:T(8,128)(2,1)}, u32[]{:S(2)}, u32[]{:S(2)}) collective-permute-start(bf16[256,640]{0,1:T(8,128)(2,1)} %collective-permute-done.1), channel_id=1, source_target_pairs={{0,64},{32,96},{64,0},{96,32},{1,65},{33,97},{65,1},{97,33},{2,66}... | collective-permute-start | bytes 983048 | tf_op jit(solution)/shard_map/ppermute | solution.py:16
  94.9 3.0 %copy-start.19 = (bf16[256,640]{0,1:T(8,128)(2,1)}, bf16[256,640]{0,1:T(8,128)(2,1)S(1)}, u32[]{:S(2)}) copy-start(bf16[256,640]{0,1:T(8,128)(2,1)S(1)} %collective-permute-done.7) | copy-start | bytes 983044
  94.9 23.8 %collective-permute-start.2 = (bf16[256,640]{0,1:T(8,128)(2,1)}, bf16[256,640]{0,1:T(8,128)(2,1)}, u32[]{:S(2)}, u32[]{:S(2)}) collective-permute-start(bf16[256,640]{0,1:T(8,128)(2,1)} %collective-permute-done.1), channel_id=1, source_target_pairs={{0,32},{32,0},{64,96},{96,64},{1,33},{33,1},{65,97},{97,65},{2,34}... | collective-permute-start | bytes 983048 | tf_op jit(solution)/shard_map/ppermute | solution.py:16
  99.8 1.0 copy-start.14
  101.6 29.6 %all-to-all-start.2 = ((f32[32,24,128]{2,1,0:T(8,128)}), f32[32,24,128]{2,1,0:T(8,128)S(1)}, u32[]{:S(2)}, u32[]{:S(2)}) async-start(f32[32,24,128]{2,1,0:T(8,128)} %broadcast_in_dim.52), calls=%async_computation.2 | async-start | bytes 786432 | tf_op jit(solution)/shard_map/all_to_all | solution.py:109
  118.6 1.6 copy-start.13
  118.6 1.7 copy-start.12
  118.6 1.8 %copy-start.11 = (bf16[1,256,640]{2,1,0:T(8,128)(2,1)S(1)}, bf16[1,256,640]{2,1,0:T(8,128)(2,1)}, u32[]{:S(2)}) copy-start(bf16[1,256,640]{2,1,0:T(8,128)(2,1)} %copy.25) | copy-start | bytes 983044
  118.7 1.8 %copy-start.10 = (bf16[1,256,640]{2,1,0:T(8,128)(2,1)S(1)}, bf16[1,256,640]{2,1,0:T(8,128)(2,1)}, u32[]{:S(2)}) copy-start(bf16[1,256,640]{2,1,0:T(8,128)(2,1)} %copy.26) | copy-start | bytes 983044
  118.7 1.8 %copy-start.9 = (bf16[1,256,640]{2,1,0:T(8,128)(2,1)S(1)}, bf16[1,256,640]{2,1,0:T(8,128)(2,1)}, u32[]{:S(2)}) copy-start(bf16[1,256,640]{2,1,0:T(8,128)(2,1)} %copy.27) | copy-start | bytes 983044
  120.2 6.4 %copy-start.4 = (bf16[4,256,640]{1,2,0:T(8,128)(2,1)}, bf16[4,256,640]{1,2,0:T(8,128)(2,1)S(1)}, u32[]{:S(2)}) copy-start(bf16[4,256,640]{1,2,0:T(8,128)(2,1)S(1)} %pad_maximum_fusion.1) | copy-start | bytes 3932164
  120.3 1.2 copy-start.8
  120.3 1.6 copy-start.7
  124.0 25.0 %collective-permute-start.12 = (bf16[256,1024]{1,0:T(8,128)(2,1)}, bf16[256,1024]{1,0:T(8,128)(2,1)}, u32[]{:S(2)}, u32[]{:S(2)}) collective-permute-start(bf16[256,1024]{1,0:T(8,128)(2,1)} %get-tuple-element.12), channel_id=1, source_target_pairs={{0,8},{8,16},{16,24},{24,0},{1,9},{9,17},{17,25},{25,1},{2,10},{10... | collective-permute-start | bytes 1572872 | tf_op jit(solution)/shard_map/ppermute | solution.py:20
  125.1 19.1 %collective-permute-start.16 = (bf16[256,1024]{1,0:T(8,128)(2,1)}, bf16[256,1024]{1,0:T(8,128)(2,1)}, u32[]{:S(2)}, u32[]{:S(2)}) collective-permute-start(bf16[256,1024]{1,0:T(8,128)(2,1)} %get-tuple-element.13), channel_id=1, source_target_pairs={{0,24},{8,0},{16,8},{24,16},{1,25},{9,1},{17,9},{25,17},{2,26},{10... | collective-permute-start | bytes 1572872 | tf_op jit(solution)/shard_map/ppermute | solution.py:20
  127.7 1.3 copy-start.2
  129.9 24.5 %collective-permute-start.14 = (bf16[256,1024]{1,0:T(8,128)(2,1)}, bf16[256,1024]{1,0:T(8,128)(2,1)}, u32[]{:S(2)}, u32[]{:S(2)}) collective-permute-start(bf16[256,1024]{1,0:T(8,128)(2,1)} %slice.120), channel_id=1, source_target_pairs={{0,24},{8,0},{16,8},{24,16},{1,25},{9,1},{17,9},{25,17},{2,26},{10... | collective-permute-start | bytes 1572872 | tf_op jit(solution)/shard_map/ppermute | solution.py:20
  134.3 4.9 %copy-start.5 = (bf16[4,256,640]{1,2,0:T(8,128)(2,1)S(1)}, bf16[4,256,640]{1,2,0:T(8,128)(2,1)}, u32[]{:S(2)}) copy-start(bf16[4,256,640]{1,2,0:T(8,128)(2,1)} %copy-done.4) | copy-start | bytes 3932164
  137.2 7.1 %copy-start.3 = (f32[256,2048]{1,0:T(8,128)S(1)}, f32[256,2048]{1,0:T(8,128)}, u32[]{:S(2)}) copy-start(f32[256,2048]{1,0:T(8,128)} %copy-done.2) | copy-start | bytes 6291460
  137.2 3.9 %collective-permute-start.18 = (f32[384,128]{0,1:T(8,128)S(1)}, f32[384,128]{0,1:T(8,128)S(1)}, u32[]{:S(2)}, u32[]{:S(2)}) collective-permute-start(f32[384,128]{0,1:T(8,128)S(1)} %pad_maximum_fusion.3), channel_id=1, source_target_pairs={{0,32},{32,0},{1,33},{33,1},{2,34},{34,2},{3,35},{35,3},{4,36},{36... | collective-permute-start | bytes 589832 | tf_op jit(solution)/shard_map/ppermute | solution.py:16
  141.1 15.1 %collective-permute-start.15 = (bf16[256,1024]{1,0:T(8,128)(2,1)}, bf16[256,1024]{1,0:T(8,128)(2,1)}, u32[]{:S(2)}, u32[]{:S(2)}) collective-permute-start(bf16[256,1024]{1,0:T(8,128)(2,1)} %slice.119), channel_id=1, source_target_pairs={{0,8},{8,16},{16,24},{24,0},{1,9},{9,17},{17,25},{25,1},{2,10},{10... | collective-permute-start | bytes 1572872 | tf_op jit(solution)/shard_map/ppermute | solution.py:20
  141.1 12.2 %collective-permute-start.19 = (f32[384,128]{0,1:T(8,128)S(1)}, f32[384,128]{0,1:T(8,128)S(1)}, u32[]{:S(2)}, u32[]{:S(2)}) collective-permute-start(f32[384,128]{0,1:T(8,128)S(1)} %fusion.65), channel_id=1, source_target_pairs={{0,64},{64,0},{1,65},{65,1},{2,66},{66,2},{3,67},{67,3},{4,68},{68... | collective-permute-start | bytes 589832 | tf_op jit(solution)/shard_map/ppermute | solution.py:16
  146.3 14.3 %collective-permute-start.17 = (bf16[256,1024]{1,0:T(8,128)(2,1)}, bf16[256,1024]{1,0:T(8,128)(2,1)}, u32[]{:S(2)}, u32[]{:S(2)}) collective-permute-start(bf16[256,1024]{1,0:T(8,128)(2,1)} %fusion.33), channel_id=1, source_target_pairs={{0,24},{8,0},{16,8},{24,16},{1,25},{9,1},{17,9},{25,17},{2,26},{10... | collective-permute-start | bytes 1572872 | tf_op jit(solution)/shard_map/ppermute | solution.py:20
  151.0 16.4 %collective-permute-start.13 = (bf16[256,1024]{1,0:T(8,128)(2,1)}, bf16[256,1024]{1,0:T(8,128)(2,1)}, u32[]{:S(2)}, u32[]{:S(2)}) collective-permute-start(bf16[256,1024]{1,0:T(8,128)(2,1)} %fusion.35), channel_id=1, source_target_pairs={{0,8},{8,16},{16,24},{24,0},{1,9},{9,17},{17,25},{25,1},{2,10},{10... | collective-permute-start | bytes 1572872 | tf_op jit(solution)/shard_map/ppermute | solution.py:20

commit v2 on v1

v2 whole, which is shorter than its diff:
```python
import functools
import math

import jax
import jax.numpy as jnp
from jax import lax
from jax.experimental import pallas as pl
from jax.experimental.pallas import tpu as pltpu
from jax.sharding import Mesh, PartitionSpec as P

ROW = ("z", "xl", "y")
AUX = ("xh", "core")
PLANE = ("xl", "y")
BF = jnp.bfloat16
F32 = jnp.float32
SHARDS = 8
VMEM_LIMIT = 16 * 1024 * 1024


def flip(value, axis, mask, size):
    return lax.ppermute(value, axis, [(k, k ^ mask) for k in range(size)])


def shift(value, axis, step, size):
    return lax.ppermute(value, axis, [(k, (k + step) % size) for k in range(size)])


def spot(s):
    return (s % 2) * 4 + s // 2


def two_term(value):
    high = lax.reduce_precision(value, 8, 7)
    return high.astype(BF), (value - high).astype(BF)


def screened(screen_ref, t, orbit_ref, parity, begin):
    return jnp.concatenate(
        [
            orbit_ref[v] * screen_ref[t, 2 * v + parity].astype(F32).astype(BF)
            for v in range(begin, begin + SHARDS)
        ],
        axis=0,
    )


def one_parity(parity, screen_ref, slab_ref, orbit_ref, t):
    quantity = slab_ref.shape[0]
    shards, tile, _ = orbit_ref.shape
    total = None
    for begin in range(0, shards, SHARDS):
        block = jnp.concatenate(
            [
                slab_ref[
                    :,
                    t * tile : (t + 1) * tile,
                    pl.ds(pl.multiple_of((2 * v + parity) * tile, tile), tile),
                ].reshape(quantity * tile, tile)
                for v in range(begin, begin + SHARDS)
            ],
            axis=1,
        )
        term = jnp.dot(
            block,
            screened(screen_ref, t, orbit_ref, parity, begin),
            preferred_element_type=F32,
        )
        total = term if total is None else total + term
    return total


def begin_kernel(parity_ref, screen_ref, slab_ref, orbit_ref, kept_ref, out_ref, sems):
    quantity, rows, _ = kept_ref.shape
    tile = orbit_ref.shape[1]
    groups = rows // tile
    copies = []
    for t in range(groups):
        for q in range(quantity):
            part = (q, pl.ds(t * tile, tile))
            copies.append(
                pltpu.make_async_copy(slab_ref.at[part], kept_ref.at[part], sems.at[t, q])
            )
            copies[-1].start()
    for t in range(groups):
        for q in range(quantity):
            copies[t * quantity + q].wait()
        out_ref[t] = one_parity(parity_ref[0], screen_ref, kept_ref, orbit_ref, t)


def end_kernel(parity_ref, screen_ref, kept_ref, orbit_ref, begun_ref, out_ref):
    quantity, rows, _ = kept_ref.shape
    tile = orbit_ref.shape[1]
    for t in range(rows // tile):
        total = begun_ref[t] + one_parity(parity_ref[0], screen_ref, kept_ref, orbit_ref, t)
        for q in range(quantity):
            out_ref[t * tile : (t + 1) * tile, q * tile : (q + 1) * tile] = total[
                q * tile : (q + 1) * tile
            ].astype(BF)


def half_begin(parity, screen, slab, orbit):
    quantity, rows, _ = slab.shape
    _, tile, occupied = orbit.shape
    groups = rows // tile
    vmem = pl.BlockSpec(memory_space=pltpu.VMEM)
    smem = pl.BlockSpec(memory_space=pltpu.SMEM)
    return pl.pallas_call(
        begin_kernel,
        in_specs=[smem, smem, pl.BlockSpec(memory_space=pl.ANY), vmem],
        out_specs=[vmem, vmem],
        out_shape=[
            jax.ShapeDtypeStruct(slab.shape, BF),
            jax.ShapeDtypeStruct((groups, quantity * tile, occupied), F32),
        ],
        scratch_shapes=[pltpu.SemaphoreType.DMA((groups, quantity))],
        compiler_params=pltpu.CompilerParams(vmem_limit_bytes=VMEM_LIMIT),
        cost_estimate=pl.CostEstimate(
            flops=slab.size * occupied, bytes_accessed=2 * slab.size, transcendentals=0
        ),
    )(parity, screen, slab, orbit)


def half_end(parity, screen, kept, orbit, begun):
    quantity, rows, _ = kept.shape
    vmem = pl.BlockSpec(memory_space=pltpu.VMEM)
    smem = pl.BlockSpec(memory_space=pltpu.SMEM)
    return pl.pallas_call(
        end_kernel,
        in_specs=[smem, smem, vmem, vmem, vmem],
        out_specs=vmem,
        out_shape=jax.ShapeDtypeStruct((rows, quantity * orbit.shape[2]), BF),
        compiler_params=pltpu.CompilerParams(vmem_limit_bytes=VMEM_LIMIT),
        cost_estimate=pl.CostEstimate(
            flops=kept.size * orbit.shape[2], bytes_accessed=kept.size, transcendentals=0
        ),
    )(parity, screen, kept, orbit, begun)


def plain(body, out_shape, scalars, *args):
    vmem = pl.BlockSpec(memory_space=pltpu.VMEM)
    return pl.pallas_call(
        body,
        in_specs=[pl.BlockSpec(memory_space=pltpu.SMEM)] + [vmem] * len(args),
        out_specs=[vmem] * len(out_shape),
        out_shape=out_shape,
        compiler_params=pltpu.CompilerParams(vmem_limit_bytes=VMEM_LIMIT),
        cost_estimate=pl.CostEstimate(
            flops=10**9, bytes_accessed=4 * 10**6, transcendentals=0
        ),
    )(scalars, *args)


def chosen(where_ref, step, rows):
    at = where_ref[step]
    block = rows[0][...]
    for m in (1, 2, 3):
        block = jnp.where(at == m, rows[m][...], block)
    return block


def times(block, cols):
    return lax.dot_general(
        block, cols, (((1,), (1,)), ((), ())), preferred_element_type=F32
    )


def product_kernel(where_ref, r0, r1, r2, r3, c1, c2, c3, c4, *outs):
    n = c1.shape[0]
    for step, out_a, out_b in zip((2, 1, 3, 0), outs[::2], outs[1::2], strict=True):
        block = chosen(where_ref, step, (r0, r1, r2, r3))
        own = times(block, r0[...])
        out_a[:, :n] = times(block, c1[...]).astype(out_a.dtype)
        out_a[:, n : 2 * n] = times(block, c2[...]).astype(out_a.dtype)
        out_a[:, 2 * n :] = own[:, : n // 2].astype(out_a.dtype)
        out_b[:, :n] = times(block, c3[...]).astype(out_b.dtype)
        out_b[:, n : 2 * n] = times(block, c4[...]).astype(out_b.dtype)
        out_b[:, 2 * n :] = own[:, n // 2 :].astype(out_b.dtype)


def relay_kernel(_, up_a, far_a, down_b, far_b, out_a, out_b):
    out_a[...] = (up_a[...] + far_a[...].astype(F32)).astype(BF)
    out_b[...] = (down_b[...] + far_b[...].astype(F32)).astype(BF)


def home_kernel(_, home_a, up_a, down_a, home_b, up_b, down_b, a_ref, b_ref, t1, t2, t3, *, scale):
    n = t1.shape[0]
    a = (home_a[...] + up_a[...].astype(F32) + down_a[...].astype(F32)) * scale
    b = (home_b[...] + up_b[...].astype(F32) + down_b[...].astype(F32)) * scale
    a_ref[...] = a
    b_ref[...] = b
    t1[...] = a[:, :n].astype(BF)
    t2[...] = a[:, n : 2 * n].astype(BF)
    t3[...] = b[:, :n].astype(BF)


def place_kernel(place_ref, a_ref, b_ref, t1, t2, t3, out_ref):
    n = t1.shape[0]

    def at(k):
        return pl.ds(pl.multiple_of(place_ref[k] * n, 128), n)

    out_ref[:, at(1)] = a_ref[:, :n]
    out_ref[:, at(2)] = a_ref[:, n : 2 * n]
    out_ref[:, at(3)] = b_ref[:, :n]
    out_ref[:, at(4)] = b_ref[:, n : 2 * n]
    out_ref[:, at(0)] = jnp.concatenate([a_ref[:, 2 * n :], b_ref[:, 2 * n :]], axis=1)
    out_ref[:, at(7)] = t1[...].astype(F32).T
    out_ref[:, at(6)] = t2[...].astype(F32).T
    out_ref[:, at(5)] = t3[...].astype(F32).T


def on_device(slab, screen, orbitals, hcore):
    quantity, row_count, basis = slab.shape
    occupied = orbitals.shape[1]
    depth = quantity * occupied
    core = lax.axis_index("core")
    aux = lax.axis_index(AUX)
    z = lax.axis_index("z")
    plane = lax.axis_index("y") * 2 + lax.axis_index("xl")
    row_devices = lax.axis_size(ROW)
    scale = 1.0 / math.sqrt(quantity * 4 * occupied)

    own = lax.dynamic_slice_in_dim(orbitals, core * (row_count // 2), row_count // 2, 0)
    mine = lax.all_to_all(
        jnp.broadcast_to(own[None], (row_devices,) + own.shape), ROW, 0, 0, tiled=True
    )
    other = flip(mine, "core", 1, 2)

    kept, begun = half_begin(core[None], screen[0], slab, mine)
    flat = half_end(1 - core[None], screen[0], kept, other, begun)

    swapped = lax.ppermute(
        flat, ("xh", "core", "z"), [(a * 4 + k, k * 4 + a) for a in range(4) for k in range(4)]
    )
    shards = hcore.shape[1] // row_count
    pair = [lax.dynamic_slice_in_dim(v, aux * shards, shards, 0) for v in (mine, other)]
    column_orbitals = jnp.stack(
        [jnp.where(core == 0, *pair), jnp.where(core == 0, *pair[::-1])], axis=1
    ).reshape(hcore.shape[1], occupied)
    high, low = two_term(hcore)
    core_part = jnp.dot(high, column_orbitals, preferred_element_type=F32) + jnp.dot(
        low, column_orbitals, preferred_element_type=F32
    )
    orbit_rows = orbitals.astype(F32)
    core_projection = jnp.dot(orbit_rows.T, core_part, precision=lax.Precision.HIGHEST)
    overlap = lax.dot_general(
        flat, orbitals, (((0,), (0,)), ((), ())), preferred_element_type=F32
    )
    summed = jnp.concatenate([overlap, core_projection], axis=0)

    factors = [swapped, flip(swapped, "core", 1, 2), flip(swapped, "xh", 1, 2)]
    factors.append(flip(factors[2], "core", 1, 2))
    factors += [
        lax.ppermute(swapped, PLANE, [(spot((s + m) % 8), spot(s)) for s in range(8)])
        for m in (1, 2, 3, 4)
    ]
    pieces = summed.reshape(row_devices, -1, occupied)
    piece = jnp.sum(lax.all_to_all(pieces, ROW, 0, 0, tiled=True), axis=0)
    where = ((z + jnp.arange(4, dtype=jnp.int32)) % 4) ^ aux
    part = jax.ShapeDtypeStruct((row_count, 5 * row_count // 2), BF)
    part_f32 = jax.ShapeDtypeStruct(part.shape, F32)
    far_a, far_b, up_a, up_b, down_a, down_b, home_a, home_b = plain(
        product_kernel,
        [part, part, part_f32, part, part, part_f32, part_f32, part_f32],
        where,
        *factors,
    )
    far_a = shift(far_a, "z", 1, 4)
    far_b = shift(far_b, "z", -1, 4)
    up_b = shift(up_b, "z", 1, 4)
    down_a = shift(down_a, "z", -1, 4)
    up_a, down_b = plain(relay_kernel, [part, part], where, up_a, far_a, down_b, far_b)
    up_a = shift(up_a, "z", 1, 4)
    down_b = shift(down_b, "z", -1, 4)
    tile = jax.ShapeDtypeStruct((row_count, row_count), BF)
    home_a, home_b, *tiles = plain(
        functools.partial(home_kernel, scale=scale),
        [part_f32, part_f32, tile, tile, tile],
        where,
        home_a,
        up_a,
        down_a,
        home_b,
        up_b,
        down_b,
    )
    turned = [
        lax.ppermute(
            tile,
            AUX + ROW,
            [
                (a * 32 + k * 8 + spot(s), k * 32 + a * 8 + spot((s + m) % 8))
                for a in range(4)
                for k in range(4)
                for s in range(8)
            ],
        )
        for m, tile in zip((1, 2, 3), tiles, strict=True)
    ]
    place = spot((plane + jnp.arange(8, dtype=jnp.int32)) % 8)
    (exchange,) = plain(
        place_kernel,
        [jax.ShapeDtypeStruct(hcore.shape, F32)],
        place,
        home_a,
        home_b,
        *turned,
    )

    summed = lax.all_to_all(
        jnp.broadcast_to(piece[None], pieces.shape), ROW, 0, 0, tiled=True
    ).reshape(summed.shape)
    overlap, core_projection = summed[:depth], summed[depth:]
    o_high, o_low = two_term(overlap)
    exchange_part = jnp.dot(flat, o_high, preferred_element_type=F32) + jnp.dot(
        flat, o_low, preferred_element_type=F32
    )
    applied = core_part - (0.5 * scale) * exchange_part
    projection = core_projection - (0.5 * scale) * jnp.dot(
        overlap.T, overlap, precision=lax.Precision.HIGHEST
    )
    both = jnp.concatenate([applied, projection], axis=0)
    both = both + flip(both, "core", 1, 2)
    both = both + flip(both, "xh", 1, 2)
    applied, projection = both[:row_count], both[row_count:]
    gradient = applied - jnp.dot(orbit_rows, projection, precision=lax.Precision.HIGHEST)
    return (exchange, gradient)


def solution(mesh):
    finer = Mesh(mesh.devices.reshape(2, 2, 4, 2, 4), AUX + ROW)
    in_specs = (P(AUX, ROW, None), P(AUX, ROW, None), P(ROW, None), P(ROW, AUX))
    out_specs = (P(ROW, AUX), P(ROW, None))
    return jax.shard_map(
        on_device, mesh=finer, in_specs=in_specs, out_specs=out_specs, check_vma=False
    )
```

time: 173 us -> 160 us (0.925)
  matrix products: 27.2 us -> 5.98 us
  Pallas kernels: 0 us -> 20.6 us
  local copies, waits for them, and re-layouts: 26.8 us -> 7.98 us
  waiting for transfers between devices: 22.9 us -> 37.4 us
  other arithmetic: 11 us -> 1.01 us
  starting transfers between devices: 57.5 us -> 59.8 us
    pallas_call x0 -> x6, Pallas kernels: none -> 20.6 us  [the longest x1 10.5 us: half_begin(): pl.pallas_call(begin_kernel, in_specs=[smem, smem, pl.BlockSpec(memory_sp...]
    ppermute x0 -> x7, starting transfers between devices: none -> 20 us  [the longest x3 12.9 us: on_device(): lax.ppermute(tile, AUX + ROW, [(a * 32 + k * 8 + spot(s), k * 32 + a * 8...]
    dot_general x6 -> x0, matrix products: 19.7 us -> none  [the longest x2 14.1 us: on_device(): jnp.einsum('qmn,ni->qmi', block, kept, preferred_element_type=F32)]
    ppermute x0 -> x7, waiting for transfers between devices: none -> 17.5 us  [the longest x3 14.9 us: on_device(): lax.ppermute(tile, AUX + ROW, [(a * 32 + k * 8 + spot(s), k * 32 + a * 8...]
    ppermute x13 -> x6, starting transfers between devices: 34.1 us -> 17.6 us  [flip(): return lax.ppermute(value, axis, [(k, k ^ mask) for k in range(size)])]
    broadcast_in_dim x8 -> x0, local copies, waits for them, and re-layouts: 13.3 us -> none  [the longest x7 13.1 us: on_device(): lax.dynamic_update_index_in_dim(cols, flip(swapped, PLANE, m, 8), plane ^...]
    all_to_all x1, waiting for transfers between devices: 0.01 us -> 5.51 us  [on_device(): piece = jnp.sum(lax.all_to_all(pieces, ROW, 0, 0, tiled=True), axis=0)]
    ppermute x6, waiting for transfers between devices: 13 us -> 7.59 us  [shift(): lax.ppermute(value, axis, [(k, (k + step) % size) for k in range(size)])]
  transfers between devices with their start and end apart: 22 -> 22, of which waited for: 6 -> 9; matrix products, arithmetic and copies ran while one was open for 24% -> 4% of each run, Pallas kernels for 0% -> 7%
where the time goes in v2:
time: 160 us; the launch traced here: 159 us
  starting transfers between devices  59.8 us (37%)
  waiting for transfers between devices  37.4 us (23%)
  blocking collectives  25.1 us (16%)
  Pallas kernels  20.6 us (13%)
  local copies, waits for them, and re-layouts  7.98 us (5%)
  matrix products  5.98 us (4%)
    all_to_all x1, blocking collectives, on_device(): lax.all_to_all(jnp.broadcast_to(own[None], (row_devices,) + own.shape), R...  25.1 us
    ppermute x6, starting transfers between devices, flip(): return lax.ppermute(value, axis, [(k, k ^ mask) for k in range(size)])  17.6 us
    ppermute x3, waiting for transfers between devices, on_device(): lax.ppermute(tile, AUX + ROW, [(a * 32 + k * 8 + spot(s), k * 32 + a * 8...  14.9 us
    ppermute x3, starting transfers between devices, on_device(): lax.ppermute(tile, AUX + ROW, [(a * 32 + k * 8 + spot(s), k * 32 + a * 8...  12.9 us
    pallas_call x1, Pallas kernels, half_begin(): pl.pallas_call(begin_kernel, in_specs=[smem, smem, pl.BlockSpec(memory_sp...  10.5 us
    ppermute x6, starting transfers between devices, shift(): lax.ppermute(value, axis, [(k, (k + step) % size) for k in range(size)])  8.1 us
    ppermute x6, waiting for transfers between devices, shift(): lax.ppermute(value, axis, [(k, (k + step) % size) for k in range(size)])  7.59 us
    ppermute x4, starting transfers between devices, on_device(): lax.ppermute(swapped, PLANE, [(spot((s + m) % 8), spot(s)) for s in range...  7.05 us
  transfers between devices with their start and end apart: 22, of which 9 were waited for; matrix products, arithmetic and copies ran while one was open for 4% of the time, Pallas kernels for 7%

profile of v2, /device:TPU:1, one launch (start us, length us, event | category | flops | bytes accessed | tf_op | source)
XLA Modules:
  0.0 158.7 jit_solution(3064993627346632504)
XLA Ops:
  0.7 0.8 copy-done
  1.7 25.1 %all_to_all.15.orbit_ref = bf16[32,128,128]{2,1,0:T(8,128)(2,1)S(1)} all-to-all(bf16[32,128,128]{2,1,0:T(8,128)(2,1)S(1)} %broadcast_in_dim.7), channel_id=1, replica_groups=mesh['xh'=2,'core'=2,'z'=4,'xl'=2,'y'=4] {'z','xl','y'}, dimensions={0} | all-to-all | bytes 2097152 | tf_op jit(solution)/shard_map/all_to_all | solution.py:224
  26.8 1.8 %collective-permute-start = (bf16[32,128,128]{2,1,0:T(8,128)(2,1)S(1)}, bf16[32,128,128]{2,1,0:T(8,128)(2,1)S(1)}, u32[]{:S(2)}, u32[]{:S(2)}) collective-permute-start(bf16[32,128,128]{2,1,0:T(8,128)(2,1)S(1)} %all_to_all.15.orbit_ref), channel_id=1, source_target_pairs={{0,32},{32,0},{1,33},{33,1},{2,34},{34,2},{3,35},{35,3},{4,36},{36... | collective-permute-start | bytes 3145736 | tf_op jit(solution)/shard_map/ppermute | solution.py:21
  28.7 10.5 %shard_map.59 = (bf16[5,256,8192]{2,1,0:T(8,128)(2,1)S(1)}, f32[2,640,128]{2,1,0:T(8,128)S(1)}) custom-call(s32[1]{0:T(128)} %bitcast.parity_ref, s32[2,64]{1,0:T(2,128)S(1)} %bitcast.26, bf16[5,256,8192]{2,1,0:T(8,128)(2,1)} %slab_ref.1, bf16[32,128,128]{2,1,0:T(8,128)(2,1)S(1)} %all_to_all.15.orbit_ref), custom_call_target="tpu_custom_call" | custom-call | flops 1342177280 | bytes 20971520 | tf_op jit(solution)/shard_map/pallas_call | solution.py:107
  39.4 1.4 copy-done.6
  40.8 0.5 convolution_bitcast_fusion.1
  41.3 0.5 convolution_add_fusion.1
  42.0 3.7 %shard_map.60 = bf16[256,640]{1,0:T(8,128)(2,1)S(1)} custom-call(s32[1]{0:T(128)S(6)} %sub.23.parity_ref, s32[2,64]{1,0:T(2,128)S(1)} %bitcast.27, bf16[5,256,8192]{2,1,0:T(8,128)(2,1)S(1)} %get-tuple-element.19.kept_ref, bf16[32,128,128]{2,1,0:T(8,128)(2,1)S(1)} %collective-permute-done.orbit_ref, f32[2,640,128]{2,1,0:T(8,128)S(1)} %get-tuple-element.20.begun_ref), custom_call_target="tpu_custom_call" | custom-call | flops 1342177280 | bytes 10485760 | tf_op jit(solution)/shard_map/pallas_call | solution.py:127
  45.7 0.3 fusion.18
  46.0 0.8 pad_maximum_fusion.1
  46.8 5.2 %all-to-all-start.1 = ((f32[32,24,128]{2,1,0:T(8,128)}), f32[32,24,128]{2,1,0:T(8,128)S(1)}, u32[]{:S(2)}, u32[]{:S(2)}) async-start(f32[32,24,128]{2,1,0:T(8,128)} %bitcast.7), calls=%async_computation.1 | async-start | bytes 786432 | tf_op jit(solution)/shard_map/all_to_all | solution.py:258
  52.1 3.6 %collective-permute-start.1 = (bf16[256,640]{1,0:T(8,128)(2,1)S(1)}, bf16[256,640]{1,0:T(8,128)(2,1)S(1)}, u32[]{:S(2)}, u32[]{:S(2)}) collective-permute-start(bf16[256,640]{1,0:T(8,128)(2,1)S(1)} %shard_map.60), channel_id=1, source_target_pairs={{0,0},{8,32},{16,64},{24,96},{32,8},{40,40},{48,72},{56,104},{64,1... | collective-permute-start | bytes 983048 | tf_op jit(solution)/shard_map/ppermute | solution.py:232
  55.7 5.5 %all-to-all-done.1 = f32[32,24,128]{2,1,0:T(8,128)S(1)} async-done(((f32[32,24,128]{2,1,0:T(8,128)}), f32[32,24,128]{2,1,0:T(8,128)S(1)}, u32[]{:S(2)}, u32[]{:S(2)}) %all-to-all-start.1) | async-done | bytes 393248 | tf_op jit(solution)/shard_map/all_to_all | solution.py:258
  61.2 0.8 broadcast_in_dim.8
  62.0 5.2 %all-to-all-start.2 = ((f32[32,24,128]{2,1,0:T(8,128)}), f32[32,24,128]{2,1,0:T(8,128)}, u32[]{:S(2)}, u32[]{:S(2)}) async-start(f32[32,24,128]{2,1,0:T(8,128)} %broadcast_in_dim.8), calls=%async_computation.2 | async-start | bytes 786432 | tf_op jit(solution)/shard_map/all_to_all | solution.py:310
  67.3 3.2 %collective-permute-start.3 = (bf16[256,640]{1,0:T(8,128)(2,1)S(1)}, bf16[256,640]{1,0:T(8,128)(2,1)S(1)}, u32[]{:S(2)}, u32[]{:S(2)}) collective-permute-start(bf16[256,640]{1,0:T(8,128)(2,1)S(1)} %collective-permute-done.1.r0), channel_id=1, source_target_pairs={{0,64},{64,0},{1,65},{65,1},{2,66},{66,2},{3,67},{67,3},{4,68},{68... | collective-permute-start | bytes 983048 | tf_op jit(solution)/shard_map/ppermute | solution.py:21
  70.4 1.7 %collective-permute-start.2 = (bf16[256,640]{1,0:T(8,128)(2,1)S(1)}, bf16[256,640]{1,0:T(8,128)(2,1)S(1)}, u32[]{:S(2)}, u32[]{:S(2)}) collective-permute-start(bf16[256,640]{1,0:T(8,128)(2,1)S(1)} %collective-permute-done.1.r0), channel_id=1, source_target_pairs={{0,32},{32,0},{1,33},{33,1},{2,34},{34,2},{3,35},{35,3},{4,36},{36... | collective-permute-start | bytes 983048 | tf_op jit(solution)/shard_map/ppermute | solution.py:21
  72.2 2.9 %collective-permute-start.5 = (bf16[256,640]{1,0:T(8,128)(2,1)S(1)}, bf16[256,640]{1,0:T(8,128)(2,1)S(1)}, u32[]{:S(2)}, u32[]{:S(2)}) collective-permute-start(bf16[256,640]{1,0:T(8,128)(2,1)S(1)} %collective-permute-done.1.r0), channel_id=1, source_target_pairs={{4,0},{1,4},{5,1},{2,5},{6,2},{3,6},{7,3},{0,7},{12,8},{9,12},{13,... | collective-permute-start | bytes 983048 | tf_op jit(solution)/shard_map/ppermute | solution.py:254
  75.1 0.6 collective-permute-start.6
  75.7 0.9 collective-permute-start.7
  76.5 3.2 %collective-permute-done.3.r2 = bf16[256,640]{1,0:T(8,128)(2,1)S(1)} collective-permute-done((bf16[256,640]{1,0:T(8,128)(2,1)S(1)}, bf16[256,640]{1,0:T(8,128)(2,1)S(1)}, u32[]{:S(2)}, u32[]{:S(2)}) %collective-permute-start.3) | collective-permute-done | bytes 327712 | tf_op jit(solution)/shard_map/ppermute | solution.py:21
  79.7 2.7 %collective-permute-start.8 = (bf16[256,640]{1,0:T(8,128)(2,1)S(1)}, bf16[256,640]{1,0:T(8,128)(2,1)S(1)}, u32[]{:S(2)}, u32[]{:S(2)}) collective-permute-start(bf16[256,640]{1,0:T(8,128)(2,1)S(1)} %collective-permute-done.1.r0), channel_id=1, source_target_pairs={{2,0},{6,4},{3,1},{7,5},{0,2},{4,6},{1,3},{5,7},{10,8},{14,12},{11... | collective-permute-start | bytes 983048 | tf_op jit(solution)/shard_map/ppermute | solution.py:254
  82.4 5.7 %collective-permute-start.4 = (bf16[256,640]{1,0:T(8,128)(2,1)S(1)}, bf16[256,640]{1,0:T(8,128)(2,1)S(1)}, u32[]{:S(2)}, u32[]{:S(2)}) collective-permute-start(bf16[256,640]{1,0:T(8,128)(2,1)S(1)} %collective-permute-done.3.r2), channel_id=1, source_target_pairs={{0,32},{32,0},{1,33},{33,1},{2,34},{34,2},{3,35},{35,3},{4,36},{36... | collective-permute-start | bytes 983048 | tf_op jit(solution)/shard_map/ppermute | solution.py:21
  88.1 1.2 fusion.7
  89.3 0.8 slice.17
  90.3 1.2 fusion.2
  91.6 2.5 %collective-permute-done.7.c3 = bf16[256,640]{1,0:T(8,128)(2,1)S(1)} collective-permute-done((bf16[256,640]{1,0:T(8,128)(2,1)S(1)}, bf16[256,640]{1,0:T(8,128)(2,1)S(1)}, u32[]{:S(2)}, u32[]{:S(2)}) %collective-permute-start.7) | collective-permute-done | bytes 327712 | tf_op jit(solution)/shard_map/ppermute | solution.py:254
  94.1 2.8 %shard_map.61 = (bf16[256,640]{1,0:T(8,128)(2,1)S(1)}, bf16[256,640]{1,0:T(8,128)(2,1)S(1)}, f32[256,640]{1,0:T(8,128)S(1)}, bf16[256,640]{1,0:T(8,128)(2,1)S(1)...) custom-call(s32[4]{0:T(128)S(1)} %fusion.14.where_ref._, ...), custom_call_target="tpu_custom_call" | custom-call | flops 1000000000 | bytes 4000000 | tf_op jit(solution)/shard_map/pallas_call | solution.py:141
  96.9 0.8 copy-done.4
  97.7 2.4 %collective-permute-start.10 = (bf16[256,640]{1,0:T(8,128)(2,1)S(1)}, bf16[256,640]{1,0:T(8,128)(2,1)S(1)}, u32[]{:S(2)}, u32[]{:S(2)}) collective-permute-start(bf16[256,640]{1,0:T(8,128)(2,1)S(1)} %get-tuple-element.25), channel_id=1, source_target_pairs={{0,24},{8,0},{16,8},{24,16},{1,25},{9,1},{17,9},{25,17},{2,26},{10... | collective-permute-start | bytes 983048 | tf_op jit(solution)/shard_map/ppermute | solution.py:25
  100.1 1.8 %fusion.3 = f32[128,128]{0,1:T(8,128)S(1)} fusion(f32[128,128]{0,1:T(8,128)S(1)} %copy.22, f32[768,128]{1,0:T(8,128)} %bitcast.8), kind=kOutput, calls=%fused_computation.10 | convolution fusion | flops 125861888 | bytes 458752 | tf_op jit(solution)/shard_map/dot_general | solution.py:319
  101.9 2.7 %collective-permute-start.18 = (f32[384,128]{0,1:T(8,128)S(1)}, f32[384,128]{0,1:T(8,128)S(1)}, u32[]{:S(2)}, u32[]{:S(2)}) collective-permute-start(f32[384,128]{0,1:T(8,128)S(1)} %pad_maximum_fusion.2), channel_id=1, source_target_pairs={{0,32},{32,0},{1,33},{33,1},{2,34},{34,2},{3,35},{35,3},{4,36},{36... | collective-permute-start | bytes 589832 | tf_op jit(solution)/shard_map/ppermute | solution.py:21
  104.6 3.0 %collective-permute-start.12 = (bf16[256,640]{1,0:T(8,128)(2,1)S(1)}, bf16[256,640]{1,0:T(8,128)(2,1)S(1)}, u32[]{:S(2)}, u32[]{:S(2)}) collective-permute-start(bf16[256,640]{1,0:T(8,128)(2,1)S(1)} %get-tuple-element.27), channel_id=1, source_target_pairs={{0,24},{8,0},{16,8},{24,16},{1,25},{9,1},{17,9},{25,17},{2,26},{10... | collective-permute-start | bytes 983048 | tf_op jit(solution)/shard_map/ppermute | solution.py:25
  107.8 0.7 shard_map.62
  108.6 2.7 %collective-permute-start.14 = (bf16[256,640]{1,0:T(8,128)(2,1)S(1)}, bf16[256,640]{1,0:T(8,128)(2,1)S(1)}, u32[]{:S(2)}, u32[]{:S(2)}) collective-permute-start(bf16[256,640]{1,0:T(8,128)(2,1)S(1)} %get-tuple-element.30), channel_id=1, source_target_pairs={{0,24},{8,0},{16,8},{24,16},{1,25},{9,1},{17,9},{25,17},{2,26},{10... | collective-permute-start | bytes 983048 | tf_op jit(solution)/shard_map/ppermute | solution.py:25
  111.3 2.4 %collective-permute-start.19 = (f32[384,128]{0,1:T(8,128)S(1)}, f32[384,128]{0,1:T(8,128)S(1)}, u32[]{:S(2)}, u32[]{:S(2)}) collective-permute-start(f32[384,128]{0,1:T(8,128)S(1)} %fusion.17), channel_id=1, source_target_pairs={{0,64},{64,0},{1,65},{65,1},{2,66},{66,2},{3,67},{67,3},{4,68},{68... | collective-permute-start | bytes 589832 | tf_op jit(solution)/shard_map/ppermute | solution.py:21
  113.7 3.7 %collective-permute-done.19 = f32[384,128]{0,1:T(8,128)S(1)} collective-permute-done((f32[384,128]{0,1:T(8,128)S(1)}, f32[384,128]{0,1:T(8,128)S(1)}, u32[]{:S(2)}, u32[]{:S(2)}) %collective-permute-start.19) | collective-permute-done | bytes 196640 | tf_op jit(solution)/shard_map/ppermute | solution.py:21
  117.4 0.3 collective-permute-done.13.up_b
  117.8 7.0 %collective-permute-done.11.up_a = bf16[256,640]{1,0:T(8,128)(2,1)S(1)} collective-permute-done((bf16[256,640]{1,0:T(8,128)(2,1)S(1)}, bf16[256,640]{1,0:T(8,128)(2,1)S(1)}, u32[]{:S(2)}, u32[]{:S(2)}) %collective-permute-start.11) | collective-permute-done | bytes 327712 | tf_op jit(solution)/shard_map/ppermute | solution.py:25
  124.8 1.1 copy-done.3
  125.9 1.1 copy-done.5
  127.0 0.8 shard_map.63
  127.8 9.3 %collective-permute-start.15 = (bf16[256,256]{1,0:T(8,128)(2,1)S(1)}, bf16[256,256]{1,0:T(8,128)(2,1)S(1)}, u32[]{:S(2)}, u32[]{:S(2)}) collective-permute-start(bf16[256,256]{1,0:T(8,128)(2,1)S(1)} %get-tuple-element.33), channel_id=1, source_target_pairs={{0,4},{4,1},{1,5},{5,2},{2,6},{6,3},{3,7},{7,0},{8,36},{12,33},{9,... | collective-permute-start | bytes 393224 | tf_op jit(solution)/shard_map/ppermute | solution.py:288
  137.1 3.7 %collective-permute-start.16 = (bf16[256,256]{1,0:T(8,128)(2,1)S(1)}, bf16[256,256]{1,0:T(8,128)(2,1)S(1)}, u32[]{:S(2)}, u32[]{:S(2)}) collective-permute-start(bf16[256,256]{1,0:T(8,128)(2,1)S(1)} %get-tuple-element.34), channel_id=1, source_target_pairs={{0,1},{4,5},{1,2},{5,6},{2,3},{6,7},{3,0},{7,4},{8,33},{12,37},{9,... | collective-permute-start | bytes 393224 | tf_op jit(solution)/shard_map/ppermute | solution.py:288
  141.0 0.8 copy.17
  141.7 6.9 %collective-permute-done.15.t1 = bf16[256,256]{1,0:T(8,128)(2,1)S(1)} collective-permute-done((bf16[256,256]{1,0:T(8,128)(2,1)S(1)}, bf16[256,256]{1,0:T(8,128)(2,1)S(1)}, u32[]{:S(2)}, u32[]{:S(2)}) %collective-permute-start.15) | collective-permute-done | bytes 131104 | tf_op jit(solution)/shard_map/ppermute | solution.py:288
  148.6 8.0 %collective-permute-done.16.t2 = bf16[256,256]{1,0:T(8,128)(2,1)S(1)} collective-permute-done((bf16[256,256]{1,0:T(8,128)(2,1)S(1)}, bf16[256,256]{1,0:T(8,128)(2,1)S(1)}, u32[]{:S(2)}, u32[]{:S(2)}) %collective-permute-start.16) | collective-permute-done | bytes 131104 | tf_op jit(solution)/shard_map/ppermute | solution.py:288
  156.7 2.1 %shard_map.64 = f32[256,2048]{1,0:T(8,128)} custom-call(s32[8]{0:T(128)S(1)} %fusion.13.place_ref, f32[256,640]{1,0:T(8,128)S(1)} %get-tuple-element.31.a_ref, f32[256,640]{1,0:T(8,128)S(1)} %get-tuple-element.32.b_ref, bf16[256,256]{1,0:T(8,128)(2,1)S(1)} %collective-permute-done.15.t1, bf16[256,256]{1,0:T(8,128)(2,1)S(1)} %collective-permute-done.16.t2, ...), custom_call_target="tpu_custom_call" | custom-call | flops 1000000000 | bytes 4000000 | tf_op jit(solution)/shard_map/pallas_call | solution.py:141
  (41 shorter events, 1.4 us)
Async XLA Ops:
  0.6 0.8 copy-start
  0.6 28.0 %copy-start.1 = (s32[1,2,64]{2,1,0:T(2,128)S(1)}, s32[1,2,64]{2,1,0:T(2,128)}, u32[]{:S(2)}) copy-start(s32[1,2,64]{2,1,0:T(2,128)} %param.5) | copy-start | bytes 1540
  26.8 12.4 %collective-permute-start = (bf16[32,128,128]{2,1,0:T(8,128)(2,1)S(1)}, bf16[32,128,128]{2,1,0:T(8,128)(2,1)S(1)}, u32[]{:S(2)}, u32[]{:S(2)}) collective-permute-start(bf16[32,128,128]{2,1,0:T(8,128)(2,1)S(1)} %all_to_all.15.orbit_ref), channel_id=1, source_target_pairs={{0,32},{32,0},{1,33},{33,1},{2,34},{34,2},{3,35},{35,3},{4,36},{36... | collective-permute-start | bytes 3145736 | tf_op jit(solution)/shard_map/ppermute | solution.py:21
  39.2 1.6 %copy-start.6 = (f32[256,2048]{1,0:T(8,128)S(1)}, f32[256,2048]{1,0:T(8,128)}, u32[]{:S(2)}) copy-start(f32[256,2048]{1,0:T(8,128)} %param.7) | copy-start | bytes 6291460
  46.8 14.4 %all-to-all-start.1 = ((f32[32,24,128]{2,1,0:T(8,128)}), f32[32,24,128]{2,1,0:T(8,128)S(1)}, u32[]{:S(2)}, u32[]{:S(2)}) async-start(f32[32,24,128]{2,1,0:T(8,128)} %bitcast.7), calls=%async_computation.1 | async-start | bytes 786432 | tf_op jit(solution)/shard_map/all_to_all | solution.py:258
  52.1 15.2 %collective-permute-start.1 = (bf16[256,640]{1,0:T(8,128)(2,1)S(1)}, bf16[256,640]{1,0:T(8,128)(2,1)S(1)}, u32[]{:S(2)}, u32[]{:S(2)}) collective-permute-start(bf16[256,640]{1,0:T(8,128)(2,1)S(1)} %shard_map.60), channel_id=1, source_target_pairs={{0,0},{8,32},{16,64},{24,96},{32,8},{40,40},{48,72},{56,104},{64,1... | collective-permute-start | bytes 983048 | tf_op jit(solution)/shard_map/ppermute | solution.py:232
  62.0 26.1 %all-to-all-start.2 = ((f32[32,24,128]{2,1,0:T(8,128)}), f32[32,24,128]{2,1,0:T(8,128)}, u32[]{:S(2)}, u32[]{:S(2)}) async-start(f32[32,24,128]{2,1,0:T(8,128)} %broadcast_in_dim.8), calls=%async_computation.2 | async-start | bytes 786432 | tf_op jit(solution)/shard_map/all_to_all | solution.py:310
  67.3 12.5 %collective-permute-start.3 = (bf16[256,640]{1,0:T(8,128)(2,1)S(1)}, bf16[256,640]{1,0:T(8,128)(2,1)S(1)}, u32[]{:S(2)}, u32[]{:S(2)}) collective-permute-start(bf16[256,640]{1,0:T(8,128)(2,1)S(1)} %collective-permute-done.1.r0), channel_id=1, source_target_pairs={{0,64},{64,0},{1,65},{65,1},{2,66},{66,2},{3,67},{67,3},{4,68},{68... | collective-permute-start | bytes 983048 | tf_op jit(solution)/shard_map/ppermute | solution.py:21
  70.4 12.0 %collective-permute-start.2 = (bf16[256,640]{1,0:T(8,128)(2,1)S(1)}, bf16[256,640]{1,0:T(8,128)(2,1)S(1)}, u32[]{:S(2)}, u32[]{:S(2)}) collective-permute-start(bf16[256,640]{1,0:T(8,128)(2,1)S(1)} %collective-permute-done.1.r0), channel_id=1, source_target_pairs={{0,32},{32,0},{1,33},{33,1},{2,34},{34,2},{3,35},{35,3},{4,36},{36... | collective-permute-start | bytes 983048 | tf_op jit(solution)/shard_map/ppermute | solution.py:21
  72.2 19.4 %collective-permute-start.5 = (bf16[256,640]{1,0:T(8,128)(2,1)S(1)}, bf16[256,640]{1,0:T(8,128)(2,1)S(1)}, u32[]{:S(2)}, u32[]{:S(2)}) collective-permute-start(bf16[256,640]{1,0:T(8,128)(2,1)S(1)} %collective-permute-done.1.r0), channel_id=1, source_target_pairs={{4,0},{1,4},{5,1},{2,5},{6,2},{3,6},{7,3},{0,7},{12,8},{9,12},{13,... | collective-permute-start | bytes 983048 | tf_op jit(solution)/shard_map/ppermute | solution.py:254
  75.1 16.4 %collective-permute-start.6 = (bf16[256,640]{1,0:T(8,128)(2,1)S(1)}, bf16[256,640]{1,0:T(8,128)(2,1)S(1)}, u32[]{:S(2)}, u32[]{:S(2)}) collective-permute-start(bf16[256,640]{1,0:T(8,128)(2,1)S(1)} %collective-permute-done.1.r0), channel_id=1, source_target_pairs={{1,0},{5,4},{2,1},{6,5},{3,2},{7,6},{0,3},{4,7},{9,8},{13,12},{10,... | collective-permute-start | bytes 983048 | tf_op jit(solution)/shard_map/ppermute | solution.py:254
  75.7 18.4 %collective-permute-start.7 = (bf16[256,640]{1,0:T(8,128)(2,1)S(1)}, bf16[256,640]{1,0:T(8,128)(2,1)S(1)}, u32[]{:S(2)}, u32[]{:S(2)}) collective-permute-start(bf16[256,640]{1,0:T(8,128)(2,1)S(1)} %collective-permute-done.1.r0), channel_id=1, source_target_pairs={{5,0},{2,4},{6,1},{3,5},{7,2},{0,6},{4,3},{1,7},{13,8},{10,12},{14... | collective-permute-start | bytes 983048 | tf_op jit(solution)/shard_map/ppermute | solution.py:254
  79.7 14.4 %collective-permute-start.8 = (bf16[256,640]{1,0:T(8,128)(2,1)S(1)}, bf16[256,640]{1,0:T(8,128)(2,1)S(1)}, u32[]{:S(2)}, u32[]{:S(2)}) collective-permute-start(bf16[256,640]{1,0:T(8,128)(2,1)S(1)} %collective-permute-done.1.r0), channel_id=1, source_target_pairs={{2,0},{6,4},{3,1},{7,5},{0,2},{4,6},{1,3},{5,7},{10,8},{14,12},{11... | collective-permute-start | bytes 983048 | tf_op jit(solution)/shard_map/ppermute | solution.py:254
  82.4 11.7 %collective-permute-start.4 = (bf16[256,640]{1,0:T(8,128)(2,1)S(1)}, bf16[256,640]{1,0:T(8,128)(2,1)S(1)}, u32[]{:S(2)}, u32[]{:S(2)}) collective-permute-start(bf16[256,640]{1,0:T(8,128)(2,1)S(1)} %collective-permute-done.3.r2), channel_id=1, source_target_pairs={{0,32},{32,0},{1,33},{33,1},{2,34},{34,2},{3,35},{35,3},{4,36},{36... | collective-permute-start | bytes 983048 | tf_op jit(solution)/shard_map/ppermute | solution.py:21
  96.9 0.8 copy-start.4
  97.7 10.8 %copy-start.2 = (f32[256,640]{1,0:T(8,128)}, f32[256,640]{1,0:T(8,128)S(1)}, u32[]{:S(2)}) copy-start(f32[256,640]{1,0:T(8,128)S(1)} %get-tuple-element.21.home_a) | copy-start | bytes 1966084
  97.7 9.9 %collective-permute-start.10 = (bf16[256,640]{1,0:T(8,128)(2,1)S(1)}, bf16[256,640]{1,0:T(8,128)(2,1)S(1)}, u32[]{:S(2)}, u32[]{:S(2)}) collective-permute-start(bf16[256,640]{1,0:T(8,128)(2,1)S(1)} %get-tuple-element.25), channel_id=1, source_target_pairs={{0,24},{8,0},{16,8},{24,16},{1,25},{9,1},{17,9},{25,17},{2,26},{10... | collective-permute-start | bytes 983048 | tf_op jit(solution)/shard_map/ppermute | solution.py:25
  100.1 7.7 %collective-permute-start.9 = (bf16[256,640]{1,0:T(8,128)(2,1)S(1)}, bf16[256,640]{1,0:T(8,128)(2,1)S(1)}, u32[]{:S(2)}, u32[]{:S(2)}) collective-permute-start(bf16[256,640]{1,0:T(8,128)(2,1)S(1)} %get-tuple-element.23), channel_id=1, source_target_pairs={{0,8},{8,16},{16,24},{24,0},{1,9},{9,17},{17,25},{25,1},{2,10},{10... | collective-permute-start | bytes 983048 | tf_op jit(solution)/shard_map/ppermute | solution.py:25
  101.9 9.4 %collective-permute-start.18 = (f32[384,128]{0,1:T(8,128)S(1)}, f32[384,128]{0,1:T(8,128)S(1)}, u32[]{:S(2)}, u32[]{:S(2)}) collective-permute-start(f32[384,128]{0,1:T(8,128)S(1)} %pad_maximum_fusion.2), channel_id=1, source_target_pairs={{0,32},{32,0},{1,33},{33,1},{2,34},{34,2},{3,35},{35,3},{4,36},{36... | collective-permute-start | bytes 589832 | tf_op jit(solution)/shard_map/ppermute | solution.py:21
  104.6 12.8 %collective-permute-start.12 = (bf16[256,640]{1,0:T(8,128)(2,1)S(1)}, bf16[256,640]{1,0:T(8,128)(2,1)S(1)}, u32[]{:S(2)}, u32[]{:S(2)}) collective-permute-start(bf16[256,640]{1,0:T(8,128)(2,1)S(1)} %get-tuple-element.27), channel_id=1, source_target_pairs={{0,24},{8,0},{16,8},{24,16},{1,25},{9,1},{17,9},{25,17},{2,26},{10... | collective-permute-start | bytes 983048 | tf_op jit(solution)/shard_map/ppermute | solution.py:25
  107.6 10.2 %collective-permute-start.13 = (bf16[256,640]{1,0:T(8,128)(2,1)S(1)}, bf16[256,640]{1,0:T(8,128)(2,1)S(1)}, u32[]{:S(2)}, u32[]{:S(2)}) collective-permute-start(bf16[256,640]{1,0:T(8,128)(2,1)S(1)} %get-tuple-element.29), channel_id=1, source_target_pairs={{0,8},{8,16},{16,24},{24,0},{1,9},{9,17},{17,25},{25,1},{2,10},{10... | collective-permute-start | bytes 983048 | tf_op jit(solution)/shard_map/ppermute | solution.py:25
  108.5 16.3 %collective-permute-start.11 = (bf16[256,640]{1,0:T(8,128)(2,1)S(1)}, bf16[256,640]{1,0:T(8,128)(2,1)S(1)}, u32[]{:S(2)}, u32[]{:S(2)}) collective-permute-start(bf16[256,640]{1,0:T(8,128)(2,1)S(1)} %get-tuple-element.26), channel_id=1, source_target_pairs={{0,8},{8,16},{16,24},{24,0},{1,9},{9,17},{17,25},{25,1},{2,10},{10... | collective-permute-start | bytes 983048 | tf_op jit(solution)/shard_map/ppermute | solution.py:25
  108.6 16.2 %collective-permute-start.14 = (bf16[256,640]{1,0:T(8,128)(2,1)S(1)}, bf16[256,640]{1,0:T(8,128)(2,1)S(1)}, u32[]{:S(2)}, u32[]{:S(2)}) collective-permute-start(bf16[256,640]{1,0:T(8,128)(2,1)S(1)} %get-tuple-element.30), channel_id=1, source_target_pairs={{0,24},{8,0},{16,8},{24,16},{1,25},{9,1},{17,9},{25,17},{2,26},{10... | collective-permute-start | bytes 983048 | tf_op jit(solution)/shard_map/ppermute | solution.py:25
  111.3 6.1 %collective-permute-start.19 = (f32[384,128]{0,1:T(8,128)S(1)}, f32[384,128]{0,1:T(8,128)S(1)}, u32[]{:S(2)}, u32[]{:S(2)}) collective-permute-start(f32[384,128]{0,1:T(8,128)S(1)} %fusion.17), channel_id=1, source_target_pairs={{0,64},{64,0},{1,65},{65,1},{2,66},{66,2},{3,67},{67,3},{4,68},{68... | collective-permute-start | bytes 589832 | tf_op jit(solution)/shard_map/ppermute | solution.py:21
  124.8 1.1 copy-start.3
  125.9 1.1 copy-start.5
  127.8 20.8 %collective-permute-start.15 = (bf16[256,256]{1,0:T(8,128)(2,1)S(1)}, bf16[256,256]{1,0:T(8,128)(2,1)S(1)}, u32[]{:S(2)}, u32[]{:S(2)}) collective-permute-start(bf16[256,256]{1,0:T(8,128)(2,1)S(1)} %get-tuple-element.33), channel_id=1, source_target_pairs={{0,4},{4,1},{1,5},{5,2},{2,6},{6,3},{3,7},{7,0},{8,36},{12,33},{9,... | collective-permute-start | bytes 393224 | tf_op jit(solution)/shard_map/ppermute | solution.py:288
  137.1 19.6 %collective-permute-start.16 = (bf16[256,256]{1,0:T(8,128)(2,1)S(1)}, bf16[256,256]{1,0:T(8,128)(2,1)S(1)}, u32[]{:S(2)}, u32[]{:S(2)}) collective-permute-start(bf16[256,256]{1,0:T(8,128)(2,1)S(1)} %get-tuple-element.34), channel_id=1, source_target_pairs={{0,1},{4,5},{1,2},{5,6},{2,3},{6,7},{3,0},{7,4},{8,33},{12,37},{9,... | collective-permute-start | bytes 393224 | tf_op jit(solution)/shard_map/ppermute | solution.py:288
  140.7 15.9 %collective-permute-start.17 = (bf16[256,256]{1,0:T(8,128)(2,1)S(1)}, bf16[256,256]{1,0:T(8,128)(2,1)S(1)}, u32[]{:S(2)}, u32[]{:S(2)}) collective-permute-start(bf16[256,256]{1,0:T(8,128)(2,1)S(1)} %get-tuple-element.35), channel_id=1, source_target_pairs={{0,5},{4,2},{1,6},{5,3},{2,7},{6,0},{3,4},{7,1},{8,37},{12,34},{9,... | collective-permute-start | bytes 393224 | tf_op jit(solution)/shard_map/ppermute | solution.py:288

commit v3 on v2

v3 whole, which is shorter than its diff:
```python
import functools
import math

import jax
import jax.numpy as jnp
from jax import lax
from jax.experimental import pallas as pl
from jax.experimental.pallas import tpu as pltpu
from jax.sharding import Mesh, PartitionSpec as P

ROW = ("z", "xl", "y")
AUX = ("xh", "core")
PLANE = ("xl", "y")
BF = jnp.bfloat16
F32 = jnp.float32
SHARDS = 8
VMEM_LIMIT = 16 * 1024 * 1024


def flip(value, axis, mask, size):
    return lax.ppermute(value, axis, [(k, k ^ mask) for k in range(size)])


def shift(value, axis, step, size):
    return lax.ppermute(value, axis, [(k, (k + step) % size) for k in range(size)])


def spot(s):
    return (s % 2) * 4 + s // 2


def screened(screen_ref, t, orbit_ref, parity, begin):
    return jnp.concatenate(
        [
            orbit_ref[v] * screen_ref[t, 2 * v + parity].astype(F32).astype(BF)
            for v in range(begin, begin + SHARDS)
        ],
        axis=0,
    )


def one_chunk(parity, screen_ref, slab_ref, orbit_ref, t, begin):
    quantity = slab_ref.shape[0]
    tile = orbit_ref.shape[1]
    block = jnp.concatenate(
        [
            slab_ref[
                :,
                t * tile : (t + 1) * tile,
                pl.ds(pl.multiple_of((2 * v + parity) * tile, tile), tile),
            ].reshape(quantity * tile, tile)
            for v in range(begin, begin + SHARDS)
        ],
        axis=1,
    )
    return jnp.dot(
        block,
        screened(screen_ref, t, orbit_ref, parity, begin),
        preferred_element_type=F32,
    )


def begin_kernel(parity_ref, screen_ref, slab_ref, orbit_ref, kept_ref, out_ref, sems):
    quantity, rows, _ = kept_ref.shape
    shards, tile, _ = orbit_ref.shape
    groups = rows // tile
    width = 2 * SHARDS * tile
    chunks = shards // SHARDS
    copies = [
        pltpu.make_async_copy(
            slab_ref.at[:, :, pl.ds(c * width, width)],
            kept_ref.at[:, :, pl.ds(c * width, width)],
            sems.at[c],
        )
        for c in range(chunks)
    ]
    copies[0].start()
    copies[1].start()
    for c in range(chunks):
        copies[c].wait()
        if c + 2 < chunks:
            copies[c + 2].start()
        for t in range(groups):
            term = one_chunk(
                parity_ref[0], screen_ref, kept_ref, orbit_ref, t, c * SHARDS
            )
            out_ref[t] = term if c == 0 else out_ref[t] + term


def end_kernel(parity_ref, screen_ref, kept_ref, orbit_ref, begun_ref, out_ref):
    quantity, rows, _ = kept_ref.shape
    tile = orbit_ref.shape[1]
    for t in range(rows // tile):
        total = begun_ref[t]
        for begin in range(0, orbit_ref.shape[0], SHARDS):
            total = total + one_chunk(
                parity_ref[0], screen_ref, kept_ref, orbit_ref, t, begin
            )
        for q in range(quantity):
            out_ref[t * tile : (t + 1) * tile, q * tile : (q + 1) * tile] = total[
                q * tile : (q + 1) * tile
            ].astype(BF)


def half_begin(parity, screen, slab, orbit):
    quantity, rows, _ = slab.shape
    _, tile, occupied = orbit.shape
    groups = rows // tile
    vmem = pl.BlockSpec(memory_space=pltpu.VMEM)
    smem = pl.BlockSpec(memory_space=pltpu.SMEM)
    return pl.pallas_call(
        begin_kernel,
        in_specs=[smem, smem, pl.BlockSpec(memory_space=pl.ANY), vmem],
        out_specs=[vmem, vmem],
        out_shape=[
            jax.ShapeDtypeStruct(slab.shape, BF),
            jax.ShapeDtypeStruct((groups, quantity * tile, occupied), F32),
        ],
        scratch_shapes=[pltpu.SemaphoreType.DMA((orbit.shape[0] // SHARDS,))],
        compiler_params=pltpu.CompilerParams(vmem_limit_bytes=VMEM_LIMIT),
        cost_estimate=pl.CostEstimate(
            flops=slab.size * occupied, bytes_accessed=2 * slab.size, transcendentals=0
        ),
    )(parity, screen, slab, orbit)


def half_end(parity, screen, kept, orbit, begun):
    quantity, rows, _ = kept.shape
    vmem = pl.BlockSpec(memory_space=pltpu.VMEM)
    smem = pl.BlockSpec(memory_space=pltpu.SMEM)
    return pl.pallas_call(
        end_kernel,
        in_specs=[smem, smem, vmem, vmem, vmem],
        out_specs=vmem,
        out_shape=jax.ShapeDtypeStruct((rows, quantity * orbit.shape[2]), BF),
        compiler_params=pltpu.CompilerParams(vmem_limit_bytes=VMEM_LIMIT),
        cost_estimate=pl.CostEstimate(
            flops=kept.size * orbit.shape[2], bytes_accessed=kept.size, transcendentals=0
        ),
    )(parity, screen, kept, orbit, begun)


def plain(body, out_shape, scalars, *args, flops=10**9, limit=8 * 1024 * 1024):
    vmem = pl.BlockSpec(memory_space=pltpu.VMEM)
    return pl.pallas_call(
        body,
        in_specs=[pl.BlockSpec(memory_space=pltpu.SMEM)] + [vmem] * len(args),
        out_specs=[vmem] * len(out_shape),
        out_shape=out_shape,
        compiler_params=pltpu.CompilerParams(vmem_limit_bytes=limit),
        cost_estimate=pl.CostEstimate(
            flops=flops, bytes_accessed=4 * 10**6, transcendentals=0
        ),
    )(scalars, *args)


def chosen(where_ref, step, rows):
    at = where_ref[step]
    block = rows[0][...]
    for m in (1, 2, 3):
        block = jnp.where(at == m, rows[m][...], block)
    return block


def times(block, cols):
    return lax.dot_general(
        block, cols, (((1,), (1,)), ((), ())), preferred_element_type=F32
    )


def product_kernel(where_ref, r0, r1, r2, r3, c1, c2, c3, c4, *outs):
    n = c1.shape[0]
    for step, out_a, out_b in zip((2, 1, 3, 0), outs[::2], outs[1::2], strict=True):
        block = chosen(where_ref, step, (r0, r1, r2, r3))
        own = times(block, r0[...])
        out_a[:, :n] = times(block, c1[...]).astype(out_a.dtype)
        out_a[:, n : 2 * n] = times(block, c2[...]).astype(out_a.dtype)
        out_a[:, 2 * n :] = own[:, : n // 2].astype(out_a.dtype)
        out_b[:, :n] = times(block, c3[...]).astype(out_b.dtype)
        out_b[:, n : 2 * n] = times(block, c4[...]).astype(out_b.dtype)
        out_b[:, 2 * n :] = own[:, n // 2 :].astype(out_b.dtype)


def relay_kernel(_, up_a, far_a, down_b, far_b, out_a, out_b):
    out_a[...] = (up_a[...] + far_a[...].astype(F32)).astype(BF)
    out_b[...] = (down_b[...] + far_b[...].astype(F32)).astype(BF)


def home_kernel(
    place_ref, home_a, up_a, down_a, home_b, up_b, down_b, out_ref, t1, t2, t3, *, scale
):
    n = t1.shape[0]

    def at(k):
        return pl.ds(pl.multiple_of(place_ref[k] * n, 128), n)

    a = (home_a[...] + up_a[...].astype(F32) + down_a[...].astype(F32)) * scale
    b = (home_b[...] + up_b[...].astype(F32) + down_b[...].astype(F32)) * scale
    t1[...] = a[:, :n].astype(BF)
    t2[...] = a[:, n : 2 * n].astype(BF)
    t3[...] = b[:, :n].astype(BF)
    out_ref[:, at(1)] = a[:, :n]
    out_ref[:, at(2)] = a[:, n : 2 * n]
    out_ref[:, at(3)] = b[:, :n]
    out_ref[:, at(4)] = b[:, n : 2 * n]
    out_ref[:, at(0)] = jnp.concatenate([a[:, 2 * n :], b[:, 2 * n :]], axis=1)


def two_terms(value):
    high = value.astype(BF)
    return high, (value - high.astype(F32)).astype(BF)


def inner(left, right):
    return lax.dot_general(left, right, (((0,), (0,)), ((), ())), preferred_element_type=F32)


def outer(left, right):
    return jnp.dot(left, right, preferred_element_type=F32)


def sums_kernel(where_ref, flat_ref, orbit_ref, mine_ref, other_ref, hcore_ref, out_ref, part_ref):
    depth = flat_ref.shape[1]
    tile = mine_ref.shape[1]
    shards = hcore_ref.shape[1] // (2 * tile)
    begins_here = where_ref[0] == 0
    columns = []
    for v in range(shards):
        at = where_ref[1] * shards + v
        mine, other = mine_ref[at], other_ref[at]
        columns.append(jnp.where(begins_here, mine, other))
        columns.append(jnp.where(begins_here, other, mine))
    columns = jnp.concatenate(columns, axis=0)
    high, low = two_terms(hcore_ref[...])
    part = outer(high, columns) + outer(low, columns)
    part_ref[...] = part
    orbit = orbit_ref[...]
    high, low = two_terms(part)
    out_ref[:depth] = inner(flat_ref[...], orbit)
    out_ref[depth:] = inner(orbit, high) + inner(orbit, low)


def spread_kernel(_, pieces_ref, out_ref):
    total = jnp.sum(pieces_ref[...], axis=0)
    out_ref[...] = jnp.broadcast_to(total[None], out_ref.shape)


def applied_kernel(_, flat_ref, summed_ref, part_ref, out_ref, *, factor):
    rows, depth = flat_ref.shape
    high, low = two_terms(summed_ref[:depth])
    flat = flat_ref[...]
    out_ref[:rows] = part_ref[...] - factor * (outer(flat, high) + outer(flat, low))
    out_ref[rows:] = summed_ref[depth:] - factor * (
        inner(high, high) + inner(high, low) + inner(low, high)
    )


def add_kernel(_, left, right, out_ref):
    out_ref[...] = left[...] + right[...]


def gradient_kernel(_, orbit_ref, left, right, out_ref):
    rows = orbit_ref.shape[0]
    high, low = two_terms(left[rows:] + right[rows:])
    orbit = orbit_ref[...]
    out_ref[...] = left[:rows] + right[:rows] - (outer(orbit, high) + outer(orbit, low))


def place_kernel(place_ref, t1, t2, t3, _, out_ref, turned, sems):
    n = t1.shape[0]
    copies = []
    for k, tile in enumerate((t1, t2, t3)):
        turned[k] = tile[...].astype(F32).T
        at = pl.ds(pl.multiple_of(place_ref[7 - k] * n, 128), n)
        copies.append(pltpu.make_async_copy(turned.at[k], out_ref.at[:, at], sems.at[k]))
        copies[-1].start()
    for copy in copies:
        copy.wait()


def place(where, tiles, out):
    n = tiles[0].shape[0]
    vmem = pl.BlockSpec(memory_space=pltpu.VMEM)
    hbm = pl.BlockSpec(memory_space=pl.ANY)
    return pl.pallas_call(
        place_kernel,
        in_specs=[pl.BlockSpec(memory_space=pltpu.SMEM)] + [vmem] * 3 + [hbm],
        out_specs=hbm,
        out_shape=jax.ShapeDtypeStruct(out.shape, out.dtype),
        input_output_aliases={4: 0},
        scratch_shapes=[pltpu.VMEM((3, n, n), F32), pltpu.SemaphoreType.DMA((3,))],
        compiler_params=pltpu.CompilerParams(vmem_limit_bytes=VMEM_LIMIT),
    )(where, *tiles, out)


def on_device(slab, screen, orbitals, hcore):
    quantity, row_count, basis = slab.shape
    occupied = orbitals.shape[1]
    depth = quantity * occupied
    core = lax.axis_index("core")
    aux = lax.axis_index(AUX)
    z = lax.axis_index("z")
    plane = lax.axis_index("y") * 2 + lax.axis_index("xl")
    row_devices = lax.axis_size(ROW)
    scale = 1.0 / math.sqrt(quantity * 4 * occupied)

    own = lax.dynamic_slice_in_dim(orbitals, core * (row_count // 2), row_count // 2, 0)
    where = ((z + jnp.arange(4, dtype=jnp.int32)) % 4) ^ aux
    spots = spot((plane + jnp.arange(8, dtype=jnp.int32)) % 8)
    own, here, there, ids, where, spots = lax.optimization_barrier(
        (own, core[None], 1 - core[None], jnp.stack([core, aux]), where, spots)
    )
    mine = lax.all_to_all(
        jnp.broadcast_to(own[None], (row_devices,) + own.shape), ROW, 0, 0, tiled=True
    )
    other = flip(mine, "core", 1, 2)

    kept, begun = half_begin(here, screen[0], slab, mine)
    flat = half_end(there, screen[0], kept, other, begun)

    swapped = lax.ppermute(
        flat, ("xh", "core", "z"), [(a * 4 + k, k * 4 + a) for a in range(4) for k in range(4)]
    )
    summed, core_part = plain(
        sums_kernel,
        [
            jax.ShapeDtypeStruct((depth + occupied, occupied), F32),
            jax.ShapeDtypeStruct((row_count, occupied), F32),
        ],
        ids,
        flat,
        orbitals,
        mine,
        other,
        hcore,
        flops=10**10,
    )

    far_rows = flip(swapped, "xh", 1, 2)
    columns = [
        lax.ppermute(swapped, PLANE, [(spot((s + m) % 8), spot(s)) for s in range(8)])
        for m in (1, 2, 3, 4)
    ]
    swapped, far_rows = lax.optimization_barrier((swapped, far_rows))
    factors = [swapped, flip(swapped, "core", 1, 2), far_rows, flip(far_rows, "core", 1, 2)]
    factors += columns
    pieces = summed.reshape(row_devices, -1, occupied)
    pieces = lax.all_to_all(pieces, ROW, 0, 0, tiled=True)
    pieces, factors[4] = lax.optimization_barrier((pieces, factors[4]))
    part = jax.ShapeDtypeStruct((row_count, 5 * row_count // 2), BF)
    part_f32 = jax.ShapeDtypeStruct(part.shape, F32)
    far_a, far_b, up_a, up_b, down_a, down_b, home_a, home_b = plain(
        product_kernel,
        [part, part, part_f32, part, part, part_f32, part_f32, part_f32],
        where,
        *factors,
    )
    (pieces,) = plain(
        spread_kernel,
        [jax.ShapeDtypeStruct(pieces.shape, F32)],
        where,
        pieces,
        flops=10**10,
    )
    far_a = shift(far_a, "z", 1, 4)
    far_b = shift(far_b, "z", -1, 4)
    up_b = shift(up_b, "z", 1, 4)
    down_a = shift(down_a, "z", -1, 4)
    up_a, down_b = plain(relay_kernel, [part, part], where, up_a, far_a, down_b, far_b)
    up_a = shift(up_a, "z", 1, 4)
    down_b = shift(down_b, "z", -1, 4)
    tile = jax.ShapeDtypeStruct((row_count, row_count), BF)
    exchange, *tiles = plain(
        functools.partial(home_kernel, scale=scale),
        [jax.ShapeDtypeStruct(hcore.shape, F32), tile, tile, tile],
        spots,
        home_a,
        up_a,
        down_a,
        home_b,
        up_b,
        down_b,
    )
    turned = [
        lax.ppermute(
            tile,
            AUX + ROW,
            [
                (a * 32 + k * 8 + spot(s), k * 32 + a * 8 + spot((s + m) % 8))
                for a in range(4)
                for k in range(4)
                for s in range(8)
            ],
        )
        for m, tile in zip((1, 2, 3), tiles, strict=True)
    ]
    exchange = place(spots, turned, exchange)

    summed = lax.all_to_all(pieces, ROW, 0, 0, tiled=True).reshape(summed.shape)
    (both,) = plain(
        functools.partial(applied_kernel, factor=0.5 * scale),
        [jax.ShapeDtypeStruct((row_count + occupied, occupied), F32)],
        where,
        flat,
        summed,
        core_part,
    )
    (both,) = plain(
        add_kernel,
        [jax.ShapeDtypeStruct(both.shape, F32)],
        where,
        both,
        flip(both, "core", 1, 2),
    )
    (gradient,) = plain(
        gradient_kernel,
        [jax.ShapeDtypeStruct((row_count, occupied), F32)],
        where,
        orbitals,
        both,
        flip(both, "xh", 1, 2),
    )
    return (exchange, gradient)


def solution(mesh):
    finer = Mesh(mesh.devices.reshape(2, 2, 4, 2, 4), AUX + ROW)
    in_specs = (P(AUX, ROW, None), P(AUX, ROW, None), P(ROW, None), P(ROW, AUX))
    out_specs = (P(ROW, AUX), P(ROW, None))
    return jax.shard_map(
        on_device, mesh=finer, in_specs=in_specs, out_specs=out_specs, check_vma=False
    )
```

time: 160 us -> 148 us (0.925)
  matrix products: 5.98 us -> 0 us
  Pallas kernels: 20.6 us -> 26.5 us
  waiting for transfers between devices: 37.4 us -> 31.7 us
  starting transfers between devices: 59.8 us -> 55.3 us
    pallas_call x4 -> x8, Pallas kernels: 6.33 us -> 12.8 us  [plain(): pl.pallas_call(body, in_specs=[pl.BlockSpec(memory_space=pltpu.SMEM)] + [...]
    dot_general x8 -> x0, matrix products: 5.98 us -> none  [the longest x1 1.77 us: on_device(): jnp.dot(overlap.T, overlap, precision=lax.Precision.HIGHEST)]
    all_to_all x2, waiting for transfers between devices: 5.52 us -> 0.01 us  [the longest x1 0.01 us: on_device(): pieces = lax.all_to_all(pieces, ROW, 0, 0, tiled=True)]
    ppermute x6, waiting for transfers between devices: 6.84 us -> 10.4 us  [flip(): return lax.ppermute(value, axis, [(k, k ^ mask) for k in range(size)])]
    ppermute x6, starting transfers between devices: 17.6 us -> 15.1 us  [flip(): return lax.ppermute(value, axis, [(k, k ^ mask) for k in range(size)])]
    ppermute x3, waiting for transfers between devices: 14.9 us -> 12.7 us  [on_device(): lax.ppermute(tile, AUX + ROW, [(a * 32 + k * 8 + spot(s), k * 32 + a * 8...]
    pallas_call x1, Pallas kernels: 10.5 us -> 8.69 us  [half_begin(): pl.pallas_call(begin_kernel, in_specs=[smem, smem, pl.BlockSpec(memory_sp...]
    all_to_all x2, starting transfers between devices: 10.5 us -> 12.2 us  [the longest x1 8.18 us: on_device(): pieces = lax.all_to_all(pieces, ROW, 0, 0, tiled=True)]
  transfers between devices with their start and end apart: 22 -> 22, of which waited for: 9 -> 6; matrix products, arithmetic and copies ran while one was open for 4% -> 0% of each run, Pallas kernels for 7% -> 15%
where the time goes in v3:
time: 148 us
  starting transfers between devices  55.3 us (37%)
  waiting for transfers between devices  31.7 us (21%)
  Pallas kernels  26.5 us (18%)
  blocking collectives  25.1 us (17%)
  local copies, waits for them, and re-layouts  7.81 us (5%)
    all_to_all x1, blocking collectives, on_device(): lax.all_to_all(jnp.broadcast_to(own[None], (row_devices,) + own.shape), R...  25.1 us
    ppermute x6, starting transfers between devices, flip(): return lax.ppermute(value, axis, [(k, k ^ mask) for k in range(size)])  15.1 us
    pallas_call x8, Pallas kernels, plain(): pl.pallas_call(body, in_specs=[pl.BlockSpec(memory_space=pltpu.SMEM)] + [...  12.8 us
    ppermute x3, waiting for transfers between devices, on_device(): lax.ppermute(tile, AUX + ROW, [(a * 32 + k * 8 + spot(s), k * 32 + a * 8...  12.7 us
    ppermute x3, starting transfers between devices, on_device(): lax.ppermute(tile, AUX + ROW, [(a * 32 + k * 8 + spot(s), k * 32 + a * 8...  12.1 us
    ppermute x6, waiting for transfers between devices, flip(): return lax.ppermute(value, axis, [(k, k ^ mask) for k in range(size)])  10.4 us
    pallas_call x1, Pallas kernels, half_begin(): pl.pallas_call(begin_kernel, in_specs=[smem, smem, pl.BlockSpec(memory_sp...  8.69 us
    all_to_all x1, starting transfers between devices, on_device(): pieces = lax.all_to_all(pieces, ROW, 0, 0, tiled=True)  8.18 us
  transfers between devices with their start and end apart: 22, of which 6 were waited for; matrix products, arithmetic and copies ran while one was open for 0% of the time, Pallas kernels for 15%

profile of v3, /device:TPU:1, one launch (start us, length us, event | category | flops | bytes accessed | tf_op | source)
XLA Modules:
  0.0 147.6 jit_solution(5854128272223223836)
XLA Ops:
  0.8 0.8 constant_dynamic-slice_fusion
  1.8 25.1 %all_to_all.15.orbit_ref.mine_ref = bf16[32,128,128]{2,1,0:T(8,128)(2,1)S(1)} all-to-all(bf16[32,128,128]{2,1,0:T(8,128)(2,1)S(1)} %broadcast_in_dim.5), channel_id=1, replica_groups=mesh['xh'=2,'core'=2,'z'=4,'xl'=2,'y'=4] {'z','xl','y'}, dimensions={0} | all-to-all | bytes 2097152 | tf_op jit(solution)/shard_map/all_to_all | solution.py:313
  26.9 1.8 %collective-permute-start = (bf16[32,128,128]{2,1,0:T(8,128)(2,1)S(1)}, bf16[32,128,128]{2,1,0:T(8,128)(2,1)S(1)}, u32[]{:S(2)}, u32[]{:S(2)}) collective-permute-start(bf16[32,128,128]{2,1,0:T(8,128)(2,1)S(1)} %all_to_all.15.orbit_ref.mine_ref), channel_id=1, source_target_pairs={{0,32},{32,0},{1,33},{33,1},{2,34},{34,2},{3,35},{35,3},{4,36},{36... | collective-permute-start | bytes 3145736 | tf_op jit(solution)/shard_map/ppermute | solution.py:21
  28.7 8.7 %shard_map.59 = (bf16[5,256,8192]{2,1,0:T(8,128)(2,1)S(1)}, f32[2,640,128]{2,1,0:T(8,128)S(1)}) custom-call(s32[1]{0:T(128)} %bitcast.parity_ref, s32[2,64]{1,0:T(2,128)S(1)} %bitcast.6, bf16[5,256,8192]{2,1,0:T(8,128)(2,1)} %slab_ref.1, bf16[32,128,128]{2,1,0:T(8,128)(2,1)S(1)} %all_to_all.15.orbit_ref.mine_ref), custom_call_target="tpu_custom_call" | custom-call | flops 1342177280 | bytes 20971520 | tf_op jit(solution)/shard_map/pallas_call | solution.py:111
  37.4 3.5 %shard_map.60.flat_ref = bf16[256,640]{1,0:T(8,128)(2,1)S(1)} custom-call(s32[1]{0:T(128)S(6)} %sub.7.parity_ref, s32[2,64]{1,0:T(2,128)S(1)} %bitcast.7, bf16[5,256,8192]{2,1,0:T(8,128)(2,1)S(1)} %get-tuple-element.35.kept_ref, bf16[32,128,128]{2,1,0:T(8,128)(2,1)S(1)} %collective-permute-done.orbit_ref.other_ref, ...), custom_call_target="tpu_custom_call" | custom-call | flops 1342177280 | bytes 10485760 | tf_op jit(solution)/shard_map/pallas_call | solution.py:131
  40.9 2.1 %collective-permute-start.1 = (bf16[256,640]{1,0:T(8,128)(2,1)S(1)}, bf16[256,640]{1,0:T(8,128)(2,1)S(1)}, u32[]{:S(2)}, u32[]{:S(2)}) collective-permute-start(bf16[256,640]{1,0:T(8,128)(2,1)S(1)} %shard_map.60.flat_ref), channel_id=1, source_target_pairs={{0,0},{8,32},{16,64},{24,96},{32,8},{40,40},{48,72},{56,104},{64,1... | collective-permute-start | bytes 983048 | tf_op jit(solution)/shard_map/ppermute | solution.py:321
  43.1 2.3 %shard_map.61 = (f32[768,128]{1,0:T(8,128)}, f32[256,128]{1,0:T(8,128)S(1)}) custom-call(s32[2]{0:T(128)S(1)} %pad_add_fusion.where_ref, bf16[256,640]{1,0:T(8,128)(2,1)S(1)} %shard_map.60.flat_ref, bf16[256,128]{1,0:T(8,128)(2,1)S(1)} %copy-done, bf16[32,128,128]{2,1,0:T(8,128)(2,1)S(1)} %all_to_all.15.orbit_ref.mine_ref, ...), custom_call_target="tpu_custom_call" | custom-call | flops 10000000000 | bytes 4000000 | tf_op jit(solution)/shard_map/pallas_call | solution.py:145
  45.3 8.2 %all-to-all-start.1 = ((f32[32,24,128]{2,1,0:T(8,128)}), f32[32,24,128]{2,1,0:T(8,128)S(1)}, u32[]{:S(2)}, u32[]{:S(2)}) async-start(f32[32,24,128]{2,1,0:T(8,128)} %bitcast.3), calls=%async_computation.1 | async-start | bytes 786432 | tf_op jit(solution)/shard_map/all_to_all | solution.py:348
  53.5 3.4 %collective-permute-start.5 = (bf16[256,640]{1,0:T(8,128)(2,1)S(1)}, bf16[256,640]{1,0:T(8,128)(2,1)S(1)}, u32[]{:S(2)}, u32[]{:S(2)}) collective-permute-start(bf16[256,640]{1,0:T(8,128)(2,1)S(1)} %collective-permute-done.1.r0), channel_id=1, source_target_pairs={{4,0},{1,4},{5,1},{2,5},{6,2},{3,6},{7,3},{0,7},{12,8},{9,12},{13,... | collective-permute-start | bytes 983048 | tf_op jit(solution)/shard_map/ppermute | solution.py:341
  56.9 4.1 %collective-permute-start.2 = (bf16[256,640]{1,0:T(8,128)(2,1)S(1)}, bf16[256,640]{1,0:T(8,128)(2,1)S(1)}, u32[]{:S(2)}, u32[]{:S(2)}) collective-permute-start(bf16[256,640]{1,0:T(8,128)(2,1)S(1)} %collective-permute-done.1.r0), channel_id=1, source_target_pairs={{0,64},{64,0},{1,65},{65,1},{2,66},{66,2},{3,67},{67,3},{4,68},{68... | collective-permute-start | bytes 983048 | tf_op jit(solution)/shard_map/ppermute | solution.py:21
  61.0 1.3 collective-permute-start.8
  62.3 0.7 collective-permute-start.7
  63.0 1.5 %collective-permute-start.6 = (bf16[256,640]{1,0:T(8,128)(2,1)S(1)}, bf16[256,640]{1,0:T(8,128)(2,1)S(1)}, u32[]{:S(2)}, u32[]{:S(2)}) collective-permute-start(bf16[256,640]{1,0:T(8,128)(2,1)S(1)} %collective-permute-done.1.r0), channel_id=1, source_target_pairs={{1,0},{5,4},{2,1},{6,5},{3,2},{7,6},{0,3},{4,7},{9,8},{13,12},{10,... | collective-permute-start | bytes 983048 | tf_op jit(solution)/shard_map/ppermute | solution.py:341
  64.5 1.2 collective-permute-done.5.c1
  65.7 10.4 %collective-permute-done.2.r2 = bf16[256,640]{1,0:T(8,128)(2,1)S(1)} collective-permute-done((bf16[256,640]{1,0:T(8,128)(2,1)S(1)}, bf16[256,640]{1,0:T(8,128)(2,1)S(1)}, u32[]{:S(2)}, u32[]{:S(2)}) %collective-permute-start.2) | collective-permute-done | bytes 327712 | tf_op jit(solution)/shard_map/ppermute | solution.py:21
  76.1 2.2 %collective-permute-start.3 = (bf16[256,640]{1,0:T(8,128)(2,1)S(1)}, bf16[256,640]{1,0:T(8,128)(2,1)S(1)}, u32[]{:S(2)}, u32[]{:S(2)}) collective-permute-start(bf16[256,640]{1,0:T(8,128)(2,1)S(1)} %collective-permute-done.1.r0), channel_id=1, source_target_pairs={{0,32},{32,0},{1,33},{33,1},{2,34},{34,2},{3,35},{35,3},{4,36},{36... | collective-permute-start | bytes 983048 | tf_op jit(solution)/shard_map/ppermute | solution.py:21
  78.3 1.4 shard_map.66
  79.7 4.1 %all-to-all-start.2 = ((f32[32,24,128]{2,1,0:T(8,128)}), f32[32,24,128]{2,1,0:T(8,128)S(1)}, u32[]{:S(2)}, u32[]{:S(2)}) async-start(f32[32,24,128]{2,1,0:T(8,128)} %shard_map.66), calls=%async_computation.2 | async-start | bytes 786432 | tf_op jit(solution)/shard_map/all_to_all | solution.py:399
  83.8 0.7 copy-done.3
  84.5 0.7 copy-done.5
  85.2 1.0 copy-done.4
  86.2 1.0 copy-done.6
  87.2 3.5 %shard_map.62 = (bf16[256,640]{1,0:T(8,128)(2,1)}, bf16[256,640]{1,0:T(8,128)(2,1)}, f32[256,640]{1,0:T(8,128)S(1)}, bf16[256,640]{1,0:T(8,128)(2,1)S(1)}, bf16[...) custom-call(s32[4]{0:T(128)S(1)} %fusion.where_ref._, ...), custom_call_target="tpu_custom_call" | custom-call | flops 1000000000 | bytes 4000000 | tf_op jit(solution)/shard_map/pallas_call | solution.py:145
  90.7 0.8 copy-done.7
  91.5 0.8 copy-done.9
  92.3 0.9 copy-done.11
  93.2 0.8 copy-done.13
  94.0 1.0 collective-permute-start.9
  95.1 1.7 %collective-permute-start.10 = (bf16[256,640]{1,0:T(8,128)(2,1)}, bf16[256,640]{1,0:T(8,128)(2,1)S(1)}, u32[]{:S(2)}, u32[]{:S(2)}) collective-permute-start(bf16[256,640]{1,0:T(8,128)(2,1)} %get-tuple-element.46), channel_id=1, source_target_pairs={{0,24},{8,0},{16,8},{24,16},{1,25},{9,1},{17,9},{25,17},{2,26},{10... | collective-permute-start | bytes 983048 | tf_op jit(solution)/shard_map/ppermute | solution.py:25
  96.7 1.1 collective-permute-start.12
  97.8 0.4 collective-permute-start.13
  98.2 1.0 shard_map.67.left
  99.2 2.3 %collective-permute-start.18 = (f32[384,128]{1,0:T(8,128)S(1)}, f32[384,128]{1,0:T(8,128)S(1)}, u32[]{:S(2)}, u32[]{:S(2)}) collective-permute-start(f32[384,128]{1,0:T(8,128)S(1)} %shard_map.67.left), channel_id=1, source_target_pairs={{0,32},{32,0},{1,33},{33,1},{2,34},{34,2},{3,35},{35,3},{4,36},{36... | collective-permute-start | bytes 589832 | tf_op jit(solution)/shard_map/ppermute | solution.py:21
  101.5 2.0 %collective-permute-done.9.far_a = bf16[256,640]{1,0:T(8,128)(2,1)S(1)} collective-permute-done((bf16[256,640]{1,0:T(8,128)(2,1)}, bf16[256,640]{1,0:T(8,128)(2,1)S(1)}, u32[]{:S(2)}, u32[]{:S(2)}) %collective-permute-start.9) | collective-permute-done | bytes 327712 | tf_op jit(solution)/shard_map/ppermute | solution.py:25
  103.6 0.7 shard_map.63
  104.3 0.9 collective-permute-start.11
  105.1 1.9 %collective-permute-start.14 = (bf16[256,640]{1,0:T(8,128)(2,1)S(1)}, bf16[256,640]{1,0:T(8,128)(2,1)S(1)}, u32[]{:S(2)}, u32[]{:S(2)}) collective-permute-start(bf16[256,640]{1,0:T(8,128)(2,1)S(1)} %get-tuple-element.51), channel_id=1, source_target_pairs={{0,24},{8,0},{16,8},{24,16},{1,25},{9,1},{17,9},{25,17},{2,26},{10... | collective-permute-start | bytes 983048 | tf_op jit(solution)/shard_map/ppermute | solution.py:25
  107.0 0.6 shard_map.68.left
  107.6 4.7 %collective-permute-start.19 = (f32[384,128]{1,0:T(8,128)S(1)}, f32[384,128]{1,0:T(8,128)S(1)}, u32[]{:S(2)}, u32[]{:S(2)}) collective-permute-start(f32[384,128]{1,0:T(8,128)S(1)} %shard_map.68.left), channel_id=1, source_target_pairs={{0,64},{64,0},{1,65},{65,1},{2,66},{66,2},{3,67},{67,3},{4,68},{68... | collective-permute-start | bytes 589832 | tf_op jit(solution)/shard_map/ppermute | solution.py:21
  112.3 5.3 %collective-permute-done.11.up_a = bf16[256,640]{1,0:T(8,128)(2,1)S(1)} collective-permute-done((bf16[256,640]{1,0:T(8,128)(2,1)S(1)}, bf16[256,640]{1,0:T(8,128)(2,1)S(1)}, u32[]{:S(2)}, u32[]{:S(2)}) %collective-permute-start.11) | collective-permute-done | bytes 327712 | tf_op jit(solution)/shard_map/ppermute | solution.py:25
  117.6 2.1 %shard_map.64 = (f32[256,2048]{1,0:T(8,128)}, bf16[256,256]{1,0:T(8,128)(2,1)S(1)}, bf16[256,256]{1,0:T(8,128)(2,1)S(1)}, bf16[256,256]{1,0:T(8,128)(2,1)S(1)}) custom-call(s32[8]{0:T(128)S(1)} %fusion.2.place_ref, f32[256,640]{1,0:T(8,128)S(1)} %copy-done.8, bf16[256,640]{1,0:T(8,128)(2,1)S(1)} %collective-permute-done.11.up_a, ...), custom_call_target="tpu_custom_call" | custom-call | flops 1000000000 | bytes 4000000 | tf_op jit(solution)/shard_map/pallas_call | solution.py:145
  119.7 9.9 %collective-permute-start.15 = (bf16[256,256]{1,0:T(8,128)(2,1)S(1)}, bf16[256,256]{1,0:T(8,128)(2,1)S(1)}, u32[]{:S(2)}, u32[]{:S(2)}) collective-permute-start(bf16[256,256]{1,0:T(8,128)(2,1)S(1)} %get-tuple-element.52), channel_id=1, source_target_pairs={{0,4},{4,1},{1,5},{5,2},{2,6},{6,3},{3,7},{7,0},{8,36},{12,33},{9,... | collective-permute-start | bytes 393224 | tf_op jit(solution)/shard_map/ppermute | solution.py:385
  129.6 1.1 collective-permute-start.16
  130.7 1.1 collective-permute-start.17
  131.8 1.4 shard_map.69
  133.2 1.9 %collective-permute-done.15.t1 = bf16[256,256]{1,0:T(8,128)(2,1)S(1)} collective-permute-done((bf16[256,256]{1,0:T(8,128)(2,1)S(1)}, bf16[256,256]{1,0:T(8,128)(2,1)S(1)}, u32[]{:S(2)}, u32[]{:S(2)}) %collective-permute-start.15) | collective-permute-done | bytes 131104 | tf_op jit(solution)/shard_map/ppermute | solution.py:385
  135.1 10.8 %collective-permute-done.16.t2 = bf16[256,256]{1,0:T(8,128)(2,1)S(1)} collective-permute-done((bf16[256,256]{1,0:T(8,128)(2,1)S(1)}, bf16[256,256]{1,0:T(8,128)(2,1)S(1)}, u32[]{:S(2)}, u32[]{:S(2)}) %collective-permute-start.16) | collective-permute-done | bytes 131104 | tf_op jit(solution)/shard_map/ppermute | solution.py:385
  145.9 1.5 %shard_map.65 = f32[256,2048]{1,0:T(8,128)} custom-call(s32[8]{0:T(128)S(1)} %fusion.2.place_ref, bf16[256,256]{1,0:T(8,128)(2,1)S(1)} %collective-permute-done.15.t1, bf16[256,256]{1,0:T(8,128)(2,1)S(1)} %collective-permute-done.16.t2, bf16[256,256]{1,0:T(8,128)(2,1)S(1)} %collective-permute-done.17.t3, ...), custom_call_target="tpu_custom_call", output_to_operand_aliasing={{}: (4, {})} | custom-call | tf_op jit(solution)/shard_map/pallas_call | solution.py:285
  (43 shorter events, 0.4 us)
Async XLA Ops:
  0.6 28.1 %copy-start.1 = (s32[1,2,64]{2,1,0:T(2,128)S(1)}, s32[1,2,64]{2,1,0:T(2,128)}, u32[]{:S(2)}) copy-start(s32[1,2,64]{2,1,0:T(2,128)} %param.5) | copy-start | bytes 1540
  26.9 10.5 %collective-permute-start = (bf16[32,128,128]{2,1,0:T(8,128)(2,1)S(1)}, bf16[32,128,128]{2,1,0:T(8,128)(2,1)S(1)}, u32[]{:S(2)}, u32[]{:S(2)}) collective-permute-start(bf16[32,128,128]{2,1,0:T(8,128)(2,1)S(1)} %all_to_all.15.orbit_ref.mine_ref), channel_id=1, source_target_pairs={{0,32},{32,0},{1,33},{33,1},{2,34},{34,2},{3,35},{35,3},{4,36},{36... | collective-permute-start | bytes 3145736 | tf_op jit(solution)/shard_map/ppermute | solution.py:21
  37.4 5.6 %copy-start = (bf16[256,128]{1,0:T(8,128)(2,1)S(1)}, bf16[256,128]{1,0:T(8,128)(2,1)}, u32[]{:S(2)}) copy-start(bf16[256,128]{1,0:T(8,128)(2,1)} %orbit_ref.3) | copy-start | bytes 196612
  37.4 5.6 %copy-start.2 = (f32[256,2048]{1,0:T(8,128)S(1)}, f32[256,2048]{1,0:T(8,128)}, u32[]{:S(2)}) copy-start(f32[256,2048]{1,0:T(8,128)} %hcore_ref.1) | copy-start | bytes 6291460
  40.9 12.6 %collective-permute-start.1 = (bf16[256,640]{1,0:T(8,128)(2,1)S(1)}, bf16[256,640]{1,0:T(8,128)(2,1)S(1)}, u32[]{:S(2)}, u32[]{:S(2)}) collective-permute-start(bf16[256,640]{1,0:T(8,128)(2,1)S(1)} %shard_map.60.flat_ref), channel_id=1, source_target_pairs={{0,0},{8,32},{16,64},{24,96},{32,8},{40,40},{48,72},{56,104},{64,1... | collective-permute-start | bytes 983048 | tf_op jit(solution)/shard_map/ppermute | solution.py:321
  45.3 19.2 %all-to-all-start.1 = ((f32[32,24,128]{2,1,0:T(8,128)}), f32[32,24,128]{2,1,0:T(8,128)S(1)}, u32[]{:S(2)}, u32[]{:S(2)}) async-start(f32[32,24,128]{2,1,0:T(8,128)} %bitcast.3), calls=%async_computation.1 | async-start | bytes 786432 | tf_op jit(solution)/shard_map/all_to_all | solution.py:348
  53.5 12.2 %collective-permute-start.5 = (bf16[256,640]{1,0:T(8,128)(2,1)S(1)}, bf16[256,640]{1,0:T(8,128)(2,1)S(1)}, u32[]{:S(2)}, u32[]{:S(2)}) collective-permute-start(bf16[256,640]{1,0:T(8,128)(2,1)S(1)} %collective-permute-done.1.r0), channel_id=1, source_target_pairs={{4,0},{1,4},{5,1},{2,5},{6,2},{3,6},{7,3},{0,7},{12,8},{9,12},{13,... | collective-permute-start | bytes 983048 | tf_op jit(solution)/shard_map/ppermute | solution.py:341
  56.9 19.1 %collective-permute-start.2 = (bf16[256,640]{1,0:T(8,128)(2,1)S(1)}, bf16[256,640]{1,0:T(8,128)(2,1)S(1)}, u32[]{:S(2)}, u32[]{:S(2)}) collective-permute-start(bf16[256,640]{1,0:T(8,128)(2,1)S(1)} %collective-permute-done.1.r0), channel_id=1, source_target_pairs={{0,64},{64,0},{1,65},{65,1},{2,66},{66,2},{3,67},{67,3},{4,68},{68... | collective-permute-start | bytes 983048 | tf_op jit(solution)/shard_map/ppermute | solution.py:21
  61.0 22.7 %collective-permute-start.8 = (bf16[256,640]{1,0:T(8,128)(2,1)S(1)}, bf16[256,640]{1,0:T(8,128)(2,1)S(1)}, u32[]{:S(2)}, u32[]{:S(2)}) collective-permute-start(bf16[256,640]{1,0:T(8,128)(2,1)S(1)} %collective-permute-done.1.r0), channel_id=1, source_target_pairs={{2,0},{6,4},{3,1},{7,5},{0,2},{4,6},{1,3},{5,7},{10,8},{14,12},{11... | collective-permute-start | bytes 983048 | tf_op jit(solution)/shard_map/ppermute | solution.py:341
  62.3 21.4 %collective-permute-start.7 = (bf16[256,640]{1,0:T(8,128)(2,1)S(1)}, bf16[256,640]{1,0:T(8,128)(2,1)S(1)}, u32[]{:S(2)}, u32[]{:S(2)}) collective-permute-start(bf16[256,640]{1,0:T(8,128)(2,1)S(1)} %collective-permute-done.1.r0), channel_id=1, source_target_pairs={{5,0},{2,4},{6,1},{3,5},{7,2},{0,6},{4,3},{1,7},{13,8},{10,12},{14... | collective-permute-start | bytes 983048 | tf_op jit(solution)/shard_map/ppermute | solution.py:341
  63.0 20.7 %collective-permute-start.6 = (bf16[256,640]{1,0:T(8,128)(2,1)S(1)}, bf16[256,640]{1,0:T(8,128)(2,1)S(1)}, u32[]{:S(2)}, u32[]{:S(2)}) collective-permute-start(bf16[256,640]{1,0:T(8,128)(2,1)S(1)} %collective-permute-done.1.r0), channel_id=1, source_target_pairs={{1,0},{5,4},{2,1},{6,5},{3,2},{7,6},{0,3},{4,7},{9,8},{13,12},{10,... | collective-permute-start | bytes 983048 | tf_op jit(solution)/shard_map/ppermute | solution.py:341
  76.1 7.7 %collective-permute-start.3 = (bf16[256,640]{1,0:T(8,128)(2,1)S(1)}, bf16[256,640]{1,0:T(8,128)(2,1)S(1)}, u32[]{:S(2)}, u32[]{:S(2)}) collective-permute-start(bf16[256,640]{1,0:T(8,128)(2,1)S(1)} %collective-permute-done.1.r0), channel_id=1, source_target_pairs={{0,32},{32,0},{1,33},{33,1},{2,34},{34,2},{3,35},{35,3},{4,36},{36... | collective-permute-start | bytes 983048 | tf_op jit(solution)/shard_map/ppermute | solution.py:21
  78.3 6.2 %collective-permute-start.4 = (bf16[256,640]{1,0:T(8,128)(2,1)S(1)}, bf16[256,640]{1,0:T(8,128)(2,1)S(1)}, u32[]{:S(2)}, u32[]{:S(2)}) collective-permute-start(bf16[256,640]{1,0:T(8,128)(2,1)S(1)} %collective-permute-done.2.r2), channel_id=1, source_target_pairs={{0,32},{32,0},{1,33},{33,1},{2,34},{34,2},{3,35},{35,3},{4,36},{36... | collective-permute-start | bytes 983048 | tf_op jit(solution)/shard_map/ppermute | solution.py:21
  79.7 18.5 %all-to-all-start.2 = ((f32[32,24,128]{2,1,0:T(8,128)}), f32[32,24,128]{2,1,0:T(8,128)S(1)}, u32[]{:S(2)}, u32[]{:S(2)}) async-start(f32[32,24,128]{2,1,0:T(8,128)} %shard_map.66), calls=%async_computation.2 | async-start | bytes 786432 | tf_op jit(solution)/shard_map/all_to_all | solution.py:399
  83.8 0.7 copy-start.3
  84.5 0.7 copy-start.5
  85.2 1.0 copy-start.4
  86.2 1.0 copy-start.6
  90.7 0.8 copy-start.7
  91.5 0.8 copy-start.9
  92.3 0.9 copy-start.11
  93.2 0.8 copy-start.13
  94.0 9.5 %copy-start.12 = (f32[256,640]{1,0:T(8,128)S(1)}, f32[256,640]{1,0:T(8,128)}, u32[]{:S(2)}) copy-start(f32[256,640]{1,0:T(8,128)} %copy-done.11) | copy-start | bytes 1966084
  94.0 9.5 %collective-permute-start.9 = (bf16[256,640]{1,0:T(8,128)(2,1)}, bf16[256,640]{1,0:T(8,128)(2,1)S(1)}, u32[]{:S(2)}, u32[]{:S(2)}) collective-permute-start(bf16[256,640]{1,0:T(8,128)(2,1)} %get-tuple-element.44), channel_id=1, source_target_pairs={{0,8},{8,16},{16,24},{24,0},{1,9},{9,17},{17,25},{25,1},{2,10},{10... | collective-permute-start | bytes 983048 | tf_op jit(solution)/shard_map/ppermute | solution.py:25
  95.1 8.5 %collective-permute-start.10 = (bf16[256,640]{1,0:T(8,128)(2,1)}, bf16[256,640]{1,0:T(8,128)(2,1)S(1)}, u32[]{:S(2)}, u32[]{:S(2)}) collective-permute-start(bf16[256,640]{1,0:T(8,128)(2,1)} %get-tuple-element.46), channel_id=1, source_target_pairs={{0,24},{8,0},{16,8},{24,16},{1,25},{9,1},{17,9},{25,17},{2,26},{10... | collective-permute-start | bytes 983048 | tf_op jit(solution)/shard_map/ppermute | solution.py:25
  96.7 15.5 %collective-permute-start.12 = (bf16[256,640]{1,0:T(8,128)(2,1)S(1)}, bf16[256,640]{1,0:T(8,128)(2,1)S(1)}, u32[]{:S(2)}, u32[]{:S(2)}) collective-permute-start(bf16[256,640]{1,0:T(8,128)(2,1)S(1)} %get-tuple-element.48), channel_id=1, source_target_pairs={{0,24},{8,0},{16,8},{24,16},{1,25},{9,1},{17,9},{25,17},{2,26},{10... | collective-permute-start | bytes 983048 | tf_op jit(solution)/shard_map/ppermute | solution.py:25
  97.8 14.4 %collective-permute-start.13 = (bf16[256,640]{1,0:T(8,128)(2,1)S(1)}, bf16[256,640]{1,0:T(8,128)(2,1)S(1)}, u32[]{:S(2)}, u32[]{:S(2)}) collective-permute-start(bf16[256,640]{1,0:T(8,128)(2,1)S(1)} %get-tuple-element.50), channel_id=1, source_target_pairs={{0,8},{8,16},{16,24},{24,0},{1,9},{9,17},{17,25},{25,1},{2,10},{10... | collective-permute-start | bytes 983048 | tf_op jit(solution)/shard_map/ppermute | solution.py:25
  98.2 5.4 %copy-start.14 = (f32[256,640]{1,0:T(8,128)S(1)}, f32[256,640]{1,0:T(8,128)}, u32[]{:S(2)}) copy-start(f32[256,640]{1,0:T(8,128)} %copy-done.13) | copy-start | bytes 1966084
  99.2 7.8 %collective-permute-start.18 = (f32[384,128]{1,0:T(8,128)S(1)}, f32[384,128]{1,0:T(8,128)S(1)}, u32[]{:S(2)}, u32[]{:S(2)}) collective-permute-start(f32[384,128]{1,0:T(8,128)S(1)} %shard_map.67.left), channel_id=1, source_target_pairs={{0,32},{32,0},{1,33},{33,1},{2,34},{34,2},{3,35},{35,3},{4,36},{36... | collective-permute-start | bytes 589832 | tf_op jit(solution)/shard_map/ppermute | solution.py:21
  104.2 13.4 %copy-start.8 = (f32[256,640]{1,0:T(8,128)S(1)}, f32[256,640]{1,0:T(8,128)}, u32[]{:S(2)}) copy-start(f32[256,640]{1,0:T(8,128)} %copy-done.7) | copy-start | bytes 1966084
  104.2 13.4 %copy-start.10 = (f32[256,640]{1,0:T(8,128)S(1)}, f32[256,640]{1,0:T(8,128)}, u32[]{:S(2)}) copy-start(f32[256,640]{1,0:T(8,128)} %copy-done.9) | copy-start | bytes 1966084
  104.3 13.3 %collective-permute-start.11 = (bf16[256,640]{1,0:T(8,128)(2,1)S(1)}, bf16[256,640]{1,0:T(8,128)(2,1)S(1)}, u32[]{:S(2)}, u32[]{:S(2)}) collective-permute-start(bf16[256,640]{1,0:T(8,128)(2,1)S(1)} %get-tuple-element.47), channel_id=1, source_target_pairs={{0,8},{8,16},{16,24},{24,0},{1,9},{9,17},{17,25},{25,1},{2,10},{10... | collective-permute-start | bytes 983048 | tf_op jit(solution)/shard_map/ppermute | solution.py:25
  105.1 12.5 %collective-permute-start.14 = (bf16[256,640]{1,0:T(8,128)(2,1)S(1)}, bf16[256,640]{1,0:T(8,128)(2,1)S(1)}, u32[]{:S(2)}, u32[]{:S(2)}) collective-permute-start(bf16[256,640]{1,0:T(8,128)(2,1)S(1)} %get-tuple-element.51), channel_id=1, source_target_pairs={{0,24},{8,0},{16,8},{24,16},{1,25},{9,1},{17,9},{25,17},{2,26},{10... | collective-permute-start | bytes 983048 | tf_op jit(solution)/shard_map/ppermute | solution.py:25
  107.6 24.3 %collective-permute-start.19 = (f32[384,128]{1,0:T(8,128)S(1)}, f32[384,128]{1,0:T(8,128)S(1)}, u32[]{:S(2)}, u32[]{:S(2)}) collective-permute-start(f32[384,128]{1,0:T(8,128)S(1)} %shard_map.68.left), channel_id=1, source_target_pairs={{0,64},{64,0},{1,65},{65,1},{2,66},{66,2},{3,67},{67,3},{4,68},{68... | collective-permute-start | bytes 589832 | tf_op jit(solution)/shard_map/ppermute | solution.py:21
  119.7 15.4 %collective-permute-start.15 = (bf16[256,256]{1,0:T(8,128)(2,1)S(1)}, bf16[256,256]{1,0:T(8,128)(2,1)S(1)}, u32[]{:S(2)}, u32[]{:S(2)}) collective-permute-start(bf16[256,256]{1,0:T(8,128)(2,1)S(1)} %get-tuple-element.52), channel_id=1, source_target_pairs={{0,4},{4,1},{1,5},{5,2},{2,6},{6,3},{3,7},{7,0},{8,36},{12,33},{9,... | collective-permute-start | bytes 393224 | tf_op jit(solution)/shard_map/ppermute | solution.py:385
  129.6 16.3 %collective-permute-start.16 = (bf16[256,256]{1,0:T(8,128)(2,1)S(1)}, bf16[256,256]{1,0:T(8,128)(2,1)S(1)}, u32[]{:S(2)}, u32[]{:S(2)}) collective-permute-start(bf16[256,256]{1,0:T(8,128)(2,1)S(1)} %get-tuple-element.53), channel_id=1, source_target_pairs={{0,1},{4,5},{1,2},{5,6},{2,3},{6,7},{3,0},{7,4},{8,33},{12,37},{9,... | collective-permute-start | bytes 393224 | tf_op jit(solution)/shard_map/ppermute | solution.py:385
  130.7 15.2 %collective-permute-start.17 = (bf16[256,256]{1,0:T(8,128)(2,1)S(1)}, bf16[256,256]{1,0:T(8,128)(2,1)S(1)}, u32[]{:S(2)}, u32[]{:S(2)}) collective-permute-start(bf16[256,256]{1,0:T(8,128)(2,1)S(1)} %get-tuple-element.54), channel_id=1, source_target_pairs={{0,5},{4,2},{1,6},{5,3},{2,7},{6,0},{3,4},{7,1},{8,37},{12,34},{9,... | collective-permute-start | bytes 393224 | tf_op jit(solution)/shard_map/ppermute | solution.py:385

commit v4 on v3

--- a/solution.py
+++ b/solution.py
@@ -14,6 +14,7 @@
 BF = jnp.bfloat16
 F32 = jnp.float32
 SHARDS = 8
+OFFSETS = (1, 6, 3, 4)
 VMEM_LIMIT = 16 * 1024 * 1024
 
 
@@ -200,7 +201,7 @@
     t2[...] = a[:, n : 2 * n].astype(BF)
     t3[...] = b[:, :n].astype(BF)
     out_ref[:, at(1)] = a[:, :n]
-    out_ref[:, at(2)] = a[:, n : 2 * n]
+    out_ref[:, at(6)] = a[:, n : 2 * n]
     out_ref[:, at(3)] = b[:, :n]
     out_ref[:, at(4)] = b[:, n : 2 * n]
     out_ref[:, at(0)] = jnp.concatenate([a[:, 2 * n :], b[:, 2 * n :]], axis=1)
@@ -271,7 +272,7 @@
     copies = []
     for k, tile in enumerate((t1, t2, t3)):
         turned[k] = tile[...].astype(F32).T
-        at = pl.ds(pl.multiple_of(place_ref[7 - k] * n, 128), n)
+        at = pl.ds(pl.multiple_of(place_ref[8 - OFFSETS[k]] * n, 128), n)
         copies.append(pltpu.make_async_copy(turned.at[k], out_ref.at[:, at], sems.at[k]))
         copies[-1].start()
     for copy in copies:
@@ -318,9 +319,15 @@
     kept, begun = half_begin(here, screen[0], slab, mine)
     flat = half_end(there, screen[0], kept, other, begun)
 
-    swapped = lax.ppermute(
-        flat, ("xh", "core", "z"), [(a * 4 + k, k * 4 + a) for a in range(4) for k in range(4)]
-    )
+    swapped, far_rows = [
+        lax.ppermute(
+            flat,
+            ("xh", "core", "z"),
+            [(a * 4 + k, (k ^ m) * 4 + a) for a in range(4) for k in range(4)],
+        )
+        for m in (0, 2)
+    ]
+    swapped, far_rows = lax.optimization_barrier((swapped, far_rows))
     summed, core_part = plain(
         sums_kernel,
         [
@@ -336,12 +343,10 @@
         flops=10**10,
     )
 
-    far_rows = flip(swapped, "xh", 1, 2)
     columns = [
         lax.ppermute(swapped, PLANE, [(spot((s + m) % 8), spot(s)) for s in range(8)])
-        for m in (1, 2, 3, 4)
+        for m in OFFSETS
     ]
-    swapped, far_rows = lax.optimization_barrier((swapped, far_rows))
     factors = [swapped, flip(swapped, "core", 1, 2), far_rows, flip(far_rows, "core", 1, 2)]
     factors += columns
     pieces = summed.reshape(row_devices, -1, occupied)
@@ -392,7 +397,7 @@
                 for s in range(8)
             ],
         )
-        for m, tile in zip((1, 2, 3), tiles, strict=True)
+        for m, tile in zip(OFFSETS, tiles, strict=False)
     ]
     exchange = place(spots, turned, exchange)
 

time: 148 us -> 140 us (0.946); the launches traced: 148 us -> 138 us
  waiting for transfers between devices: 31.7 us -> 21.7 us
    ppermute x6 -> x5, waiting for transfers between devices: 10.4 us -> 0.01 us  [flip(): return lax.ppermute(value, axis, [(k, k ^ mask) for k in range(size)])]
    ppermute x3, starting transfers between devices: 12.1 us -> 6.88 us  [on_device(): lax.ppermute(tile, AUX + ROW, [(a * 32 + k * 8 + spot(s), k * 32 + a * 8...]
    ppermute x1 -> x2, starting transfers between devices: 2.09 us -> 5.88 us  [on_device(): lax.ppermute(flat, ('xh', 'core', 'z'), [(a * 4 + k, (k ^ m) * 4 + a) for...]
    all_to_all x1, starting transfers between devices: 4.06 us -> 7.55 us  [on_device(): summed = lax.all_to_all(pieces, ROW, 0, 0, tiled=True).reshape(summed.shape)]
    ppermute x4, waiting for transfers between devices: 1.19 us -> 4.15 us  [on_device(): lax.ppermute(swapped, PLANE, [(spot((s + m) % 8), spot(s)) for s in range...]
    all_to_all x1, starting transfers between devices: 8.18 us -> 5.6 us  [on_device(): pieces = lax.all_to_all(pieces, ROW, 0, 0, tiled=True)]
    ppermute x3, waiting for transfers between devices: 12.7 us -> 10.4 us  [on_device(): lax.ppermute(tile, AUX + ROW, [(a * 32 + k * 8 + spot(s), k * 32 + a * 8...]
    ppermute x6 -> x5, starting transfers between devices: 15.1 us -> 16.6 us  [flip(): return lax.ppermute(value, axis, [(k, k ^ mask) for k in range(size)])]
  transfers between devices with their start and end apart: 22 -> 22, of which waited for: 6 -> 4; matrix products, arithmetic and copies ran while one was open for 0% -> 0% of each run, Pallas kernels for 15% -> 16%
where the time goes in v4:
time: 140 us; the launch traced here: 138 us
  starting transfers between devices  55.3 us (40%)
  Pallas kernels  26.5 us (19%)
  blocking collectives  25.1 us (18%)
  waiting for transfers between devices  21.7 us (16%)
  local copies, waits for them, and re-layouts  7.8 us (6%)
    all_to_all x1, blocking collectives, on_device(): lax.all_to_all(jnp.broadcast_to(own[None], (row_devices,) + own.shape), R...  25.1 us
    ppermute x5, starting transfers between devices, flip(): return lax.ppermute(value, axis, [(k, k ^ mask) for k in range(size)])  16.6 us
    pallas_call x8, Pallas kernels, plain(): pl.pallas_call(body, in_specs=[pl.BlockSpec(memory_space=pltpu.SMEM)] + [...  12.8 us
    ppermute x3, waiting for transfers between devices, on_device(): lax.ppermute(tile, AUX + ROW, [(a * 32 + k * 8 + spot(s), k * 32 + a * 8...  10.4 us
    pallas_call x1, Pallas kernels, half_begin(): pl.pallas_call(begin_kernel, in_specs=[smem, smem, pl.BlockSpec(memory_sp...  8.69 us
    all_to_all x1, starting transfers between devices, on_device(): summed = lax.all_to_all(pieces, ROW, 0, 0, tiled=True).reshape(summed.shape)  7.55 us
    ppermute x6, waiting for transfers between devices, shift(): lax.ppermute(value, axis, [(k, (k + step) % size) for k in range(size)])  7.06 us
    ppermute x6, starting transfers between devices, shift(): lax.ppermute(value, axis, [(k, (k + step) % size) for k in range(size)])  6.89 us
  transfers between devices with their start and end apart: 22, of which 4 were waited for; matrix products, arithmetic and copies ran while one was open for 0% of the time, Pallas kernels for 16%

profile of v4, /device:TPU:1, one launch (start us, length us, event | category | flops | bytes accessed | tf_op | source)
XLA Modules:
  0.0 137.6 jit_solution(2709511260194481764)
XLA Ops:
  0.7 0.1 pad_add_fusion.where_ref
  0.8 0.8 constant_dynamic-slice_fusion
  1.5 0.2 broadcast_in_dim.5
  1.8 25.1 %all_to_all.15.orbit_ref.mine_ref = bf16[32,128,128]{2,1,0:T(8,128)(2,1)S(1)} all-to-all(bf16[32,128,128]{2,1,0:T(8,128)(2,1)S(1)} %broadcast_in_dim.5), channel_id=1, replica_groups=mesh['xh'=2,'core'=2,'z'=4,'xl'=2,'y'=4] {'z','xl','y'}, dimensions={0} | all-to-all | bytes 2097152 | tf_op jit(solution)/shard_map/all_to_all | solution.py:314
  26.9 1.8 %collective-permute-start = (bf16[32,128,128]{2,1,0:T(8,128)(2,1)S(1)}, bf16[32,128,128]{2,1,0:T(8,128)(2,1)S(1)}, u32[]{:S(2)}, u32[]{:S(2)}) collective-permute-start(bf16[32,128,128]{2,1,0:T(8,128)(2,1)S(1)} %all_to_all.15.orbit_ref.mine_ref), channel_id=1, source_target_pairs={{0,32},{32,0},{1,33},{33,1},{2,34},{34,2},{3,35},{35,3},{4,36},{36... | collective-permute-start | bytes 3145736 | tf_op jit(solution)/shard_map/ppermute | solution.py:22
  28.7 8.7 %shard_map.59 = (bf16[5,256,8192]{2,1,0:T(8,128)(2,1)S(1)}, f32[2,640,128]{2,1,0:T(8,128)S(1)}) custom-call(s32[1]{0:T(128)} %bitcast.parity_ref, s32[2,64]{1,0:T(2,128)S(1)} %bitcast.6, bf16[5,256,8192]{2,1,0:T(8,128)(2,1)} %slab_ref.1, bf16[32,128,128]{2,1,0:T(8,128)(2,1)S(1)} %all_to_all.15.orbit_ref.mine_ref), custom_call_target="tpu_custom_call" | custom-call | flops 1342177280 | bytes 20971520 | tf_op jit(solution)/shard_map/pallas_call | solution.py:112
  37.4 0.0 copy-start
  37.4 3.5 %shard_map.60.flat_ref = bf16[256,640]{1,0:T(8,128)(2,1)S(1)} custom-call(s32[1]{0:T(128)S(6)} %sub.7.parity_ref, s32[2,64]{1,0:T(2,128)S(1)} %bitcast.7, bf16[5,256,8192]{2,1,0:T(8,128)(2,1)S(1)} %get-tuple-element.35.kept_ref, bf16[32,128,128]{2,1,0:T(8,128)(2,1)S(1)} %collective-permute-done.orbit_ref.other_ref, ...), custom_call_target="tpu_custom_call" | custom-call | flops 1342177280 | bytes 10485760 | tf_op jit(solution)/shard_map/pallas_call | solution.py:132
  40.9 2.4 %collective-permute-start.2 = (bf16[256,640]{1,0:T(8,128)(2,1)S(1)}, bf16[256,640]{1,0:T(8,128)(2,1)S(1)}, u32[]{:S(2)}, u32[]{:S(2)}) collective-permute-start(bf16[256,640]{1,0:T(8,128)(2,1)S(1)} %shard_map.60.flat_ref), channel_id=1, source_target_pairs={{0,64},{8,96},{16,0},{24,32},{32,72},{40,104},{48,8},{56,40},{64,8... | collective-permute-start | bytes 983048 | tf_op jit(solution)/shard_map/ppermute | solution.py:323
  43.4 3.5 %collective-permute-start.1 = (bf16[256,640]{1,0:T(8,128)(2,1)S(1)}, bf16[256,640]{1,0:T(8,128)(2,1)S(1)}, u32[]{:S(2)}, u32[]{:S(2)}) collective-permute-start(bf16[256,640]{1,0:T(8,128)(2,1)S(1)} %shard_map.60.flat_ref), channel_id=1, source_target_pairs={{0,0},{8,32},{16,64},{24,96},{32,8},{40,40},{48,72},{56,104},{64,1... | collective-permute-start | bytes 983048 | tf_op jit(solution)/shard_map/ppermute | solution.py:323
  46.9 2.3 %shard_map.61 = (f32[768,128]{1,0:T(8,128)}, f32[256,128]{1,0:T(8,128)S(1)}) custom-call(s32[2]{0:T(128)S(1)} %pad_add_fusion.where_ref, bf16[256,640]{1,0:T(8,128)(2,1)S(1)} %shard_map.60.flat_ref, bf16[256,128]{1,0:T(8,128)(2,1)S(1)} %copy-done, bf16[32,128,128]{2,1,0:T(8,128)(2,1)S(1)} %all_to_all.15.orbit_ref.mine_ref, ...), custom_call_target="tpu_custom_call" | custom-call | flops 10000000000 | bytes 4000000 | tf_op jit(solution)/shard_map/pallas_call | solution.py:146
  49.1 5.6 %all-to-all-start.1 = ((f32[32,24,128]{2,1,0:T(8,128)}), f32[32,24,128]{2,1,0:T(8,128)S(1)}, u32[]{:S(2)}, u32[]{:S(2)}) async-start(f32[32,24,128]{2,1,0:T(8,128)} %bitcast.3), calls=%async_computation.1 | async-start | bytes 786432 | tf_op jit(solution)/shard_map/all_to_all | solution.py:353
  54.7 3.4 %collective-permute-start.5 = (bf16[256,640]{1,0:T(8,128)(2,1)S(1)}, bf16[256,640]{1,0:T(8,128)(2,1)S(1)}, u32[]{:S(2)}, u32[]{:S(2)}) collective-permute-start(bf16[256,640]{1,0:T(8,128)(2,1)S(1)} %collective-permute-done.1.r0), channel_id=1, source_target_pairs={{4,0},{1,4},{5,1},{2,5},{6,2},{3,6},{7,3},{0,7},{12,8},{9,12},{13,... | collective-permute-start | bytes 983048 | tf_op jit(solution)/shard_map/ppermute | solution.py:347
  58.1 0.6 collective-permute-start.8
  58.7 0.2 collective-permute-start.7
  59.0 1.6 %collective-permute-start.6 = (bf16[256,640]{1,0:T(8,128)(2,1)S(1)}, bf16[256,640]{1,0:T(8,128)(2,1)S(1)}, u32[]{:S(2)}, u32[]{:S(2)}) collective-permute-start(bf16[256,640]{1,0:T(8,128)(2,1)S(1)} %collective-permute-done.1.r0), channel_id=1, source_target_pairs={{3,0},{7,4},{0,1},{4,5},{1,2},{5,6},{2,3},{6,7},{11,8},{15,12},{8,... | collective-permute-start | bytes 983048 | tf_op jit(solution)/shard_map/ppermute | solution.py:347
  60.6 2.1 %collective-permute-start.3 = (bf16[256,640]{1,0:T(8,128)(2,1)S(1)}, bf16[256,640]{1,0:T(8,128)(2,1)S(1)}, u32[]{:S(2)}, u32[]{:S(2)}) collective-permute-start(bf16[256,640]{1,0:T(8,128)(2,1)S(1)} %collective-permute-done.1.r0), channel_id=1, source_target_pairs={{0,32},{32,0},{1,33},{33,1},{2,34},{34,2},{3,35},{35,3},{4,36},{36... | collective-permute-start | bytes 983048 | tf_op jit(solution)/shard_map/ppermute | solution.py:22
  62.7 4.1 %collective-permute-done.5.c1 = bf16[256,640]{1,0:T(8,128)(2,1)S(1)} collective-permute-done((bf16[256,640]{1,0:T(8,128)(2,1)S(1)}, bf16[256,640]{1,0:T(8,128)(2,1)S(1)}, u32[]{:S(2)}, u32[]{:S(2)}) %collective-permute-start.5) | collective-permute-done | bytes 327712 | tf_op jit(solution)/shard_map/ppermute | solution.py:347
  66.9 3.7 %collective-permute-start.4 = (bf16[256,640]{1,0:T(8,128)(2,1)S(1)}, bf16[256,640]{1,0:T(8,128)(2,1)S(1)}, u32[]{:S(2)}, u32[]{:S(2)}) collective-permute-start(bf16[256,640]{1,0:T(8,128)(2,1)S(1)} %collective-permute-done.2.r2), channel_id=1, source_target_pairs={{0,32},{32,0},{1,33},{33,1},{2,34},{34,2},{3,35},{35,3},{4,36},{36... | collective-permute-start | bytes 983048 | tf_op jit(solution)/shard_map/ppermute | solution.py:22
  70.6 1.4 shard_map.66
  71.9 7.6 %all-to-all-start.2 = ((f32[32,24,128]{2,1,0:T(8,128)}), f32[32,24,128]{2,1,0:T(8,128)S(1)}, u32[]{:S(2)}, u32[]{:S(2)}) async-start(f32[32,24,128]{2,1,0:T(8,128)} %shard_map.66), calls=%async_computation.2 | async-start | bytes 786432 | tf_op jit(solution)/shard_map/all_to_all | solution.py:404
  79.5 0.7 copy-done.5
  80.3 0.7 copy-done.3
  81.0 1.0 copy-done.4
  82.0 1.0 copy-done.6
  82.9 3.5 %shard_map.62 = (bf16[256,640]{1,0:T(8,128)(2,1)}, bf16[256,640]{1,0:T(8,128)(2,1)}, f32[256,640]{1,0:T(8,128)S(1)}, bf16[256,640]{1,0:T(8,128)(2,1)S(1)}, bf16[...) custom-call(s32[4]{0:T(128)S(1)} %fusion.where_ref._, ...), custom_call_target="tpu_custom_call" | custom-call | flops 1000000000 | bytes 4000000 | tf_op jit(solution)/shard_map/pallas_call | solution.py:146
  86.4 0.8 copy-done.7
  87.3 0.8 copy-done.9
  88.1 0.9 copy-done.11
  89.0 0.8 copy-done.13
  89.8 1.1 collective-permute-start.9
  90.9 1.6 %collective-permute-start.10 = (bf16[256,640]{1,0:T(8,128)(2,1)}, bf16[256,640]{1,0:T(8,128)(2,1)S(1)}, u32[]{:S(2)}, u32[]{:S(2)}) collective-permute-start(bf16[256,640]{1,0:T(8,128)(2,1)} %get-tuple-element.46), channel_id=1, source_target_pairs={{0,24},{8,0},{16,8},{24,16},{1,25},{9,1},{17,9},{25,17},{2,26},{10... | collective-permute-start | bytes 983048 | tf_op jit(solution)/shard_map/ppermute | solution.py:26
  92.5 1.1 collective-permute-start.12
  93.6 0.4 collective-permute-start.13
  94.0 1.0 shard_map.67.left
  95.0 8.3 %collective-permute-start.18 = (f32[384,128]{1,0:T(8,128)S(1)}, f32[384,128]{1,0:T(8,128)S(1)}, u32[]{:S(2)}, u32[]{:S(2)}) collective-permute-start(f32[384,128]{1,0:T(8,128)S(1)} %shard_map.67.left), channel_id=1, source_target_pairs={{0,32},{32,0},{1,33},{33,1},{2,34},{34,2},{3,35},{35,3},{4,36},{36... | collective-permute-start | bytes 589832 | tf_op jit(solution)/shard_map/ppermute | solution.py:22
  103.2 0.7 shard_map.63
  103.9 0.2 collective-permute-start.11
  104.1 2.5 %collective-permute-start.14 = (bf16[256,640]{1,0:T(8,128)(2,1)S(1)}, bf16[256,640]{1,0:T(8,128)(2,1)S(1)}, u32[]{:S(2)}, u32[]{:S(2)}) collective-permute-start(bf16[256,640]{1,0:T(8,128)(2,1)S(1)} %get-tuple-element.51), channel_id=1, source_target_pairs={{0,24},{8,0},{16,8},{24,16},{1,25},{9,1},{17,9},{25,17},{2,26},{10... | collective-permute-start | bytes 983048 | tf_op jit(solution)/shard_map/ppermute | solution.py:26
  106.7 0.6 shard_map.68.left
  107.2 0.7 collective-permute-start.19
  108.0 7.1 %collective-permute-done.11.up_a = bf16[256,640]{1,0:T(8,128)(2,1)S(1)} collective-permute-done((bf16[256,640]{1,0:T(8,128)(2,1)S(1)}, bf16[256,640]{1,0:T(8,128)(2,1)S(1)}, u32[]{:S(2)}, u32[]{:S(2)}) %collective-permute-start.11) | collective-permute-done | bytes 327712 | tf_op jit(solution)/shard_map/ppermute | solution.py:26
  115.0 2.1 %shard_map.64 = (f32[256,2048]{1,0:T(8,128)}, bf16[256,256]{1,0:T(8,128)(2,1)S(1)}, bf16[256,256]{1,0:T(8,128)(2,1)S(1)}, bf16[256,256]{1,0:T(8,128)(2,1)S(1)}) custom-call(s32[8]{0:T(128)S(1)} %fusion.2.place_ref, f32[256,640]{1,0:T(8,128)S(1)} %copy-done.8, bf16[256,640]{1,0:T(8,128)(2,1)S(1)} %collective-permute-done.11.up_a, ...), custom_call_target="tpu_custom_call" | custom-call | flops 1000000000 | bytes 4000000 | tf_op jit(solution)/shard_map/pallas_call | solution.py:146
  117.1 6.9 %collective-permute-start.15 = (bf16[256,256]{1,0:T(8,128)(2,1)S(1)}, bf16[256,256]{1,0:T(8,128)(2,1)S(1)}, u32[]{:S(2)}, u32[]{:S(2)}) collective-permute-start(bf16[256,256]{1,0:T(8,128)(2,1)S(1)} %get-tuple-element.52), channel_id=1, source_target_pairs={{0,4},{4,1},{1,5},{5,2},{2,6},{6,3},{3,7},{7,0},{8,36},{12,33},{9,... | collective-permute-start | bytes 393224 | tf_op jit(solution)/shard_map/ppermute | solution.py:390
  124.0 1.4 %shard_map.69 = f32[256,128]{1,0:T(8,128)} custom-call(s32[4]{0:T(128)S(1)} %fusion.where_ref._, bf16[256,128]{1,0:T(8,128)(2,1)S(1)} %copy-done, f32[384,128]{1,0:T(8,128)S(1)} %shard_map.68.left, f32[384,128]{1,0:T(8,128)S(1)} %collective-permute-done.19.right), custom_call_target="tpu_custom_call" | custom-call | flops 1000000000 | bytes 4000000 | tf_op jit(solution)/shard_map/pallas_call | solution.py:146
  125.4 1.9 %collective-permute-done.15.t1 = bf16[256,256]{1,0:T(8,128)(2,1)S(1)} collective-permute-done((bf16[256,256]{1,0:T(8,128)(2,1)S(1)}, bf16[256,256]{1,0:T(8,128)(2,1)S(1)}, u32[]{:S(2)}, u32[]{:S(2)}) %collective-permute-start.15) | collective-permute-done | bytes 131104 | tf_op jit(solution)/shard_map/ppermute | solution.py:390
  127.3 8.5 %collective-permute-done.16.t2 = bf16[256,256]{1,0:T(8,128)(2,1)S(1)} collective-permute-done((bf16[256,256]{1,0:T(8,128)(2,1)S(1)}, bf16[256,256]{1,0:T(8,128)(2,1)S(1)}, u32[]{:S(2)}, u32[]{:S(2)}) %collective-permute-start.16) | collective-permute-done | bytes 131104 | tf_op jit(solution)/shard_map/ppermute | solution.py:390
  135.8 1.5 %shard_map.65 = f32[256,2048]{1,0:T(8,128)} custom-call(s32[8]{0:T(128)S(1)} %fusion.2.place_ref, bf16[256,256]{1,0:T(8,128)(2,1)S(1)} %collective-permute-done.15.t1, bf16[256,256]{1,0:T(8,128)(2,1)S(1)} %collective-permute-done.16.t2, bf16[256,256]{1,0:T(8,128)(2,1)S(1)} %collective-permute-done.17.t3, ...), custom_call_target="tpu_custom_call", output_to_operand_aliasing={{}: (4, {})} | custom-call | tf_op jit(solution)/shard_map/pallas_call | solution.py:286
  (43 shorter events, 0.1 us)
Async XLA Ops:
  0.6 28.1 %copy-start.1 = (s32[1,2,64]{2,1,0:T(2,128)S(1)}, s32[1,2,64]{2,1,0:T(2,128)}, u32[]{:S(2)}) copy-start(s32[1,2,64]{2,1,0:T(2,128)} %param.5) | copy-start | bytes 1540
  26.9 10.5 %collective-permute-start = (bf16[32,128,128]{2,1,0:T(8,128)(2,1)S(1)}, bf16[32,128,128]{2,1,0:T(8,128)(2,1)S(1)}, u32[]{:S(2)}, u32[]{:S(2)}) collective-permute-start(bf16[32,128,128]{2,1,0:T(8,128)(2,1)S(1)} %all_to_all.15.orbit_ref.mine_ref), channel_id=1, source_target_pairs={{0,32},{32,0},{1,33},{33,1},{2,34},{34,2},{3,35},{35,3},{4,36},{36... | collective-permute-start | bytes 3145736 | tf_op jit(solution)/shard_map/ppermute | solution.py:22
  37.4 9.4 %copy-start = (bf16[256,128]{1,0:T(8,128)(2,1)S(1)}, bf16[256,128]{1,0:T(8,128)(2,1)}, u32[]{:S(2)}) copy-start(bf16[256,128]{1,0:T(8,128)(2,1)} %orbit_ref.3) | copy-start | bytes 196612
  37.4 9.4 %copy-start.2 = (f32[256,2048]{1,0:T(8,128)S(1)}, f32[256,2048]{1,0:T(8,128)}, u32[]{:S(2)}) copy-start(f32[256,2048]{1,0:T(8,128)} %hcore_ref.1) | copy-start | bytes 6291460
  40.9 13.8 %collective-permute-start.2 = (bf16[256,640]{1,0:T(8,128)(2,1)S(1)}, bf16[256,640]{1,0:T(8,128)(2,1)S(1)}, u32[]{:S(2)}, u32[]{:S(2)}) collective-permute-start(bf16[256,640]{1,0:T(8,128)(2,1)S(1)} %shard_map.60.flat_ref), channel_id=1, source_target_pairs={{0,64},{8,96},{16,0},{24,32},{32,72},{40,104},{48,8},{56,40},{64,8... | collective-permute-start | bytes 983048 | tf_op jit(solution)/shard_map/ppermute | solution.py:323
  43.4 11.4 %collective-permute-start.1 = (bf16[256,640]{1,0:T(8,128)(2,1)S(1)}, bf16[256,640]{1,0:T(8,128)(2,1)S(1)}, u32[]{:S(2)}, u32[]{:S(2)}) collective-permute-start(bf16[256,640]{1,0:T(8,128)(2,1)S(1)} %shard_map.60.flat_ref), channel_id=1, source_target_pairs={{0,0},{8,32},{16,64},{24,96},{32,8},{40,40},{48,72},{56,104},{64,1... | collective-permute-start | bytes 983048 | tf_op jit(solution)/shard_map/ppermute | solution.py:323
  49.1 21.5 %all-to-all-start.1 = ((f32[32,24,128]{2,1,0:T(8,128)}), f32[32,24,128]{2,1,0:T(8,128)S(1)}, u32[]{:S(2)}, u32[]{:S(2)}) async-start(f32[32,24,128]{2,1,0:T(8,128)} %bitcast.3), calls=%async_computation.1 | async-start | bytes 786432 | tf_op jit(solution)/shard_map/all_to_all | solution.py:353
  54.7 12.1 %collective-permute-start.5 = (bf16[256,640]{1,0:T(8,128)(2,1)S(1)}, bf16[256,640]{1,0:T(8,128)(2,1)S(1)}, u32[]{:S(2)}, u32[]{:S(2)}) collective-permute-start(bf16[256,640]{1,0:T(8,128)(2,1)S(1)} %collective-permute-done.1.r0), channel_id=1, source_target_pairs={{4,0},{1,4},{5,1},{2,5},{6,2},{3,6},{7,3},{0,7},{12,8},{9,12},{13,... | collective-permute-start | bytes 983048 | tf_op jit(solution)/shard_map/ppermute | solution.py:347
  58.1 22.1 %collective-permute-start.8 = (bf16[256,640]{1,0:T(8,128)(2,1)S(1)}, bf16[256,640]{1,0:T(8,128)(2,1)S(1)}, u32[]{:S(2)}, u32[]{:S(2)}) collective-permute-start(bf16[256,640]{1,0:T(8,128)(2,1)S(1)} %collective-permute-done.1.r0), channel_id=1, source_target_pairs={{2,0},{6,4},{3,1},{7,5},{0,2},{4,6},{1,3},{5,7},{10,8},{14,12},{11... | collective-permute-start | bytes 983048 | tf_op jit(solution)/shard_map/ppermute | solution.py:347
  58.7 21.5 %collective-permute-start.7 = (bf16[256,640]{1,0:T(8,128)(2,1)S(1)}, bf16[256,640]{1,0:T(8,128)(2,1)S(1)}, u32[]{:S(2)}, u32[]{:S(2)}) collective-permute-start(bf16[256,640]{1,0:T(8,128)(2,1)S(1)} %collective-permute-done.1.r0), channel_id=1, source_target_pairs={{5,0},{2,4},{6,1},{3,5},{7,2},{0,6},{4,3},{1,7},{13,8},{10,12},{14... | collective-permute-start | bytes 983048 | tf_op jit(solution)/shard_map/ppermute | solution.py:347
  59.0 21.3 %collective-permute-start.6 = (bf16[256,640]{1,0:T(8,128)(2,1)S(1)}, bf16[256,640]{1,0:T(8,128)(2,1)S(1)}, u32[]{:S(2)}, u32[]{:S(2)}) collective-permute-start(bf16[256,640]{1,0:T(8,128)(2,1)S(1)} %collective-permute-done.1.r0), channel_id=1, source_target_pairs={{3,0},{7,4},{0,1},{4,5},{1,2},{5,6},{2,3},{6,7},{11,8},{15,12},{8,... | collective-permute-start | bytes 983048 | tf_op jit(solution)/shard_map/ppermute | solution.py:347
  60.6 19.6 %collective-permute-start.3 = (bf16[256,640]{1,0:T(8,128)(2,1)S(1)}, bf16[256,640]{1,0:T(8,128)(2,1)S(1)}, u32[]{:S(2)}, u32[]{:S(2)}) collective-permute-start(bf16[256,640]{1,0:T(8,128)(2,1)S(1)} %collective-permute-done.1.r0), channel_id=1, source_target_pairs={{0,32},{32,0},{1,33},{33,1},{2,34},{34,2},{3,35},{35,3},{4,36},{36... | collective-permute-start | bytes 983048 | tf_op jit(solution)/shard_map/ppermute | solution.py:22
  66.9 12.6 %collective-permute-start.4 = (bf16[256,640]{1,0:T(8,128)(2,1)S(1)}, bf16[256,640]{1,0:T(8,128)(2,1)S(1)}, u32[]{:S(2)}, u32[]{:S(2)}) collective-permute-start(bf16[256,640]{1,0:T(8,128)(2,1)S(1)} %collective-permute-done.2.r2), channel_id=1, source_target_pairs={{0,32},{32,0},{1,33},{33,1},{2,34},{34,2},{3,35},{35,3},{4,36},{36... | collective-permute-start | bytes 983048 | tf_op jit(solution)/shard_map/ppermute | solution.py:22
  71.9 22.0 %all-to-all-start.2 = ((f32[32,24,128]{2,1,0:T(8,128)}), f32[32,24,128]{2,1,0:T(8,128)S(1)}, u32[]{:S(2)}, u32[]{:S(2)}) async-start(f32[32,24,128]{2,1,0:T(8,128)} %shard_map.66), calls=%async_computation.2 | async-start | bytes 786432 | tf_op jit(solution)/shard_map/all_to_all | solution.py:404
  79.5 0.7 copy-start.5
  80.3 0.7 copy-start.3
  81.0 1.0 copy-start.4
  82.0 1.0 copy-start.6
  86.4 0.8 copy-start.7
  87.3 0.8 copy-start.9
  88.1 0.9 copy-start.11
  89.0 0.8 copy-start.13
  89.8 13.4 %copy-start.12 = (f32[256,640]{1,0:T(8,128)S(1)}, f32[256,640]{1,0:T(8,128)}, u32[]{:S(2)}) copy-start(f32[256,640]{1,0:T(8,128)} %copy-done.11) | copy-start | bytes 1966084
  89.8 13.4 %collective-permute-start.9 = (bf16[256,640]{1,0:T(8,128)(2,1)}, bf16[256,640]{1,0:T(8,128)(2,1)S(1)}, u32[]{:S(2)}, u32[]{:S(2)}) collective-permute-start(bf16[256,640]{1,0:T(8,128)(2,1)} %get-tuple-element.44), channel_id=1, source_target_pairs={{0,8},{8,16},{16,24},{24,0},{1,9},{9,17},{17,25},{25,1},{2,10},{10... | collective-permute-start | bytes 983048 | tf_op jit(solution)/shard_map/ppermute | solution.py:26
  90.9 12.4 %collective-permute-start.10 = (bf16[256,640]{1,0:T(8,128)(2,1)}, bf16[256,640]{1,0:T(8,128)(2,1)S(1)}, u32[]{:S(2)}, u32[]{:S(2)}) collective-permute-start(bf16[256,640]{1,0:T(8,128)(2,1)} %get-tuple-element.46), channel_id=1, source_target_pairs={{0,24},{8,0},{16,8},{24,16},{1,25},{9,1},{17,9},{25,17},{2,26},{10... | collective-permute-start | bytes 983048 | tf_op jit(solution)/shard_map/ppermute | solution.py:26
  92.5 15.5 %collective-permute-start.12 = (bf16[256,640]{1,0:T(8,128)(2,1)S(1)}, bf16[256,640]{1,0:T(8,128)(2,1)S(1)}, u32[]{:S(2)}, u32[]{:S(2)}) collective-permute-start(bf16[256,640]{1,0:T(8,128)(2,1)S(1)} %get-tuple-element.48), channel_id=1, source_target_pairs={{0,24},{8,0},{16,8},{24,16},{1,25},{9,1},{17,9},{25,17},{2,26},{10... | collective-permute-start | bytes 983048 | tf_op jit(solution)/shard_map/ppermute | solution.py:26
  93.6 14.4 %collective-permute-start.13 = (bf16[256,640]{1,0:T(8,128)(2,1)S(1)}, bf16[256,640]{1,0:T(8,128)(2,1)S(1)}, u32[]{:S(2)}, u32[]{:S(2)}) collective-permute-start(bf16[256,640]{1,0:T(8,128)(2,1)S(1)} %get-tuple-element.50), channel_id=1, source_target_pairs={{0,8},{8,16},{16,24},{24,0},{1,9},{9,17},{17,25},{25,1},{2,10},{10... | collective-permute-start | bytes 983048 | tf_op jit(solution)/shard_map/ppermute | solution.py:26
  94.0 9.3 %copy-start.14 = (f32[256,640]{1,0:T(8,128)S(1)}, f32[256,640]{1,0:T(8,128)}, u32[]{:S(2)}) copy-start(f32[256,640]{1,0:T(8,128)} %copy-done.13) | copy-start | bytes 1966084
  95.0 11.7 %collective-permute-start.18 = (f32[384,128]{1,0:T(8,128)S(1)}, f32[384,128]{1,0:T(8,128)S(1)}, u32[]{:S(2)}, u32[]{:S(2)}) collective-permute-start(f32[384,128]{1,0:T(8,128)S(1)} %shard_map.67.left), channel_id=1, source_target_pairs={{0,32},{32,0},{1,33},{33,1},{2,34},{34,2},{3,35},{35,3},{4,36},{36... | collective-permute-start | bytes 589832 | tf_op jit(solution)/shard_map/ppermute | solution.py:22
  103.9 11.1 %copy-start.8 = (f32[256,640]{1,0:T(8,128)S(1)}, f32[256,640]{1,0:T(8,128)}, u32[]{:S(2)}) copy-start(f32[256,640]{1,0:T(8,128)} %copy-done.7) | copy-start | bytes 1966084
  103.9 11.1 %copy-start.10 = (f32[256,640]{1,0:T(8,128)S(1)}, f32[256,640]{1,0:T(8,128)}, u32[]{:S(2)}) copy-start(f32[256,640]{1,0:T(8,128)} %copy-done.9) | copy-start | bytes 1966084
  103.9 11.1 %collective-permute-start.11 = (bf16[256,640]{1,0:T(8,128)(2,1)S(1)}, bf16[256,640]{1,0:T(8,128)(2,1)S(1)}, u32[]{:S(2)}, u32[]{:S(2)}) collective-permute-start(bf16[256,640]{1,0:T(8,128)(2,1)S(1)} %get-tuple-element.47), channel_id=1, source_target_pairs={{0,8},{8,16},{16,24},{24,0},{1,9},{9,17},{17,25},{25,1},{2,10},{10... | collective-permute-start | bytes 983048 | tf_op jit(solution)/shard_map/ppermute | solution.py:26
  104.1 10.9 %collective-permute-start.14 = (bf16[256,640]{1,0:T(8,128)(2,1)S(1)}, bf16[256,640]{1,0:T(8,128)(2,1)S(1)}, u32[]{:S(2)}, u32[]{:S(2)}) collective-permute-start(bf16[256,640]{1,0:T(8,128)(2,1)S(1)} %get-tuple-element.51), channel_id=1, source_target_pairs={{0,24},{8,0},{16,8},{24,16},{1,25},{9,1},{17,9},{25,17},{2,26},{10... | collective-permute-start | bytes 983048 | tf_op jit(solution)/shard_map/ppermute | solution.py:26
  107.2 16.8 %collective-permute-start.19 = (f32[384,128]{1,0:T(8,128)S(1)}, f32[384,128]{1,0:T(8,128)S(1)}, u32[]{:S(2)}, u32[]{:S(2)}) collective-permute-start(f32[384,128]{1,0:T(8,128)S(1)} %shard_map.68.left), channel_id=1, source_target_pairs={{0,64},{64,0},{1,65},{65,1},{2,66},{66,2},{3,67},{67,3},{4,68},{68... | collective-permute-start | bytes 589832 | tf_op jit(solution)/shard_map/ppermute | solution.py:22
  117.1 10.2 %collective-permute-start.15 = (bf16[256,256]{1,0:T(8,128)(2,1)S(1)}, bf16[256,256]{1,0:T(8,128)(2,1)S(1)}, u32[]{:S(2)}, u32[]{:S(2)}) collective-permute-start(bf16[256,256]{1,0:T(8,128)(2,1)S(1)} %get-tuple-element.52), channel_id=1, source_target_pairs={{0,4},{4,1},{1,5},{5,2},{2,6},{6,3},{3,7},{7,0},{8,36},{12,33},{9,... | collective-permute-start | bytes 393224 | tf_op jit(solution)/shard_map/ppermute | solution.py:390
  124.0 11.8 %collective-permute-start.16 = (bf16[256,256]{1,0:T(8,128)(2,1)S(1)}, bf16[256,256]{1,0:T(8,128)(2,1)S(1)}, u32[]{:S(2)}, u32[]{:S(2)}) collective-permute-start(bf16[256,256]{1,0:T(8,128)(2,1)S(1)} %get-tuple-element.53), channel_id=1, source_target_pairs={{0,3},{4,7},{1,0},{5,4},{2,1},{6,5},{3,2},{7,6},{8,35},{12,39},{9,... | collective-permute-start | bytes 393224 | tf_op jit(solution)/shard_map/ppermute | solution.py:390
  124.0 11.8 %collective-permute-start.17 = (bf16[256,256]{1,0:T(8,128)(2,1)S(1)}, bf16[256,256]{1,0:T(8,128)(2,1)S(1)}, u32[]{:S(2)}, u32[]{:S(2)}) collective-permute-start(bf16[256,256]{1,0:T(8,128)(2,1)S(1)} %get-tuple-element.54), channel_id=1, source_target_pairs={{0,5},{4,2},{1,6},{5,3},{2,7},{6,0},{3,4},{7,1},{8,37},{12,34},{9,... | collective-permute-start | bytes 393224 | tf_op jit(solution)/shard_map/ppermute | solution.py:390

commit v5 on v4

--- a/solution.py
+++ b/solution.py
@@ -347,7 +347,8 @@
         lax.ppermute(swapped, PLANE, [(spot((s + m) % 8), spot(s)) for s in range(8)])
         for m in OFFSETS
     ]
-    factors = [swapped, flip(swapped, "core", 1, 2), far_rows, flip(far_rows, "core", 1, 2)]
+    near, far = flip(jnp.stack([swapped, far_rows]), "core", 1, 2)
+    factors = [swapped, near, far_rows, far]
     factors += columns
     pieces = summed.reshape(row_devices, -1, occupied)
     pieces = lax.all_to_all(pieces, ROW, 0, 0, tiled=True)

time: 140 us -> 138 us (0.986)
  local copies, waits for them, and re-layouts: 7.8 us -> 4.48 us
    unnamed x30 -> x22, local copies, waits for them, and re-layouts: 6.81 us -> 3.43 us
    ppermute x5 -> x4, starting transfers between devices: 16.6 us -> 15.4 us  [flip(): return lax.ppermute(value, axis, [(k, k ^ mask) for k in range(size)])]
  transfers between devices with their start and end apart: 22 -> 21, of which waited for: 4 -> 5; matrix products, arithmetic and copies ran while one was open for 0% -> 1% of each run, Pallas kernels for 16% -> 16%
where the time goes in v5:
time: 138 us; the launch traced here: 136 us
  starting transfers between devices  55.1 us (40%)
  Pallas kernels  26.5 us (19%)
  blocking collectives  25.1 us (18%)
  waiting for transfers between devices  22.2 us (16%)
  local copies, waits for them, and re-layouts  4.48 us (3%)
    all_to_all x1, blocking collectives, on_device(): lax.all_to_all(jnp.broadcast_to(own[None], (row_devices,) + own.shape), R...  25.1 us
    ppermute x4, starting transfers between devices, flip(): return lax.ppermute(value, axis, [(k, k ^ mask) for k in range(size)])  15.4 us
    pallas_call x8, Pallas kernels, plain(): pl.pallas_call(body, in_specs=[pl.BlockSpec(memory_space=pltpu.SMEM)] + [...  12.8 us
    ppermute x3, waiting for transfers between devices, on_device(): lax.ppermute(tile, AUX + ROW, [(a * 32 + k * 8 + spot(s), k * 32 + a * 8...  10.9 us
    pallas_call x1, Pallas kernels, half_begin(): pl.pallas_call(begin_kernel, in_specs=[smem, smem, pl.BlockSpec(memory_sp...  8.69 us
    all_to_all x1, starting transfers between devices, on_device(): summed = lax.all_to_all(pieces, ROW, 0, 0, tiled=True).reshape(summed.shape)  7.84 us
    ppermute x3, starting transfers between devices, on_device(): lax.ppermute(tile, AUX + ROW, [(a * 32 + k * 8 + spot(s), k * 32 + a * 8...  7.68 us
    ppermute x6, waiting for transfers between devices, shift(): lax.ppermute(value, axis, [(k, (k + step) % size) for k in range(size)])  7.07 us
  transfers between devices with their start and end apart: 21, of which 5 were waited for; matrix products, arithmetic and copies ran while one was open for 1% of the time, Pallas kernels for 16%

profile of v5, /device:TPU:1, one launch (start us, length us, event | category | flops | bytes accessed | tf_op | source)
XLA Modules:
  0.0 135.5 jit_solution(6327396626739344769)
XLA Ops:
  0.7 0.1 pad_add_fusion.where_ref
  0.8 0.8 constant_dynamic-slice_fusion
  1.5 0.2 broadcast_in_dim.5
  1.8 25.1 %all_to_all.15.orbit_ref.mine_ref = bf16[32,128,128]{2,1,0:T(8,128)(2,1)S(1)} all-to-all(bf16[32,128,128]{2,1,0:T(8,128)(2,1)S(1)} %broadcast_in_dim.5), channel_id=1, replica_groups=mesh['xh'=2,'core'=2,'z'=4,'xl'=2,'y'=4] {'z','xl','y'}, dimensions={0} | all-to-all | bytes 2097152 | tf_op jit(solution)/shard_map/all_to_all | solution.py:314
  26.9 1.8 %collective-permute-start = (bf16[32,128,128]{2,1,0:T(8,128)(2,1)S(1)}, bf16[32,128,128]{2,1,0:T(8,128)(2,1)S(1)}, u32[]{:S(2)}, u32[]{:S(2)}) collective-permute-start(bf16[32,128,128]{2,1,0:T(8,128)(2,1)S(1)} %all_to_all.15.orbit_ref.mine_ref), channel_id=1, source_target_pairs={{0,32},{32,0},{1,33},{33,1},{2,34},{34,2},{3,35},{35,3},{4,36},{36... | collective-permute-start | bytes 3145736 | tf_op jit(solution)/shard_map/ppermute | solution.py:22
  28.7 8.7 %shard_map.59 = (bf16[5,256,8192]{2,1,0:T(8,128)(2,1)S(1)}, f32[2,640,128]{2,1,0:T(8,128)S(1)}) custom-call(s32[1]{0:T(128)} %bitcast.parity_ref, s32[2,64]{1,0:T(2,128)S(1)} %bitcast.14, bf16[5,256,8192]{2,1,0:T(8,128)(2,1)} %slab_ref.1, bf16[32,128,128]{2,1,0:T(8,128)(2,1)S(1)} %all_to_all.15.orbit_ref.mine_ref), custom_call_target="tpu_custom_call" | custom-call | flops 1342177280 | bytes 20971520 | tf_op jit(solution)/shard_map/pallas_call | solution.py:112
  37.4 0.0 copy-start
  37.4 0.0 copy-start.2
  37.4 3.5 %shard_map.60.flat_ref = bf16[256,640]{1,0:T(8,128)(2,1)S(1)} custom-call(s32[1]{0:T(128)S(6)} %sub.7.parity_ref, s32[2,64]{1,0:T(2,128)S(1)} %bitcast.15, bf16[5,256,8192]{2,1,0:T(8,128)(2,1)S(1)} %get-tuple-element.35.kept_ref, bf16[32,128,128]{2,1,0:T(8,128)(2,1)S(1)} %collective-permute-done.orbit_ref.other_ref, ...), custom_call_target="tpu_custom_call" | custom-call | flops 1342177280 | bytes 10485760 | tf_op jit(solution)/shard_map/pallas_call | solution.py:132
  40.9 2.4 %collective-permute-start.2 = (bf16[256,640]{1,0:T(8,128)(2,1)S(1)}, bf16[256,640]{1,0:T(8,128)(2,1)S(1)}, u32[]{:S(2)}, u32[]{:S(2)}) collective-permute-start(bf16[256,640]{1,0:T(8,128)(2,1)S(1)} %shard_map.60.flat_ref), channel_id=1, source_target_pairs={{0,64},{8,96},{16,0},{24,32},{32,72},{40,104},{48,8},{56,40},{64,8... | collective-permute-start | bytes 983048 | tf_op jit(solution)/shard_map/ppermute | solution.py:323
  43.4 3.5 %collective-permute-start.1 = (bf16[256,640]{1,0:T(8,128)(2,1)S(1)}, bf16[256,640]{1,0:T(8,128)(2,1)S(1)}, u32[]{:S(2)}, u32[]{:S(2)}) collective-permute-start(bf16[256,640]{1,0:T(8,128)(2,1)S(1)} %shard_map.60.flat_ref), channel_id=1, source_target_pairs={{0,0},{8,32},{16,64},{24,96},{32,8},{40,40},{48,72},{56,104},{64,1... | collective-permute-start | bytes 983048 | tf_op jit(solution)/shard_map/ppermute | solution.py:323
  46.9 2.3 %shard_map.61 = (f32[768,128]{1,0:T(8,128)}, f32[256,128]{1,0:T(8,128)S(1)}) custom-call(s32[2]{0:T(128)S(1)} %pad_add_fusion.where_ref, bf16[256,640]{1,0:T(8,128)(2,1)S(1)} %shard_map.60.flat_ref, bf16[256,128]{1,0:T(8,128)(2,1)S(1)} %copy-done, bf16[32,128,128]{2,1,0:T(8,128)(2,1)S(1)} %all_to_all.15.orbit_ref.mine_ref, ...), custom_call_target="tpu_custom_call" | custom-call | flops 10000000000 | bytes 4000000 | tf_op jit(solution)/shard_map/pallas_call | solution.py:146
  49.1 5.6 %all-to-all-start.1 = ((f32[32,24,128]{2,1,0:T(8,128)}), f32[32,24,128]{2,1,0:T(8,128)S(1)}, u32[]{:S(2)}, u32[]{:S(2)}) async-start(f32[32,24,128]{2,1,0:T(8,128)} %bitcast.7), calls=%async_computation.1 | async-start | bytes 786432 | tf_op jit(solution)/shard_map/all_to_all | solution.py:354
  54.7 3.4 %collective-permute-start.4 = (bf16[256,640]{1,0:T(8,128)(2,1)S(1)}, bf16[256,640]{1,0:T(8,128)(2,1)S(1)}, u32[]{:S(2)}, u32[]{:S(2)}) collective-permute-start(bf16[256,640]{1,0:T(8,128)(2,1)S(1)} %collective-permute-done.1.r0), channel_id=1, source_target_pairs={{4,0},{1,4},{5,1},{2,5},{6,2},{3,6},{7,3},{0,7},{12,8},{9,12},{13,... | collective-permute-start | bytes 983048 | tf_op jit(solution)/shard_map/ppermute | solution.py:347
  58.2 0.6 collective-permute-start.7
  58.7 0.2 collective-permute-start.6
  59.0 1.6 %collective-permute-start.5 = (bf16[256,640]{1,0:T(8,128)(2,1)S(1)}, bf16[256,640]{1,0:T(8,128)(2,1)S(1)}, u32[]{:S(2)}, u32[]{:S(2)}) collective-permute-start(bf16[256,640]{1,0:T(8,128)(2,1)S(1)} %collective-permute-done.1.r0), channel_id=1, source_target_pairs={{3,0},{7,4},{0,1},{4,5},{1,2},{5,6},{2,3},{6,7},{11,8},{15,12},{8,... | collective-permute-start | bytes 983048 | tf_op jit(solution)/shard_map/ppermute | solution.py:347
  60.6 0.9 pad_maximum_fusion
  61.5 2.1 %collective-permute-start.3 = (bf16[2,256,640]{2,1,0:T(8,128)(2,1)}, bf16[2,256,640]{2,1,0:T(8,128)(2,1)S(1)}, u32[]{:S(2)}, u32[]{:S(2)}) collective-permute-start(bf16[2,256,640]{2,1,0:T(8,128)(2,1)} %pad_maximum_fusion), channel_id=1, source_target_pairs={{0,32},{32,0},{1,33},{33,1},{2,34},{34,2},{3,35},{35,3},{4,36},{36... | collective-permute-start | bytes 1966088 | tf_op jit(solution)/shard_map/ppermute | solution.py:22
  63.6 3.2 %collective-permute-done.4.c1 = bf16[256,640]{1,0:T(8,128)(2,1)S(1)} collective-permute-done((bf16[256,640]{1,0:T(8,128)(2,1)S(1)}, bf16[256,640]{1,0:T(8,128)(2,1)S(1)}, u32[]{:S(2)}, u32[]{:S(2)}) %collective-permute-start.4) | collective-permute-done | bytes 327712 | tf_op jit(solution)/shard_map/ppermute | solution.py:347
  66.9 1.3 shard_map.66
  68.2 7.8 %all-to-all-start.2 = ((f32[32,24,128]{2,1,0:T(8,128)}), f32[32,24,128]{2,1,0:T(8,128)S(1)}, u32[]{:S(2)}, u32[]{:S(2)}) async-start(f32[32,24,128]{2,1,0:T(8,128)} %shard_map.66), calls=%async_computation.2 | async-start | bytes 786432 | tf_op jit(solution)/shard_map/all_to_all | solution.py:405
  76.1 0.1 slice_bitcast_fusion
  76.2 1.0 collective-permute-done.5.c2
  77.1 3.5 %shard_map.62 = (bf16[256,640]{1,0:T(8,128)(2,1)}, bf16[256,640]{1,0:T(8,128)(2,1)}, f32[256,640]{1,0:T(8,128)S(1)}, bf16[256,640]{1,0:T(8,128)(2,1)S(1)}, bf16[...) custom-call(s32[4]{0:T(128)S(1)} %fusion.where_ref._, ...), custom_call_target="tpu_custom_call" | custom-call | flops 1000000000 | bytes 4000000 | tf_op jit(solution)/shard_map/pallas_call | solution.py:146
  80.6 0.8 copy-done.3
  81.5 0.9 copy-done.5
  82.3 0.9 copy-done.7
  83.2 0.8 copy-done.9
  84.0 1.2 collective-permute-start.8
  85.2 1.5 %collective-permute-start.9 = (bf16[256,640]{1,0:T(8,128)(2,1)}, bf16[256,640]{1,0:T(8,128)(2,1)S(1)}, u32[]{:S(2)}, u32[]{:S(2)}) collective-permute-start(bf16[256,640]{1,0:T(8,128)(2,1)} %get-tuple-element.46), channel_id=1, source_target_pairs={{0,24},{8,0},{16,8},{24,16},{1,25},{9,1},{17,9},{25,17},{2,26},{10... | collective-permute-start | bytes 983048 | tf_op jit(solution)/shard_map/ppermute | solution.py:26
  86.7 1.4 %collective-permute-start.11 = (bf16[256,640]{1,0:T(8,128)(2,1)S(1)}, bf16[256,640]{1,0:T(8,128)(2,1)S(1)}, u32[]{:S(2)}, u32[]{:S(2)}) collective-permute-start(bf16[256,640]{1,0:T(8,128)(2,1)S(1)} %get-tuple-element.48), channel_id=1, source_target_pairs={{0,24},{8,0},{16,8},{24,16},{1,25},{9,1},{17,9},{25,17},{2,26},{10... | collective-permute-start | bytes 983048 | tf_op jit(solution)/shard_map/ppermute | solution.py:26
  88.1 0.1 collective-permute-start.12
  88.2 1.0 shard_map.67.left
  89.2 10.7 %collective-permute-start.17 = (f32[384,128]{1,0:T(8,128)S(1)}, f32[384,128]{1,0:T(8,128)S(1)}, u32[]{:S(2)}, u32[]{:S(2)}) collective-permute-start(f32[384,128]{1,0:T(8,128)S(1)} %shard_map.67.left), channel_id=1, source_target_pairs={{0,32},{32,0},{1,33},{33,1},{2,34},{34,2},{3,35},{35,3},{4,36},{36... | collective-permute-start | bytes 589832 | tf_op jit(solution)/shard_map/ppermute | solution.py:22
  100.0 0.7 shard_map.63
  100.6 0.0 copy-start.4
  100.6 0.2 collective-permute-start.10
  100.8 2.5 %collective-permute-start.13 = (bf16[256,640]{1,0:T(8,128)(2,1)S(1)}, bf16[256,640]{1,0:T(8,128)(2,1)S(1)}, u32[]{:S(2)}, u32[]{:S(2)}) collective-permute-start(bf16[256,640]{1,0:T(8,128)(2,1)S(1)} %get-tuple-element.51), channel_id=1, source_target_pairs={{0,24},{8,0},{16,8},{24,16},{1,25},{9,1},{17,9},{25,17},{2,26},{10... | collective-permute-start | bytes 983048 | tf_op jit(solution)/shard_map/ppermute | solution.py:26
  103.4 0.6 shard_map.68.left
  104.0 0.7 collective-permute-start.18
  104.7 7.1 %collective-permute-done.10.up_a = bf16[256,640]{1,0:T(8,128)(2,1)S(1)} collective-permute-done((bf16[256,640]{1,0:T(8,128)(2,1)S(1)}, bf16[256,640]{1,0:T(8,128)(2,1)S(1)}, u32[]{:S(2)}, u32[]{:S(2)}) %collective-permute-start.10) | collective-permute-done | bytes 327712 | tf_op jit(solution)/shard_map/ppermute | solution.py:26
  111.7 2.1 %shard_map.64 = (f32[256,2048]{1,0:T(8,128)}, bf16[256,256]{1,0:T(8,128)(2,1)S(1)}, bf16[256,256]{1,0:T(8,128)(2,1)S(1)}, bf16[256,256]{1,0:T(8,128)(2,1)S(1)}) custom-call(s32[8]{0:T(128)S(1)} %fusion.2.place_ref, f32[256,640]{1,0:T(8,128)S(1)} %copy-done.4, bf16[256,640]{1,0:T(8,128)(2,1)S(1)} %collective-permute-done.10.up_a, ...), custom_call_target="tpu_custom_call" | custom-call | flops 1000000000 | bytes 4000000 | tf_op jit(solution)/shard_map/pallas_call | solution.py:146
  113.8 7.7 %collective-permute-start.14 = (bf16[256,256]{1,0:T(8,128)(2,1)S(1)}, bf16[256,256]{1,0:T(8,128)(2,1)S(1)}, u32[]{:S(2)}, u32[]{:S(2)}) collective-permute-start(bf16[256,256]{1,0:T(8,128)(2,1)S(1)} %get-tuple-element.52), channel_id=1, source_target_pairs={{0,4},{4,1},{1,5},{5,2},{2,6},{6,3},{3,7},{7,0},{8,36},{12,33},{9,... | collective-permute-start | bytes 393224 | tf_op jit(solution)/shard_map/ppermute | solution.py:391
  121.5 1.4 %shard_map.69 = f32[256,128]{1,0:T(8,128)} custom-call(s32[4]{0:T(128)S(1)} %fusion.where_ref._, bf16[256,128]{1,0:T(8,128)(2,1)S(1)} %copy-done, f32[384,128]{1,0:T(8,128)S(1)} %shard_map.68.left, f32[384,128]{1,0:T(8,128)S(1)} %collective-permute-done.18.right), custom_call_target="tpu_custom_call" | custom-call | flops 1000000000 | bytes 4000000 | tf_op jit(solution)/shard_map/pallas_call | solution.py:146
  122.9 2.7 %collective-permute-done.14.t1 = bf16[256,256]{1,0:T(8,128)(2,1)S(1)} collective-permute-done((bf16[256,256]{1,0:T(8,128)(2,1)S(1)}, bf16[256,256]{1,0:T(8,128)(2,1)S(1)}, u32[]{:S(2)}, u32[]{:S(2)}) %collective-permute-start.14) | collective-permute-done | bytes 131104 | tf_op jit(solution)/shard_map/ppermute | solution.py:391
  125.6 8.2 %collective-permute-done.15.t2 = bf16[256,256]{1,0:T(8,128)(2,1)S(1)} collective-permute-done((bf16[256,256]{1,0:T(8,128)(2,1)S(1)}, bf16[256,256]{1,0:T(8,128)(2,1)S(1)}, u32[]{:S(2)}, u32[]{:S(2)}) %collective-permute-start.15) | collective-permute-done | bytes 131104 | tf_op jit(solution)/shard_map/ppermute | solution.py:391
  133.8 1.5 %shard_map.65 = f32[256,2048]{1,0:T(8,128)} custom-call(s32[8]{0:T(128)S(1)} %fusion.2.place_ref, bf16[256,256]{1,0:T(8,128)(2,1)S(1)} %collective-permute-done.14.t1, bf16[256,256]{1,0:T(8,128)(2,1)S(1)} %collective-permute-done.15.t2, bf16[256,256]{1,0:T(8,128)(2,1)S(1)} %collective-permute-done.16.t3, ...), custom_call_target="tpu_custom_call", output_to_operand_aliasing={{}: (4, {})} | custom-call | tf_op jit(solution)/shard_map/pallas_call | solution.py:286
  (35 shorter events, 0.1 us)
Async XLA Ops:
  0.6 28.1 %copy-start.1 = (s32[1,2,64]{2,1,0:T(2,128)S(1)}, s32[1,2,64]{2,1,0:T(2,128)}, u32[]{:S(2)}) copy-start(s32[1,2,64]{2,1,0:T(2,128)} %param.5) | copy-start | bytes 1540
  26.9 10.5 %collective-permute-start = (bf16[32,128,128]{2,1,0:T(8,128)(2,1)S(1)}, bf16[32,128,128]{2,1,0:T(8,128)(2,1)S(1)}, u32[]{:S(2)}, u32[]{:S(2)}) collective-permute-start(bf16[32,128,128]{2,1,0:T(8,128)(2,1)S(1)} %all_to_all.15.orbit_ref.mine_ref), channel_id=1, source_target_pairs={{0,32},{32,0},{1,33},{33,1},{2,34},{34,2},{3,35},{35,3},{4,36},{36... | collective-permute-start | bytes 3145736 | tf_op jit(solution)/shard_map/ppermute | solution.py:22
  37.4 9.4 %copy-start = (bf16[256,128]{1,0:T(8,128)(2,1)S(1)}, bf16[256,128]{1,0:T(8,128)(2,1)}, u32[]{:S(2)}) copy-start(bf16[256,128]{1,0:T(8,128)(2,1)} %orbit_ref.3) | copy-start | bytes 196612
  37.4 9.4 %copy-start.2 = (f32[256,2048]{1,0:T(8,128)S(1)}, f32[256,2048]{1,0:T(8,128)}, u32[]{:S(2)}) copy-start(f32[256,2048]{1,0:T(8,128)} %hcore_ref.1) | copy-start | bytes 6291460
  40.9 13.8 %collective-permute-start.2 = (bf16[256,640]{1,0:T(8,128)(2,1)S(1)}, bf16[256,640]{1,0:T(8,128)(2,1)S(1)}, u32[]{:S(2)}, u32[]{:S(2)}) collective-permute-start(bf16[256,640]{1,0:T(8,128)(2,1)S(1)} %shard_map.60.flat_ref), channel_id=1, source_target_pairs={{0,64},{8,96},{16,0},{24,32},{32,72},{40,104},{48,8},{56,40},{64,8... | collective-permute-start | bytes 983048 | tf_op jit(solution)/shard_map/ppermute | solution.py:323
  43.4 11.4 %collective-permute-start.1 = (bf16[256,640]{1,0:T(8,128)(2,1)S(1)}, bf16[256,640]{1,0:T(8,128)(2,1)S(1)}, u32[]{:S(2)}, u32[]{:S(2)}) collective-permute-start(bf16[256,640]{1,0:T(8,128)(2,1)S(1)} %shard_map.60.flat_ref), channel_id=1, source_target_pairs={{0,0},{8,32},{16,64},{24,96},{32,8},{40,40},{48,72},{56,104},{64,1... | collective-permute-start | bytes 983048 | tf_op jit(solution)/shard_map/ppermute | solution.py:323
  49.1 14.5 %all-to-all-start.1 = ((f32[32,24,128]{2,1,0:T(8,128)}), f32[32,24,128]{2,1,0:T(8,128)S(1)}, u32[]{:S(2)}, u32[]{:S(2)}) async-start(f32[32,24,128]{2,1,0:T(8,128)} %bitcast.7), calls=%async_computation.1 | async-start | bytes 786432 | tf_op jit(solution)/shard_map/all_to_all | solution.py:354
  54.7 12.1 %collective-permute-start.4 = (bf16[256,640]{1,0:T(8,128)(2,1)S(1)}, bf16[256,640]{1,0:T(8,128)(2,1)S(1)}, u32[]{:S(2)}, u32[]{:S(2)}) collective-permute-start(bf16[256,640]{1,0:T(8,128)(2,1)S(1)} %collective-permute-done.1.r0), channel_id=1, source_target_pairs={{4,0},{1,4},{5,1},{2,5},{6,2},{3,6},{7,3},{0,7},{12,8},{9,12},{13,... | collective-permute-start | bytes 983048 | tf_op jit(solution)/shard_map/ppermute | solution.py:347
  58.2 18.0 %collective-permute-start.7 = (bf16[256,640]{1,0:T(8,128)(2,1)S(1)}, bf16[256,640]{1,0:T(8,128)(2,1)S(1)}, u32[]{:S(2)}, u32[]{:S(2)}) collective-permute-start(bf16[256,640]{1,0:T(8,128)(2,1)S(1)} %collective-permute-done.1.r0), channel_id=1, source_target_pairs={{2,0},{6,4},{3,1},{7,5},{0,2},{4,6},{1,3},{5,7},{10,8},{14,12},{11... | collective-permute-start | bytes 983048 | tf_op jit(solution)/shard_map/ppermute | solution.py:347
  58.7 17.4 %collective-permute-start.6 = (bf16[256,640]{1,0:T(8,128)(2,1)S(1)}, bf16[256,640]{1,0:T(8,128)(2,1)S(1)}, u32[]{:S(2)}, u32[]{:S(2)}) collective-permute-start(bf16[256,640]{1,0:T(8,128)(2,1)S(1)} %collective-permute-done.1.r0), channel_id=1, source_target_pairs={{5,0},{2,4},{6,1},{3,5},{7,2},{0,6},{4,3},{1,7},{13,8},{10,12},{14... | collective-permute-start | bytes 983048 | tf_op jit(solution)/shard_map/ppermute | solution.py:347
  59.0 18.2 %collective-permute-start.5 = (bf16[256,640]{1,0:T(8,128)(2,1)S(1)}, bf16[256,640]{1,0:T(8,128)(2,1)S(1)}, u32[]{:S(2)}, u32[]{:S(2)}) collective-permute-start(bf16[256,640]{1,0:T(8,128)(2,1)S(1)} %collective-permute-done.1.r0), channel_id=1, source_target_pairs={{3,0},{7,4},{0,1},{4,5},{1,2},{5,6},{2,3},{6,7},{11,8},{15,12},{8,... | collective-permute-start | bytes 983048 | tf_op jit(solution)/shard_map/ppermute | solution.py:347
  61.5 14.6 %collective-permute-start.3 = (bf16[2,256,640]{2,1,0:T(8,128)(2,1)}, bf16[2,256,640]{2,1,0:T(8,128)(2,1)S(1)}, u32[]{:S(2)}, u32[]{:S(2)}) collective-permute-start(bf16[2,256,640]{2,1,0:T(8,128)(2,1)} %pad_maximum_fusion), channel_id=1, source_target_pairs={{0,32},{32,0},{1,33},{33,1},{2,34},{34,2},{3,35},{35,3},{4,36},{36... | collective-permute-start | bytes 1966088 | tf_op jit(solution)/shard_map/ppermute | solution.py:22
  68.2 20.0 %all-to-all-start.2 = ((f32[32,24,128]{2,1,0:T(8,128)}), f32[32,24,128]{2,1,0:T(8,128)S(1)}, u32[]{:S(2)}, u32[]{:S(2)}) async-start(f32[32,24,128]{2,1,0:T(8,128)} %shard_map.66), calls=%async_computation.2 | async-start | bytes 786432 | tf_op jit(solution)/shard_map/all_to_all | solution.py:405
  80.6 0.8 copy-start.3
  81.5 0.9 copy-start.5
  82.3 0.9 copy-start.7
  83.2 0.8 copy-start.9
  84.0 15.9 %copy-start.8 = (f32[256,640]{1,0:T(8,128)S(1)}, f32[256,640]{1,0:T(8,128)}, u32[]{:S(2)}) copy-start(f32[256,640]{1,0:T(8,128)} %copy-done.7) | copy-start | bytes 1966084
  84.0 15.9 %collective-permute-start.8 = (bf16[256,640]{1,0:T(8,128)(2,1)}, bf16[256,640]{1,0:T(8,128)(2,1)S(1)}, u32[]{:S(2)}, u32[]{:S(2)}) collective-permute-start(bf16[256,640]{1,0:T(8,128)(2,1)} %get-tuple-element.44), channel_id=1, source_target_pairs={{0,8},{8,16},{16,24},{24,0},{1,9},{9,17},{17,25},{25,1},{2,10},{10... | collective-permute-start | bytes 983048 | tf_op jit(solution)/shard_map/ppermute | solution.py:26
  85.2 14.7 %collective-permute-start.9 = (bf16[256,640]{1,0:T(8,128)(2,1)}, bf16[256,640]{1,0:T(8,128)(2,1)S(1)}, u32[]{:S(2)}, u32[]{:S(2)}) collective-permute-start(bf16[256,640]{1,0:T(8,128)(2,1)} %get-tuple-element.46), channel_id=1, source_target_pairs={{0,24},{8,0},{16,8},{24,16},{1,25},{9,1},{17,9},{25,17},{2,26},{10... | collective-permute-start | bytes 983048 | tf_op jit(solution)/shard_map/ppermute | solution.py:26
  86.7 17.9 %collective-permute-start.11 = (bf16[256,640]{1,0:T(8,128)(2,1)S(1)}, bf16[256,640]{1,0:T(8,128)(2,1)S(1)}, u32[]{:S(2)}, u32[]{:S(2)}) collective-permute-start(bf16[256,640]{1,0:T(8,128)(2,1)S(1)} %get-tuple-element.48), channel_id=1, source_target_pairs={{0,24},{8,0},{16,8},{24,16},{1,25},{9,1},{17,9},{25,17},{2,26},{10... | collective-permute-start | bytes 983048 | tf_op jit(solution)/shard_map/ppermute | solution.py:26
  88.1 16.6 %collective-permute-start.12 = (bf16[256,640]{1,0:T(8,128)(2,1)S(1)}, bf16[256,640]{1,0:T(8,128)(2,1)S(1)}, u32[]{:S(2)}, u32[]{:S(2)}) collective-permute-start(bf16[256,640]{1,0:T(8,128)(2,1)S(1)} %get-tuple-element.50), channel_id=1, source_target_pairs={{0,8},{8,16},{16,24},{24,0},{1,9},{9,17},{17,25},{25,1},{2,10},{10... | collective-permute-start | bytes 983048 | tf_op jit(solution)/shard_map/ppermute | solution.py:26
  88.2 11.8 %copy-start.10 = (f32[256,640]{1,0:T(8,128)S(1)}, f32[256,640]{1,0:T(8,128)}, u32[]{:S(2)}) copy-start(f32[256,640]{1,0:T(8,128)} %copy-done.9) | copy-start | bytes 1966084
  89.2 14.2 %collective-permute-start.17 = (f32[384,128]{1,0:T(8,128)S(1)}, f32[384,128]{1,0:T(8,128)S(1)}, u32[]{:S(2)}, u32[]{:S(2)}) collective-permute-start(f32[384,128]{1,0:T(8,128)S(1)} %shard_map.67.left), channel_id=1, source_target_pairs={{0,32},{32,0},{1,33},{33,1},{2,34},{34,2},{3,35},{35,3},{4,36},{36... | collective-permute-start | bytes 589832 | tf_op jit(solution)/shard_map/ppermute | solution.py:22
  100.6 11.1 %copy-start.4 = (f32[256,640]{1,0:T(8,128)S(1)}, f32[256,640]{1,0:T(8,128)}, u32[]{:S(2)}) copy-start(f32[256,640]{1,0:T(8,128)} %copy-done.3) | copy-start | bytes 1966084
  100.6 11.1 %copy-start.6 = (f32[256,640]{1,0:T(8,128)S(1)}, f32[256,640]{1,0:T(8,128)}, u32[]{:S(2)}) copy-start(f32[256,640]{1,0:T(8,128)} %copy-done.5) | copy-start | bytes 1966084
  100.6 11.1 %collective-permute-start.10 = (bf16[256,640]{1,0:T(8,128)(2,1)S(1)}, bf16[256,640]{1,0:T(8,128)(2,1)S(1)}, u32[]{:S(2)}, u32[]{:S(2)}) collective-permute-start(bf16[256,640]{1,0:T(8,128)(2,1)S(1)} %get-tuple-element.47), channel_id=1, source_target_pairs={{0,8},{8,16},{16,24},{24,0},{1,9},{9,17},{17,25},{25,1},{2,10},{10... | collective-permute-start | bytes 983048 | tf_op jit(solution)/shard_map/ppermute | solution.py:26
  100.8 10.9 %collective-permute-start.13 = (bf16[256,640]{1,0:T(8,128)(2,1)S(1)}, bf16[256,640]{1,0:T(8,128)(2,1)S(1)}, u32[]{:S(2)}, u32[]{:S(2)}) collective-permute-start(bf16[256,640]{1,0:T(8,128)(2,1)S(1)} %get-tuple-element.51), channel_id=1, source_target_pairs={{0,24},{8,0},{16,8},{24,16},{1,25},{9,1},{17,9},{25,17},{2,26},{10... | collective-permute-start | bytes 983048 | tf_op jit(solution)/shard_map/ppermute | solution.py:26
  104.0 17.5 %collective-permute-start.18 = (f32[384,128]{1,0:T(8,128)S(1)}, f32[384,128]{1,0:T(8,128)S(1)}, u32[]{:S(2)}, u32[]{:S(2)}) collective-permute-start(f32[384,128]{1,0:T(8,128)S(1)} %shard_map.68.left), channel_id=1, source_target_pairs={{0,64},{64,0},{1,65},{65,1},{2,66},{66,2},{3,67},{67,3},{4,68},{68... | collective-permute-start | bytes 589832 | tf_op jit(solution)/shard_map/ppermute | solution.py:22
  113.8 11.7 %collective-permute-start.14 = (bf16[256,256]{1,0:T(8,128)(2,1)S(1)}, bf16[256,256]{1,0:T(8,128)(2,1)S(1)}, u32[]{:S(2)}, u32[]{:S(2)}) collective-permute-start(bf16[256,256]{1,0:T(8,128)(2,1)S(1)} %get-tuple-element.52), channel_id=1, source_target_pairs={{0,4},{4,1},{1,5},{5,2},{2,6},{6,3},{3,7},{7,0},{8,36},{12,33},{9,... | collective-permute-start | bytes 393224 | tf_op jit(solution)/shard_map/ppermute | solution.py:391
  121.5 12.3 %collective-permute-start.15 = (bf16[256,256]{1,0:T(8,128)(2,1)S(1)}, bf16[256,256]{1,0:T(8,128)(2,1)S(1)}, u32[]{:S(2)}, u32[]{:S(2)}) collective-permute-start(bf16[256,256]{1,0:T(8,128)(2,1)S(1)} %get-tuple-element.53), channel_id=1, source_target_pairs={{0,3},{4,7},{1,0},{5,4},{2,1},{6,5},{3,2},{7,6},{8,35},{12,39},{9,... | collective-permute-start | bytes 393224 | tf_op jit(solution)/shard_map/ppermute | solution.py:391
  121.5 12.3 %collective-permute-start.16 = (bf16[256,256]{1,0:T(8,128)(2,1)S(1)}, bf16[256,256]{1,0:T(8,128)(2,1)S(1)}, u32[]{:S(2)}, u32[]{:S(2)}) collective-permute-start(bf16[256,256]{1,0:T(8,128)(2,1)S(1)} %get-tuple-element.54), channel_id=1, source_target_pairs={{0,5},{4,2},{1,6},{5,3},{2,7},{6,0},{3,4},{7,1},{8,37},{12,34},{9,... | collective-permute-start | bytes 393224 | tf_op jit(solution)/shard_map/ppermute | solution.py:391

commit v6 on v5

--- a/solution.py
+++ b/solution.py
@@ -183,8 +183,8 @@
 
 
 def relay_kernel(_, up_a, far_a, down_b, far_b, out_a, out_b):
-    out_a[...] = (up_a[...] + far_a[...].astype(F32)).astype(BF)
-    out_b[...] = (down_b[...] + far_b[...].astype(F32)).astype(BF)
+    out_a[...] = (up_a[...].astype(F32) + far_a[...].astype(F32)).astype(BF)
+    out_b[...] = (down_b[...].astype(F32) + far_b[...].astype(F32)).astype(BF)
 
 
 def home_kernel(
@@ -195,8 +195,8 @@
     def at(k):
         return pl.ds(pl.multiple_of(place_ref[k] * n, 128), n)
 
-    a = (home_a[...] + up_a[...].astype(F32) + down_a[...].astype(F32)) * scale
-    b = (home_b[...] + up_b[...].astype(F32) + down_b[...].astype(F32)) * scale
+    a = (home_a[...].astype(F32) + up_a[...].astype(F32) + down_a[...].astype(F32)) * scale
+    b = (home_b[...].astype(F32) + up_b[...].astype(F32) + down_b[...].astype(F32)) * scale
     t1[...] = a[:, :n].astype(BF)
     t2[...] = a[:, n : 2 * n].astype(BF)
     t3[...] = b[:, :n].astype(BF)
@@ -354,10 +354,9 @@
     pieces = lax.all_to_all(pieces, ROW, 0, 0, tiled=True)
     pieces, factors[4] = lax.optimization_barrier((pieces, factors[4]))
     part = jax.ShapeDtypeStruct((row_count, 5 * row_count // 2), BF)
-    part_f32 = jax.ShapeDtypeStruct(part.shape, F32)
     far_a, far_b, up_a, up_b, down_a, down_b, home_a, home_b = plain(
         product_kernel,
-        [part, part, part_f32, part, part, part_f32, part_f32, part_f32],
+        [part] * 8,
         where,
         *factors,
     )

time: 138 us -> 137 us (level)
  no operation moved by 1% of the time
where the time goes in v6:
time: 137 us; the launch traced here: 135 us
  starting transfers between devices  55.1 us (40%)
  Pallas kernels  26.6 us (19%)
  blocking collectives  25.1 us (18%)
  waiting for transfers between devices  22.2 us (16%)
  local copies, waits for them, and re-layouts  4.01 us (3%)
    all_to_all x1, blocking collectives, on_device(): lax.all_to_all(jnp.broadcast_to(own[None], (row_devices,) + own.shape), R...  25.1 us
    ppermute x4, starting transfers between devices, flip(): return lax.ppermute(value, axis, [(k, k ^ mask) for k in range(size)])  15.4 us
    pallas_call x8, Pallas kernels, plain(): pl.pallas_call(body, in_specs=[pl.BlockSpec(memory_space=pltpu.SMEM)] + [...  12.9 us
    ppermute x3, waiting for transfers between devices, on_device(): lax.ppermute(tile, AUX + ROW, [(a * 32 + k * 8 + spot(s), k * 32 + a * 8...  10.9 us
    pallas_call x1, Pallas kernels, half_begin(): pl.pallas_call(begin_kernel, in_specs=[smem, smem, pl.BlockSpec(memory_sp...  8.69 us
    all_to_all x1, starting transfers between devices, on_device(): summed = lax.all_to_all(pieces, ROW, 0, 0, tiled=True).reshape(summed.shape)  7.84 us
    ppermute x3, starting transfers between devices, on_device(): lax.ppermute(tile, AUX + ROW, [(a * 32 + k * 8 + spot(s), k * 32 + a * 8...  7.63 us
    ppermute x6, waiting for transfers between devices, shift(): lax.ppermute(value, axis, [(k, (k + step) % size) for k in range(size)])  7.06 us
  transfers between devices with their start and end apart: 21, of which 5 were waited for; matrix products, arithmetic and copies ran while one was open for 1% of the time, Pallas kernels for 16%

profile of v6, /device:TPU:1, one launch (start us, length us, event | category | flops | bytes accessed | tf_op | source)
XLA Modules:
  0.0 135.0 jit_solution(14577963924102878483)
XLA Ops:
  0.7 0.1 pad_add_fusion.where_ref
  0.8 0.8 constant_dynamic-slice_fusion
  1.5 0.2 broadcast_in_dim.5
  1.8 25.1 %all_to_all.15.orbit_ref.mine_ref = bf16[32,128,128]{2,1,0:T(8,128)(2,1)S(1)} all-to-all(bf16[32,128,128]{2,1,0:T(8,128)(2,1)S(1)} %broadcast_in_dim.5), channel_id=1, replica_groups=mesh['xh'=2,'core'=2,'z'=4,'xl'=2,'y'=4] {'z','xl','y'}, dimensions={0} | all-to-all | bytes 2097152 | tf_op jit(solution)/shard_map/all_to_all | solution.py:314
  26.9 1.8 %collective-permute-start = (bf16[32,128,128]{2,1,0:T(8,128)(2,1)S(1)}, bf16[32,128,128]{2,1,0:T(8,128)(2,1)S(1)}, u32[]{:S(2)}, u32[]{:S(2)}) collective-permute-start(bf16[32,128,128]{2,1,0:T(8,128)(2,1)S(1)} %all_to_all.15.orbit_ref.mine_ref), channel_id=1, source_target_pairs={{0,32},{32,0},{1,33},{33,1},{2,34},{34,2},{3,35},{35,3},{4,36},{36... | collective-permute-start | bytes 3145736 | tf_op jit(solution)/shard_map/ppermute | solution.py:22
  28.7 8.7 %shard_map.59 = (bf16[5,256,8192]{2,1,0:T(8,128)(2,1)S(1)}, f32[2,640,128]{2,1,0:T(8,128)S(1)}) custom-call(s32[1]{0:T(128)} %bitcast.parity_ref, s32[2,64]{1,0:T(2,128)S(1)} %bitcast.14, bf16[5,256,8192]{2,1,0:T(8,128)(2,1)} %slab_ref.1, bf16[32,128,128]{2,1,0:T(8,128)(2,1)S(1)} %all_to_all.15.orbit_ref.mine_ref), custom_call_target="tpu_custom_call" | custom-call | flops 1342177280 | bytes 20971520 | tf_op jit(solution)/shard_map/pallas_call | solution.py:112
  37.4 0.0 collective-permute-done.orbit_ref.other_ref
  37.4 0.0 copy-start
  37.4 0.0 copy-start.2
  37.4 3.5 %shard_map.60.flat_ref = bf16[256,640]{1,0:T(8,128)(2,1)S(1)} custom-call(s32[1]{0:T(128)S(6)} %sub.7.parity_ref, s32[2,64]{1,0:T(2,128)S(1)} %bitcast.15, bf16[5,256,8192]{2,1,0:T(8,128)(2,1)S(1)} %get-tuple-element.35.kept_ref, bf16[32,128,128]{2,1,0:T(8,128)(2,1)S(1)} %collective-permute-done.orbit_ref.other_ref, ...), custom_call_target="tpu_custom_call" | custom-call | flops 1342177280 | bytes 10485760 | tf_op jit(solution)/shard_map/pallas_call | solution.py:132
  40.9 2.4 %collective-permute-start.2 = (bf16[256,640]{1,0:T(8,128)(2,1)S(1)}, bf16[256,640]{1,0:T(8,128)(2,1)S(1)}, u32[]{:S(2)}, u32[]{:S(2)}) collective-permute-start(bf16[256,640]{1,0:T(8,128)(2,1)S(1)} %shard_map.60.flat_ref), channel_id=1, source_target_pairs={{0,64},{8,96},{16,0},{24,32},{32,72},{40,104},{48,8},{56,40},{64,8... | collective-permute-start | bytes 983048 | tf_op jit(solution)/shard_map/ppermute | solution.py:323
  43.4 3.5 %collective-permute-start.1 = (bf16[256,640]{1,0:T(8,128)(2,1)S(1)}, bf16[256,640]{1,0:T(8,128)(2,1)S(1)}, u32[]{:S(2)}, u32[]{:S(2)}) collective-permute-start(bf16[256,640]{1,0:T(8,128)(2,1)S(1)} %shard_map.60.flat_ref), channel_id=1, source_target_pairs={{0,0},{8,32},{16,64},{24,96},{32,8},{40,40},{48,72},{56,104},{64,1... | collective-permute-start | bytes 983048 | tf_op jit(solution)/shard_map/ppermute | solution.py:323
  46.9 2.3 %shard_map.61 = (f32[768,128]{1,0:T(8,128)}, f32[256,128]{1,0:T(8,128)S(1)}) custom-call(s32[2]{0:T(128)S(1)} %pad_add_fusion.where_ref, bf16[256,640]{1,0:T(8,128)(2,1)S(1)} %shard_map.60.flat_ref, bf16[256,128]{1,0:T(8,128)(2,1)S(1)} %copy-done, bf16[32,128,128]{2,1,0:T(8,128)(2,1)S(1)} %all_to_all.15.orbit_ref.mine_ref, ...), custom_call_target="tpu_custom_call" | custom-call | flops 10000000000 | bytes 4000000 | tf_op jit(solution)/shard_map/pallas_call | solution.py:146
  49.1 5.6 %all-to-all-start.1 = ((f32[32,24,128]{2,1,0:T(8,128)}), f32[32,24,128]{2,1,0:T(8,128)S(1)}, u32[]{:S(2)}, u32[]{:S(2)}) async-start(f32[32,24,128]{2,1,0:T(8,128)} %bitcast.7), calls=%async_computation.1 | async-start | bytes 786432 | tf_op jit(solution)/shard_map/all_to_all | solution.py:354
  54.7 3.4 %collective-permute-start.4 = (bf16[256,640]{1,0:T(8,128)(2,1)S(1)}, bf16[256,640]{1,0:T(8,128)(2,1)S(1)}, u32[]{:S(2)}, u32[]{:S(2)}) collective-permute-start(bf16[256,640]{1,0:T(8,128)(2,1)S(1)} %collective-permute-done.1.r0), channel_id=1, source_target_pairs={{4,0},{1,4},{5,1},{2,5},{6,2},{3,6},{7,3},{0,7},{12,8},{9,12},{13,... | collective-permute-start | bytes 983048 | tf_op jit(solution)/shard_map/ppermute | solution.py:347
  58.2 0.6 collective-permute-start.7
  58.7 0.2 collective-permute-start.6
  59.0 1.6 %collective-permute-start.5 = (bf16[256,640]{1,0:T(8,128)(2,1)S(1)}, bf16[256,640]{1,0:T(8,128)(2,1)S(1)}, u32[]{:S(2)}, u32[]{:S(2)}) collective-permute-start(bf16[256,640]{1,0:T(8,128)(2,1)S(1)} %collective-permute-done.1.r0), channel_id=1, source_target_pairs={{3,0},{7,4},{0,1},{4,5},{1,2},{5,6},{2,3},{6,7},{11,8},{15,12},{8,... | collective-permute-start | bytes 983048 | tf_op jit(solution)/shard_map/ppermute | solution.py:347
  60.6 0.9 pad_maximum_fusion
  61.5 2.1 %collective-permute-start.3 = (bf16[2,256,640]{2,1,0:T(8,128)(2,1)}, bf16[2,256,640]{2,1,0:T(8,128)(2,1)S(1)}, u32[]{:S(2)}, u32[]{:S(2)}) collective-permute-start(bf16[2,256,640]{2,1,0:T(8,128)(2,1)} %pad_maximum_fusion), channel_id=1, source_target_pairs={{0,32},{32,0},{1,33},{33,1},{2,34},{34,2},{3,35},{35,3},{4,36},{36... | collective-permute-start | bytes 1966088 | tf_op jit(solution)/shard_map/ppermute | solution.py:22
  63.6 3.2 %collective-permute-done.4.c1 = bf16[256,640]{1,0:T(8,128)(2,1)S(1)} collective-permute-done((bf16[256,640]{1,0:T(8,128)(2,1)S(1)}, bf16[256,640]{1,0:T(8,128)(2,1)S(1)}, u32[]{:S(2)}, u32[]{:S(2)}) %collective-permute-start.4) | collective-permute-done | bytes 327712 | tf_op jit(solution)/shard_map/ppermute | solution.py:347
  66.9 1.4 %shard_map.66 = f32[32,24,128]{2,1,0:T(8,128)} custom-call(s32[4]{0:T(128)S(1)} %fusion.where_ref._, f32[32,24,128]{2,1,0:T(8,128)S(1)} %all-to-all-done.1.pieces_ref), custom_call_target="tpu_custom_call" | custom-call | flops 10000000000 | bytes 4000000 | tf_op jit(solution)/shard_map/pallas_call | solution.py:146
  68.2 7.8 %all-to-all-start.2 = ((f32[32,24,128]{2,1,0:T(8,128)}), f32[32,24,128]{2,1,0:T(8,128)S(1)}, u32[]{:S(2)}, u32[]{:S(2)}) async-start(f32[32,24,128]{2,1,0:T(8,128)} %shard_map.66), calls=%async_computation.2 | async-start | bytes 786432 | tf_op jit(solution)/shard_map/all_to_all | solution.py:404
  76.1 0.1 slice_bitcast_fusion
  76.2 0.9 collective-permute-done.5.c2
  77.1 3.5 %shard_map.62 = (bf16[256,640]{1,0:T(8,128)(2,1)}, bf16[256,640]{1,0:T(8,128)(2,1)}, bf16[256,640]{1,0:T(8,128)(2,1)S(1)}, bf16[256,640]{1,0:T(8,128)(2,1)S(1)},...) custom-call(s32[4]{0:T(128)S(1)} %fusion.where_ref._, ...), custom_call_target="tpu_custom_call" | custom-call | flops 1000000000 | bytes 4000000 | tf_op jit(solution)/shard_map/pallas_call | solution.py:146
  80.6 0.7 copy-done.3
  81.3 0.7 copy-done.5
  82.0 0.8 copy-done.7
  82.8 0.7 copy-done.9
  83.5 1.2 collective-permute-start.8
  84.7 1.5 %collective-permute-start.9 = (bf16[256,640]{1,0:T(8,128)(2,1)}, bf16[256,640]{1,0:T(8,128)(2,1)S(1)}, u32[]{:S(2)}, u32[]{:S(2)}) collective-permute-start(bf16[256,640]{1,0:T(8,128)(2,1)} %get-tuple-element.46), channel_id=1, source_target_pairs={{0,24},{8,0},{16,8},{24,16},{1,25},{9,1},{17,9},{25,17},{2,26},{10... | collective-permute-start | bytes 983048 | tf_op jit(solution)/shard_map/ppermute | solution.py:26
  86.2 1.4 %collective-permute-start.11 = (bf16[256,640]{1,0:T(8,128)(2,1)S(1)}, bf16[256,640]{1,0:T(8,128)(2,1)S(1)}, u32[]{:S(2)}, u32[]{:S(2)}) collective-permute-start(bf16[256,640]{1,0:T(8,128)(2,1)S(1)} %get-tuple-element.48), channel_id=1, source_target_pairs={{0,24},{8,0},{16,8},{24,16},{1,25},{9,1},{17,9},{25,17},{2,26},{10... | collective-permute-start | bytes 983048 | tf_op jit(solution)/shard_map/ppermute | solution.py:26
  87.6 0.1 collective-permute-start.12
  87.7 1.0 shard_map.67.left
  88.7 10.8 %collective-permute-start.17 = (f32[384,128]{1,0:T(8,128)S(1)}, f32[384,128]{1,0:T(8,128)S(1)}, u32[]{:S(2)}, u32[]{:S(2)}) collective-permute-start(f32[384,128]{1,0:T(8,128)S(1)} %shard_map.67.left), channel_id=1, source_target_pairs={{0,32},{32,0},{1,33},{33,1},{2,34},{34,2},{3,35},{35,3},{4,36},{36... | collective-permute-start | bytes 589832 | tf_op jit(solution)/shard_map/ppermute | solution.py:22
  99.5 0.7 shard_map.63
  100.2 0.2 collective-permute-start.10
  100.4 2.6 %collective-permute-start.13 = (bf16[256,640]{1,0:T(8,128)(2,1)S(1)}, bf16[256,640]{1,0:T(8,128)(2,1)S(1)}, u32[]{:S(2)}, u32[]{:S(2)}) collective-permute-start(bf16[256,640]{1,0:T(8,128)(2,1)S(1)} %get-tuple-element.51), channel_id=1, source_target_pairs={{0,24},{8,0},{16,8},{24,16},{1,25},{9,1},{17,9},{25,17},{2,26},{10... | collective-permute-start | bytes 983048 | tf_op jit(solution)/shard_map/ppermute | solution.py:26
  102.9 0.6 shard_map.68.left
  103.5 0.7 collective-permute-start.18
  104.2 7.0 %collective-permute-done.10.up_a = bf16[256,640]{1,0:T(8,128)(2,1)S(1)} collective-permute-done((bf16[256,640]{1,0:T(8,128)(2,1)S(1)}, bf16[256,640]{1,0:T(8,128)(2,1)S(1)}, u32[]{:S(2)}, u32[]{:S(2)}) %collective-permute-start.10) | collective-permute-done | bytes 327712 | tf_op jit(solution)/shard_map/ppermute | solution.py:26
  111.3 2.1 %shard_map.64 = (f32[256,2048]{1,0:T(8,128)}, bf16[256,256]{1,0:T(8,128)(2,1)S(1)}, bf16[256,256]{1,0:T(8,128)(2,1)S(1)}, bf16[256,256]{1,0:T(8,128)(2,1)S(1)}) custom-call(s32[8]{0:T(128)S(1)} %fusion.2.place_ref, bf16[256,640]{1,0:T(8,128)(2,1)S(1)} %copy-done.4, bf16[256,640]{1,0:T(8,128)(2,1)S(1)} %collective-permute-done.10.up_a, ...), custom_call_target="tpu_custom_call" | custom-call | flops 1000000000 | bytes 4000000 | tf_op jit(solution)/shard_map/pallas_call | solution.py:146
  113.4 7.6 %collective-permute-start.14 = (bf16[256,256]{1,0:T(8,128)(2,1)S(1)}, bf16[256,256]{1,0:T(8,128)(2,1)S(1)}, u32[]{:S(2)}, u32[]{:S(2)}) collective-permute-start(bf16[256,256]{1,0:T(8,128)(2,1)S(1)} %get-tuple-element.52), channel_id=1, source_target_pairs={{0,4},{4,1},{1,5},{5,2},{2,6},{6,3},{3,7},{7,0},{8,36},{12,33},{9,... | collective-permute-start | bytes 393224 | tf_op jit(solution)/shard_map/ppermute | solution.py:390
  121.0 1.4 %shard_map.69 = f32[256,128]{1,0:T(8,128)} custom-call(s32[4]{0:T(128)S(1)} %fusion.where_ref._, bf16[256,128]{1,0:T(8,128)(2,1)S(1)} %copy-done, f32[384,128]{1,0:T(8,128)S(1)} %shard_map.68.left, f32[384,128]{1,0:T(8,128)S(1)} %collective-permute-done.18.right), custom_call_target="tpu_custom_call" | custom-call | flops 1000000000 | bytes 4000000 | tf_op jit(solution)/shard_map/pallas_call | solution.py:146
  122.4 2.7 %collective-permute-done.14.t1 = bf16[256,256]{1,0:T(8,128)(2,1)S(1)} collective-permute-done((bf16[256,256]{1,0:T(8,128)(2,1)S(1)}, bf16[256,256]{1,0:T(8,128)(2,1)S(1)}, u32[]{:S(2)}, u32[]{:S(2)}) %collective-permute-start.14) | collective-permute-done | bytes 131104 | tf_op jit(solution)/shard_map/ppermute | solution.py:390
  125.1 8.2 %collective-permute-done.15.t2 = bf16[256,256]{1,0:T(8,128)(2,1)S(1)} collective-permute-done((bf16[256,256]{1,0:T(8,128)(2,1)S(1)}, bf16[256,256]{1,0:T(8,128)(2,1)S(1)}, u32[]{:S(2)}, u32[]{:S(2)}) %collective-permute-start.15) | collective-permute-done | bytes 131104 | tf_op jit(solution)/shard_map/ppermute | solution.py:390
  133.3 1.5 %shard_map.65 = f32[256,2048]{1,0:T(8,128)} custom-call(s32[8]{0:T(128)S(1)} %fusion.2.place_ref, bf16[256,256]{1,0:T(8,128)(2,1)S(1)} %collective-permute-done.14.t1, bf16[256,256]{1,0:T(8,128)(2,1)S(1)} %collective-permute-done.15.t2, bf16[256,256]{1,0:T(8,128)(2,1)S(1)} %collective-permute-done.16.t3, ...), custom_call_target="tpu_custom_call", output_to_operand_aliasing={{}: (4, {})} | custom-call | tf_op jit(solution)/shard_map/pallas_call | solution.py:286
  (35 shorter events, 0.1 us)
Async XLA Ops:
  0.6 28.1 %copy-start.1 = (s32[1,2,64]{2,1,0:T(2,128)S(1)}, s32[1,2,64]{2,1,0:T(2,128)}, u32[]{:S(2)}) copy-start(s32[1,2,64]{2,1,0:T(2,128)} %param.5) | copy-start | bytes 1540
  26.9 10.5 %collective-permute-start = (bf16[32,128,128]{2,1,0:T(8,128)(2,1)S(1)}, bf16[32,128,128]{2,1,0:T(8,128)(2,1)S(1)}, u32[]{:S(2)}, u32[]{:S(2)}) collective-permute-start(bf16[32,128,128]{2,1,0:T(8,128)(2,1)S(1)} %all_to_all.15.orbit_ref.mine_ref), channel_id=1, source_target_pairs={{0,32},{32,0},{1,33},{33,1},{2,34},{34,2},{3,35},{35,3},{4,36},{36... | collective-permute-start | bytes 3145736 | tf_op jit(solution)/shard_map/ppermute | solution.py:22
  37.4 9.4 %copy-start = (bf16[256,128]{1,0:T(8,128)(2,1)S(1)}, bf16[256,128]{1,0:T(8,128)(2,1)}, u32[]{:S(2)}) copy-start(bf16[256,128]{1,0:T(8,128)(2,1)} %orbit_ref.3) | copy-start | bytes 196612
  37.4 9.4 %copy-start.2 = (f32[256,2048]{1,0:T(8,128)S(1)}, f32[256,2048]{1,0:T(8,128)}, u32[]{:S(2)}) copy-start(f32[256,2048]{1,0:T(8,128)} %hcore_ref.1) | copy-start | bytes 6291460
  40.9 13.8 %collective-permute-start.2 = (bf16[256,640]{1,0:T(8,128)(2,1)S(1)}, bf16[256,640]{1,0:T(8,128)(2,1)S(1)}, u32[]{:S(2)}, u32[]{:S(2)}) collective-permute-start(bf16[256,640]{1,0:T(8,128)(2,1)S(1)} %shard_map.60.flat_ref), channel_id=1, source_target_pairs={{0,64},{8,96},{16,0},{24,32},{32,72},{40,104},{48,8},{56,40},{64,8... | collective-permute-start | bytes 983048 | tf_op jit(solution)/shard_map/ppermute | solution.py:323
  43.4 11.4 %collective-permute-start.1 = (bf16[256,640]{1,0:T(8,128)(2,1)S(1)}, bf16[256,640]{1,0:T(8,128)(2,1)S(1)}, u32[]{:S(2)}, u32[]{:S(2)}) collective-permute-start(bf16[256,640]{1,0:T(8,128)(2,1)S(1)} %shard_map.60.flat_ref), channel_id=1, source_target_pairs={{0,0},{8,32},{16,64},{24,96},{32,8},{40,40},{48,72},{56,104},{64,1... | collective-permute-start | bytes 983048 | tf_op jit(solution)/shard_map/ppermute | solution.py:323
  49.1 14.5 %all-to-all-start.1 = ((f32[32,24,128]{2,1,0:T(8,128)}), f32[32,24,128]{2,1,0:T(8,128)S(1)}, u32[]{:S(2)}, u32[]{:S(2)}) async-start(f32[32,24,128]{2,1,0:T(8,128)} %bitcast.7), calls=%async_computation.1 | async-start | bytes 786432 | tf_op jit(solution)/shard_map/all_to_all | solution.py:354
  54.7 12.1 %collective-permute-start.4 = (bf16[256,640]{1,0:T(8,128)(2,1)S(1)}, bf16[256,640]{1,0:T(8,128)(2,1)S(1)}, u32[]{:S(2)}, u32[]{:S(2)}) collective-permute-start(bf16[256,640]{1,0:T(8,128)(2,1)S(1)} %collective-permute-done.1.r0), channel_id=1, source_target_pairs={{4,0},{1,4},{5,1},{2,5},{6,2},{3,6},{7,3},{0,7},{12,8},{9,12},{13,... | collective-permute-start | bytes 983048 | tf_op jit(solution)/shard_map/ppermute | solution.py:347
  58.2 18.0 %collective-permute-start.7 = (bf16[256,640]{1,0:T(8,128)(2,1)S(1)}, bf16[256,640]{1,0:T(8,128)(2,1)S(1)}, u32[]{:S(2)}, u32[]{:S(2)}) collective-permute-start(bf16[256,640]{1,0:T(8,128)(2,1)S(1)} %collective-permute-done.1.r0), channel_id=1, source_target_pairs={{2,0},{6,4},{3,1},{7,5},{0,2},{4,6},{1,3},{5,7},{10,8},{14,12},{11... | collective-permute-start | bytes 983048 | tf_op jit(solution)/shard_map/ppermute | solution.py:347
  58.7 17.4 %collective-permute-start.6 = (bf16[256,640]{1,0:T(8,128)(2,1)S(1)}, bf16[256,640]{1,0:T(8,128)(2,1)S(1)}, u32[]{:S(2)}, u32[]{:S(2)}) collective-permute-start(bf16[256,640]{1,0:T(8,128)(2,1)S(1)} %collective-permute-done.1.r0), channel_id=1, source_target_pairs={{5,0},{2,4},{6,1},{3,5},{7,2},{0,6},{4,3},{1,7},{13,8},{10,12},{14... | collective-permute-start | bytes 983048 | tf_op jit(solution)/shard_map/ppermute | solution.py:347
  59.0 18.2 %collective-permute-start.5 = (bf16[256,640]{1,0:T(8,128)(2,1)S(1)}, bf16[256,640]{1,0:T(8,128)(2,1)S(1)}, u32[]{:S(2)}, u32[]{:S(2)}) collective-permute-start(bf16[256,640]{1,0:T(8,128)(2,1)S(1)} %collective-permute-done.1.r0), channel_id=1, source_target_pairs={{3,0},{7,4},{0,1},{4,5},{1,2},{5,6},{2,3},{6,7},{11,8},{15,12},{8,... | collective-permute-start | bytes 983048 | tf_op jit(solution)/shard_map/ppermute | solution.py:347
  61.5 14.6 %collective-permute-start.3 = (bf16[2,256,640]{2,1,0:T(8,128)(2,1)}, bf16[2,256,640]{2,1,0:T(8,128)(2,1)S(1)}, u32[]{:S(2)}, u32[]{:S(2)}) collective-permute-start(bf16[2,256,640]{2,1,0:T(8,128)(2,1)} %pad_maximum_fusion), channel_id=1, source_target_pairs={{0,32},{32,0},{1,33},{33,1},{2,34},{34,2},{3,35},{35,3},{4,36},{36... | collective-permute-start | bytes 1966088 | tf_op jit(solution)/shard_map/ppermute | solution.py:22
  68.2 19.4 %all-to-all-start.2 = ((f32[32,24,128]{2,1,0:T(8,128)}), f32[32,24,128]{2,1,0:T(8,128)S(1)}, u32[]{:S(2)}, u32[]{:S(2)}) async-start(f32[32,24,128]{2,1,0:T(8,128)} %shard_map.66), calls=%async_computation.2 | async-start | bytes 786432 | tf_op jit(solution)/shard_map/all_to_all | solution.py:404
  80.6 0.7 copy-start.3
  81.3 0.7 copy-start.5
  82.0 0.8 copy-start.7
  82.8 0.7 copy-start.9
  83.5 15.9 %copy-start.8 = (bf16[256,640]{1,0:T(8,128)(2,1)S(1)}, bf16[256,640]{1,0:T(8,128)(2,1)}, u32[]{:S(2)}) copy-start(bf16[256,640]{1,0:T(8,128)(2,1)} %copy-done.7) | copy-start | bytes 983044
  83.5 15.9 %copy-start.10 = (bf16[256,640]{1,0:T(8,128)(2,1)S(1)}, bf16[256,640]{1,0:T(8,128)(2,1)}, u32[]{:S(2)}) copy-start(bf16[256,640]{1,0:T(8,128)(2,1)} %copy-done.9) | copy-start | bytes 983044
  83.5 15.9 %collective-permute-start.8 = (bf16[256,640]{1,0:T(8,128)(2,1)}, bf16[256,640]{1,0:T(8,128)(2,1)S(1)}, u32[]{:S(2)}, u32[]{:S(2)}) collective-permute-start(bf16[256,640]{1,0:T(8,128)(2,1)} %get-tuple-element.44), channel_id=1, source_target_pairs={{0,8},{8,16},{16,24},{24,0},{1,9},{9,17},{17,25},{25,1},{2,10},{10... | collective-permute-start | bytes 983048 | tf_op jit(solution)/shard_map/ppermute | solution.py:26
  84.7 14.8 %collective-permute-start.9 = (bf16[256,640]{1,0:T(8,128)(2,1)}, bf16[256,640]{1,0:T(8,128)(2,1)S(1)}, u32[]{:S(2)}, u32[]{:S(2)}) collective-permute-start(bf16[256,640]{1,0:T(8,128)(2,1)} %get-tuple-element.46), channel_id=1, source_target_pairs={{0,24},{8,0},{16,8},{24,16},{1,25},{9,1},{17,9},{25,17},{2,26},{10... | collective-permute-start | bytes 983048 | tf_op jit(solution)/shard_map/ppermute | solution.py:26
  86.2 18.0 %collective-permute-start.11 = (bf16[256,640]{1,0:T(8,128)(2,1)S(1)}, bf16[256,640]{1,0:T(8,128)(2,1)S(1)}, u32[]{:S(2)}, u32[]{:S(2)}) collective-permute-start(bf16[256,640]{1,0:T(8,128)(2,1)S(1)} %get-tuple-element.48), channel_id=1, source_target_pairs={{0,24},{8,0},{16,8},{24,16},{1,25},{9,1},{17,9},{25,17},{2,26},{10... | collective-permute-start | bytes 983048 | tf_op jit(solution)/shard_map/ppermute | solution.py:26
  87.6 16.6 %collective-permute-start.12 = (bf16[256,640]{1,0:T(8,128)(2,1)S(1)}, bf16[256,640]{1,0:T(8,128)(2,1)S(1)}, u32[]{:S(2)}, u32[]{:S(2)}) collective-permute-start(bf16[256,640]{1,0:T(8,128)(2,1)S(1)} %get-tuple-element.50), channel_id=1, source_target_pairs={{0,8},{8,16},{16,24},{24,0},{1,9},{9,17},{17,25},{25,1},{2,10},{10... | collective-permute-start | bytes 983048 | tf_op jit(solution)/shard_map/ppermute | solution.py:26
  88.7 14.3 %collective-permute-start.17 = (f32[384,128]{1,0:T(8,128)S(1)}, f32[384,128]{1,0:T(8,128)S(1)}, u32[]{:S(2)}, u32[]{:S(2)}) collective-permute-start(f32[384,128]{1,0:T(8,128)S(1)} %shard_map.67.left), channel_id=1, source_target_pairs={{0,32},{32,0},{1,33},{33,1},{2,34},{34,2},{3,35},{35,3},{4,36},{36... | collective-permute-start | bytes 589832 | tf_op jit(solution)/shard_map/ppermute | solution.py:22
  100.2 11.1 %copy-start.4 = (bf16[256,640]{1,0:T(8,128)(2,1)S(1)}, bf16[256,640]{1,0:T(8,128)(2,1)}, u32[]{:S(2)}) copy-start(bf16[256,640]{1,0:T(8,128)(2,1)} %copy-done.3) | copy-start | bytes 983044
  100.2 11.1 %copy-start.6 = (bf16[256,640]{1,0:T(8,128)(2,1)S(1)}, bf16[256,640]{1,0:T(8,128)(2,1)}, u32[]{:S(2)}) copy-start(bf16[256,640]{1,0:T(8,128)(2,1)} %copy-done.5) | copy-start | bytes 983044
  100.2 11.1 %collective-permute-start.10 = (bf16[256,640]{1,0:T(8,128)(2,1)S(1)}, bf16[256,640]{1,0:T(8,128)(2,1)S(1)}, u32[]{:S(2)}, u32[]{:S(2)}) collective-permute-start(bf16[256,640]{1,0:T(8,128)(2,1)S(1)} %get-tuple-element.47), channel_id=1, source_target_pairs={{0,8},{8,16},{16,24},{24,0},{1,9},{9,17},{17,25},{25,1},{2,10},{10... | collective-permute-start | bytes 983048 | tf_op jit(solution)/shard_map/ppermute | solution.py:26
  100.4 10.9 %collective-permute-start.13 = (bf16[256,640]{1,0:T(8,128)(2,1)S(1)}, bf16[256,640]{1,0:T(8,128)(2,1)S(1)}, u32[]{:S(2)}, u32[]{:S(2)}) collective-permute-start(bf16[256,640]{1,0:T(8,128)(2,1)S(1)} %get-tuple-element.51), channel_id=1, source_target_pairs={{0,24},{8,0},{16,8},{24,16},{1,25},{9,1},{17,9},{25,17},{2,26},{10... | collective-permute-start | bytes 983048 | tf_op jit(solution)/shard_map/ppermute | solution.py:26
  103.5 17.5 %collective-permute-start.18 = (f32[384,128]{1,0:T(8,128)S(1)}, f32[384,128]{1,0:T(8,128)S(1)}, u32[]{:S(2)}, u32[]{:S(2)}) collective-permute-start(f32[384,128]{1,0:T(8,128)S(1)} %shard_map.68.left), channel_id=1, source_target_pairs={{0,64},{64,0},{1,65},{65,1},{2,66},{66,2},{3,67},{67,3},{4,68},{68... | collective-permute-start | bytes 589832 | tf_op jit(solution)/shard_map/ppermute | solution.py:22
  113.4 11.7 %collective-permute-start.14 = (bf16[256,256]{1,0:T(8,128)(2,1)S(1)}, bf16[256,256]{1,0:T(8,128)(2,1)S(1)}, u32[]{:S(2)}, u32[]{:S(2)}) collective-permute-start(bf16[256,256]{1,0:T(8,128)(2,1)S(1)} %get-tuple-element.52), channel_id=1, source_target_pairs={{0,4},{4,1},{1,5},{5,2},{2,6},{6,3},{3,7},{7,0},{8,36},{12,33},{9,... | collective-permute-start | bytes 393224 | tf_op jit(solution)/shard_map/ppermute | solution.py:390
  121.0 12.3 %collective-permute-start.15 = (bf16[256,256]{1,0:T(8,128)(2,1)S(1)}, bf16[256,256]{1,0:T(8,128)(2,1)S(1)}, u32[]{:S(2)}, u32[]{:S(2)}) collective-permute-start(bf16[256,256]{1,0:T(8,128)(2,1)S(1)} %get-tuple-element.53), channel_id=1, source_target_pairs={{0,3},{4,7},{1,0},{5,4},{2,1},{6,5},{3,2},{7,6},{8,35},{12,39},{9,... | collective-permute-start | bytes 393224 | tf_op jit(solution)/shard_map/ppermute | solution.py:390
  121.0 12.3 %collective-permute-start.16 = (bf16[256,256]{1,0:T(8,128)(2,1)S(1)}, bf16[256,256]{1,0:T(8,128)(2,1)S(1)}, u32[]{:S(2)}, u32[]{:S(2)}) collective-permute-start(bf16[256,256]{1,0:T(8,128)(2,1)S(1)} %get-tuple-element.54), channel_id=1, source_target_pairs={{0,5},{4,2},{1,6},{5,3},{2,7},{6,0},{3,4},{7,1},{8,37},{12,34},{9,... | collective-permute-start | bytes 393224 | tf_op jit(solution)/shard_map/ppermute | solution.py:390
